TPU v7x, 32 devices: a whole 2x2x4 slice. The times are simulated.
32 devices in a mesh: blk: 16 (over z, y, core), rows: 2 (over x).
Axes of the slice: x: 2, y: 2, z: 4, core: 2. Of those that a mesh axis runs over, the one named last changes fastest.
Arguments:
- panel: bfloat16 [4, 512, 98304], P(None, 'rows', 'blk'), may hold values from -0.01953125 to 0.01953125
- solved: bfloat16 [98304, 1024], P('blk'), may hold values from -6 to 6
- loads: float32 [4, 512, 1024], P(None, 'rows'), may hold values from -6 to 6
- window: bfloat16 [4, 512, 2048], P(None, 'rows'), may hold values from -0.25 to 0.25
- inverses: bfloat16 [4, 512, 512], P(None, 'rows'), as said below
Outputs:
- unknowns: bfloat16 [4, 512, 1024], P(None, 'rows')
Inputs may be any that keep to these rules, and one draw needn't show every extreme that they name: inverses[i] is lower triangular, the inverse of the factor's i-th diagonal block.
All inputs are finite; a program needn't handle non-finite values.
Results may differ from a plain program's by a relative error of at most 0.01.
Values may be sent and summed in bfloat16 or wider, within the bound.
No kernel may reach another device: no remote copies, remote signals or barrier semaphores. Data moves between devices by JAX's collectives and lax.ppermute only.
A program may use at most 128 MiB of HBM per device.

v0:
```python
import jax
import jax.numpy as jnp
from jax import lax
from jax.sharding import PartitionSpec as P


def shards(panel, solved, loads, window, inverses):
    partial_value = jnp.einsum("ksc,cr->ksr", panel, solved, preferred_element_type=jnp.float32)
    totals = lax.psum_scatter(partial_value, "blk", scatter_dimension=2, tiled=True)
    col_count = totals.shape[2]
    loads = lax.dynamic_slice_in_dim(loads, lax.axis_index("blk") * col_count, col_count, 2)
    remaining = loads - totals
    block_size = inverses.shape[2]
    step_count = loads.shape[0]
    full_blocks = []
    own_rows = []
    for current in range(step_count):
        residual = remaining[current]
        for earlier in range(current):
            coupling = window[current][:, earlier * block_size : (earlier + 1) * block_size]
            residual = residual - jnp.dot(
                coupling, full_blocks[earlier], preferred_element_type=jnp.float32
            )
        residual = residual.astype(jnp.bfloat16)
        inverse_now = inverses[current]
        solved_part = jnp.dot(
            inverse_now,
            lax.all_gather(residual, "rows", axis=0, tiled=True),
            preferred_element_type=jnp.float32,
        ).astype(jnp.bfloat16)
        own_rows.append(solved_part)
        if current + 1 < step_count:
            full_blocks.append(lax.all_gather(solved_part, "rows", axis=0, tiled=True))
    result = jnp.stack(own_rows)
    result = lax.all_gather(result, "blk", axis=2, tiled=True)
    return result


def solution(mesh):
    placed = (
        P(None, "rows", "blk"),
        P("blk", None),
        P(None, "rows", None),
        P(None, "rows", None),
        P(None, "rows", None),
    )
    return jax.shard_map(
        shards, mesh=mesh, in_specs=placed, out_specs=P(None, "rows", None), check_vma=False
    )
```

profile of v0, /device:TPU:0, one launch (start us, length us, event | category | flops | bytes accessed | tf_op | source)
XLA Modules:
  0.0 192.3 jit_solution(2385676979387853593)
XLA Ops:
  6.5 0.0 reduce-scatter.2.cloned.1.call-start
  6.5 19.1 %fusion = f32[4,256,1024]{1,2,0:T(8,128)} fusion(bf16[4,256,6144]{2,1,0:T(8,128)(2,1)} %param.5, bf16[6144,1024]{1,0:T(8,128)(2,1)} %param.6), kind=kOutput, calls=%fused_computation | convolution fusion | flops 12884901888 | bytes 29360128 | tf_op jit(solution)/shard_map/ksc,cr->ksr/dot_general | solution.py:8
  25.6 0.0 reduce-scatter.2.cloned.1.call-update
  25.7 0.0 all-gather.3.cloned.1.call-start
  25.7 1.2 constant_dynamic-slice_fusion
  27.0 0.2 copy.11
  27.2 2.1 %slice_bitcast_fusion = (bf16[256,2048]{1,0:T(8,128)(2,1)S(1)}, bf16[256,2048]{1,0:T(8,128)(2,1)S(1)}, bf16[256,2048]{1,0:T(8,128)(2,1)S(1)}) fusion(bf16[4,256,2048]{2,1,0:T(8,128)(2,1)} %param.8), kind=kLoop, calls=%fused_computation.22 | loop fusion | bytes 6291456 | tf_op jit(solution)/shard_map/squeeze | solution.py:20
  29.2 71.7 %reduce-scatter.2.cloned.1.call-done = f32[4,256,64]{1,2,0:T(8,128)} async-done(((f32[4,256,1024]{1,2,0:T(8,128)}), f32[4,256,64]{1,2,0:T(8,128)}) %reduce-scatter.2.cloned.1.call-update) | async-done | bytes 262160 | tf_op jit(solution)/shard_map/reduce_scatter | solution.py:9
  101.0 1.0 sub.21
  102.0 4.6 %all-gather = bf16[1,512,64]{1,2,0:T(8,128)(2,1)S(1)} all-gather(bf16[1,256,64]{1,2,0:T(8,128)(2,1)S(1)} %slice.123), channel_id=2, replica_groups=mesh['blk'=16,'rows'=2] {'rows'}, dimensions={1}, use_global_device_ids=true | all-gather | bytes 98304 | tf_op jit(solution)/shard_map/all_gather | solution.py:28
  106.6 1.1 convolution_convert_fusion.3
  107.7 4.6 %all_gather.25 = bf16[512,64]{0,1:T(8,128)(2,1)S(1)} all-gather(bf16[256,64]{0,1:T(8,128)(2,1)S(1)} %bitcast.89), channel_id=1, replica_groups=mesh['blk'=16,'rows'=2] {'rows'}, dimensions={0}, use_global_device_ids=true | all-gather | bytes 98304 | tf_op jit(solution)/shard_map/all_gather | solution.py:33
  112.3 0.2 fusion.10
  112.5 4.7 %all_gather.26 = bf16[512,64]{0,1:T(8,128)(2,1)S(1)} all-gather(bf16[256,64]{0,1:T(8,128)(2,1)S(1)} %fusion.10), channel_id=1, replica_groups=mesh['blk'=16,'rows'=2] {'rows'}, dimensions={0}, use_global_device_ids=true | all-gather | bytes 98304 | tf_op jit(solution)/shard_map/all_gather | solution.py:28
  117.2 1.1 convolution_convert_fusion.2
  118.4 4.6 %all_gather.27 = bf16[512,64]{0,1:T(8,128)(2,1)S(1)} all-gather(bf16[256,64]{0,1:T(8,128)(2,1)S(1)} %bitcast.91), channel_id=1, replica_groups=mesh['blk'=16,'rows'=2] {'rows'}, dimensions={0}, use_global_device_ids=true | all-gather | bytes 98304 | tf_op jit(solution)/shard_map/all_gather | solution.py:33
  122.9 0.2 convolution_bitcast_fusion.3
  123.1 0.2 fusion.9
  123.4 4.6 %all_gather.28 = bf16[512,64]{0,1:T(8,128)(2,1)S(1)} all-gather(bf16[256,64]{0,1:T(8,128)(2,1)S(1)} %fusion.9), channel_id=1, replica_groups=mesh['blk'=16,'rows'=2] {'rows'}, dimensions={0}, use_global_device_ids=true | all-gather | bytes 98304 | tf_op jit(solution)/shard_map/all_gather | solution.py:28
  128.0 1.1 convolution_convert_fusion.1
  129.1 4.6 %all_gather.29 = bf16[512,64]{0,1:T(8,128)(2,1)S(1)} all-gather(bf16[256,64]{0,1:T(8,128)(2,1)S(1)} %bitcast.93), channel_id=1, replica_groups=mesh['blk'=16,'rows'=2] {'rows'}, dimensions={0}, use_global_device_ids=true | all-gather | bytes 98304 | tf_op jit(solution)/shard_map/all_gather | solution.py:33
  133.7 0.2 convolution_bitcast_fusion.1
  133.9 0.2 convolution_bitcast_fusion
  134.1 0.2 fusion.8
  134.3 4.6 %all_gather.30 = bf16[512,64]{0,1:T(8,128)(2,1)S(1)} all-gather(bf16[256,64]{0,1:T(8,128)(2,1)S(1)} %fusion.8), channel_id=1, replica_groups=mesh['blk'=16,'rows'=2] {'rows'}, dimensions={0}, use_global_device_ids=true | all-gather | bytes 98304 | tf_op jit(solution)/shard_map/all_gather | solution.py:28
  138.9 1.1 fusion.11
  140.1 0.7 pad_maximum_fusion
  140.7 0.0 all-gather.3.cloned.1.call-update
  140.8 40.7 %all-gather.3.cloned.1.call-done = bf16[4,256,1024]{1,2,0:T(8,128)(2,1)} async-done(((bf16[4,256,64]{1,2,0:T(8,128)(2,1)}), bf16[4,256,1024]{1,2,0:T(8,128)(2,1)}) %all-gather.3.cloned.1.call-update) | async-done | bytes 2097168 | tf_op jit(solution)/shard_map/all_gather | solution.py:35
  181.5 3.9 %copy.8 = bf16[4,256,1024]{2,1,0:T(8,128)(2,1)} copy(bf16[4,256,1024]{1,2,0:T(8,128)(2,1)} %all-gather.3.cloned.1.call-done) | data formatting | bytes 4194304 | tf_op jit(solution)/shard_map/all_gather | solution.py:35
  (1 shorter events, 0.0 us)
Async XLA Ops:
  6.5 94.4 %reduce-scatter.2.cloned.1.call-start = ((), (), s32[]{:S(2)}) async-start(), calls=%async_computation.1 | async-start | bytes 4456448 | tf_op jit(solution)/shard_map/reduce_scatter | solution.py:9
  25.7 155.8 %all-gather.3.cloned.1.call-start = ((), (), s32[]{:S(2)}) async-start(), calls=%async_computation.2 | async-start | bytes 2228224 | tf_op jit(solution)/shard_map/all_gather | solution.py:35
Sparse Core Ops, SparseCore 0:
  25.8 75.1 reduce-scatter.1
  140.9 40.5 all-gather.2
where the time goes:
time: 193 us; the launch traced here: 192 us
  waiting for transfers between devices  112 us (58%)
  blocking collectives  32.2 us (17%)
  matrix products  24.9 us (13%)
  between operations  13.5 us (7%)
  local copies, waits for them, and re-layouts  7.45 us (4%)
    reduce_scatter x1, waiting for transfers between devices, shards(): lax.psum_scatter(partial_value, 'blk', scatter_dimension=2, tiled=True)  71.7 us
    all_gather x1, waiting for transfers between devices, shards(): result = lax.all_gather(result, 'blk', axis=2, tiled=True)  40.7 us
    dot_general x1, matrix products, shards(): jnp.einsum('ksc,cr->ksr', panel, solved, preferred_element_type=jnp.float32)  19.1 us
    all_gather x4, blocking collectives, shards(): lax.all_gather(residual, 'rows', axis=0, tiled=True)  18.5 us
    all_gather x3, blocking collectives, shards(): full_blocks.append(lax.all_gather(solved_part, 'rows', axis=0, tiled=True))  13.8 us
    dot_general x4, matrix products, shards(): jnp.dot(inverse_now, lax.all_gather(residual, 'rows', axis=0, tiled=True)...  4.57 us
    all_gather x1, local copies, waits for them, and re-layouts, shards(): result = lax.all_gather(result, 'blk', axis=2, tiled=True)  3.94 us
  transfers between devices with their start and end apart: 2, of which 2 were waited for; matrix products, arithmetic and copies ran while one was open for 2% of the time, Pallas kernels for 0%

commit v1 on v0

v1 whole, which is shorter than its diff:
```python
import functools

import jax
import jax.numpy as jnp
from jax import lax
from jax.experimental import pallas as pl
from jax.experimental.pallas import tpu as pltpu
from jax.sharding import PartitionSpec as P

BF = jnp.bfloat16
F32 = jnp.float32
GROUPS = ((0, 1), (2, 3))
LANES = 128


def swap(value, axis, size, bit):
    step = 1 << bit
    return lax.ppermute(value, axis, [(i, i ^ step) for i in range(size)])


def pick(flag, when_set, when_clear):
    return jnp.where(flag, when_set, when_clear)


def chain_kernel(steps, side_ref, own_w, far_w, own_r, far_r, *rest):
    first = steps[0]
    if first:
        before, own_out, solved, right = rest
        solved[: before.shape[0], :] = before[...]
    else:
        own_out, solved, right = rest
    half = own_r.shape[1]
    block = 2 * half
    side = side_ref[0]
    near_at = pl.multiple_of(side * half, half)
    far_at = pl.multiple_of((1 - side) * half, half)
    offset = 0
    for place, step in enumerate(steps):
        near = own_r[place].astype(F32)
        far = far_r[place].astype(F32)
        inv = slice(offset, offset + block)
        offset += block
        if step:
            win = slice(offset, offset + step * block)
            offset += step * block
            known = solved[: step * block, :]
            near = near - jnp.dot(own_w[:, win], known, preferred_element_type=F32)
            far = far - jnp.dot(far_w[:, win], known, preferred_element_type=F32)
        right[pl.ds(near_at, half), :] = near.astype(BF)
        right[pl.ds(far_at, half), :] = far.astype(BF)
        both = right[...]
        near = jnp.dot(own_w[:, inv], both, preferred_element_type=F32).astype(BF)
        far = jnp.dot(far_w[:, inv], both, preferred_element_type=F32).astype(BF)
        own_out[place] = near
        solved[pl.ds(step * block + near_at, half), :] = near
        solved[pl.ds(step * block + far_at, half), :] = far


def chain(steps, side, own_w, far_w, own_r, far_r, before):
    half, cols = own_r.shape[1:]
    block = 2 * half
    known = (steps[-1] + 1) * block
    args = [side, own_w, far_w, own_r, far_r] + ([before] if steps[0] else [])
    vmem = pl.BlockSpec(memory_space=pltpu.VMEM)
    return pl.pallas_call(
        functools.partial(chain_kernel, steps),
        in_specs=[pl.BlockSpec(memory_space=pltpu.SMEM)] + [vmem] * (len(args) - 1),
        out_specs=[vmem, vmem],
        out_shape=[
            jax.ShapeDtypeStruct((len(steps), half, cols), BF),
            jax.ShapeDtypeStruct((known, cols), BF),
        ],
        scratch_shapes=[pltpu.VMEM((block, cols), BF)],
        compiler_params=pltpu.CompilerParams(vmem_limit_bytes=40 << 20),
        name="chain",
    )(*args)


def shards(size, panel, solved, loads, window, inverses):
    me = lax.axis_index("blk")
    side = lax.axis_index("rows")
    bits = size.bit_length() - 1
    flags = [(me >> bit) & 1 == 1 for bit in range(bits)]
    step_count, half, _ = panel.shape
    block = inverses.shape[2]
    rhs = solved.shape[1]

    halvings = 0
    cols = rhs
    while halvings < bits and cols % (2 * LANES) == 0:
        cols //= 2
        halvings += 1
    place = sum(((me >> bit) & 1) * (rhs >> (bit + 1)) for bit in range(halvings))

    weights = []
    for steps in GROUPS:
        parts = []
        for step in steps:
            parts.append(inverses[step])
            if step:
                parts.append(window[step][:, : step * block])
        own = jnp.concatenate(parts, axis=1)
        mid = own.shape[1] // 2
        sent = pick(flags[0], own[:, mid:], own[:, :mid])
        here = lax.ppermute(sent, "rows", [(0, 1), (1, 0)])
        there = swap(here, "blk", size, 0)
        far = jnp.concatenate(
            [pick(flags[0], there, here), pick(flags[0], here, there)], axis=1
        )
        weights.append((own, far))

    results = []
    known = None
    for steps, (own_w, far_w) in zip(GROUPS, weights):
        count = len(steps)
        rows = panel[steps[0] : steps[-1] + 1].reshape(count * half, -1)
        part = jnp.dot(rows, solved, preferred_element_type=F32).astype(BF)
        for bit in range(halvings):
            mid = part.shape[1] // 2
            low, high = part[:, :mid], part[:, mid:]
            got = swap(pick(flags[bit], low, high), "blk", size, bit)
            part = (pick(flags[bit], high, low).astype(F32) + got.astype(F32)).astype(BF)
        for bit in range(halvings, bits):
            got = swap(part, "blk", size, bit)
            total = part.astype(F32) + got.astype(F32)
            part = total.astype(BF) if bit + 1 < bits else total
        load = lax.dynamic_slice_in_dim(loads[steps[0] : steps[-1] + 1], place, cols, 2)
        remaining = load - part.reshape(count, half, cols).astype(F32)
        far_r = lax.ppermute(remaining.astype(BF), "rows", [(0, 1), (1, 0)])
        answer, known = chain(
            steps, side[None].astype(jnp.int32), own_w, far_w, remaining, far_r, known
        )
        for bit in reversed(range(halvings)):
            got = swap(answer, "blk", size, bit)
            answer = jnp.concatenate(
                [pick(flags[bit], got, answer), pick(flags[bit], answer, got)], axis=2
            )
        results.append(answer)
    return jnp.concatenate(results, axis=0)


def solution(mesh):
    placed = (
        P(None, "rows", "blk"),
        P("blk", None),
        P(None, "rows", None),
        P(None, "rows", None),
        P(None, "rows", None),
    )
    return jax.shard_map(
        functools.partial(shards, mesh.shape["blk"]),
        mesh=mesh,
        in_specs=placed,
        out_specs=P(None, "rows", None),
        check_vma=False,
    )
```

time: 193 us -> 94 us (0.49)
  waiting for transfers between devices: 112 us -> 27.1 us
  blocking collectives: 32.2 us -> 0 us
  starting transfers between devices: 0.04 us -> 22.9 us
  between operations: 13.5 us -> 0.39 us
  other arithmetic: 1.66 us -> 13.9 us
  matrix products: 24.9 us -> 13.5 us
  local copies, waits for them, and re-layouts: 7.45 us -> 12.6 us
  Pallas kernels: 0 us -> 3.26 us
    reduce_scatter x1 -> x0, waiting for transfers between devices: 71.7 us -> none  [shards(): lax.psum_scatter(partial_value, 'blk', scatter_dimension=2, tiled=True)]
    all_gather x1 -> x0, waiting for transfers between devices: 40.7 us -> none  [shards(): result = lax.all_gather(result, 'blk', axis=2, tiled=True)]
    all_gather x7 -> x0, blocking collectives: 32.2 us -> none  [the longest x4 18.5 us: shards(): lax.all_gather(residual, 'rows', axis=0, tiled=True)]
    ppermute x0 -> x20, waiting for transfers between devices: none -> 27.1 us  [the longest x16 24 us: swap(): return lax.ppermute(value, axis, [(i, i ^ step) for i in range(size)])]
    ppermute x0 -> x20, starting transfers between devices: none -> 22.9 us  [the longest x16 18.1 us: swap(): return lax.ppermute(value, axis, [(i, i ^ step) for i in range(size)])]
    dot_general x11 -> x2, matrix products: 24.9 us -> 13.5 us  [shards(): part = jnp.dot(rows, solved, preferred_element_type=F32).astype(BF)]
    slice x1 -> x5, local copies, waits for them, and re-layouts: 0.01 us -> 7.93 us  [the longest x1 5.47 us: shards(): rows = panel[steps[0]:steps[-1] + 1].reshape(count * half, -1)]
    select_n x0 -> x16, other arithmetic: none -> 6.1 us  [pick(): return jnp.where(flag, when_set, when_clear)]
  transfers between devices with their start and end apart: 2 -> 20, of which waited for: 2 -> 9; matrix products, arithmetic and copies ran while one was open for 2% -> 22% of each run, Pallas kernels for 0% -> 3%
where the time goes in v1:
time: 94 us; the launch traced here: 93.6 us
  waiting for transfers between devices  27.1 us (29%)
  starting transfers between devices  22.9 us (24%)
  other arithmetic  13.9 us (15%)
  matrix products  13.5 us (14%)
  local copies, waits for them, and re-layouts  12.6 us (13%)
  Pallas kernels  3.26 us (3%)
    ppermute x16, waiting for transfers between devices, swap(): return lax.ppermute(value, axis, [(i, i ^ step) for i in range(size)])  24 us
    ppermute x16, starting transfers between devices, swap(): return lax.ppermute(value, axis, [(i, i ^ step) for i in range(size)])  18.1 us
    dot_general x2, matrix products, shards(): part = jnp.dot(rows, solved, preferred_element_type=F32).astype(BF)  13.5 us
    select_n x16, other arithmetic, pick(): return jnp.where(flag, when_set, when_clear)  6.1 us
    slice x1, local copies, waits for them, and re-layouts, shards(): rows = panel[steps[0]:steps[-1] + 1].reshape(count * half, -1)  5.47 us
    unnamed x12, local copies, waits for them, and re-layouts  4.22 us
    convert_element_type x6, other arithmetic, shards(): (pick(flags[bit], high, low).astype(F32) + got.astype(F32)).astype(BF)  3.6 us
    pallas_call x2, Pallas kernels, chain(): pl.pallas_call(functools.partial(chain_kernel, steps), in_specs=[pl.Block...  3.26 us
  transfers between devices with their start and end apart: 20, of which 9 were waited for; matrix products, arithmetic and copies ran while one was open for 22% of the time, Pallas kernels for 3%

profile of v1, /device:TPU:0, one launch (start us, length us, event | category | flops | bytes accessed | tf_op | source)
XLA Modules:
  0.0 93.6 jit_solution(6934944809081924747)
XLA Ops:
  0.0 5.5 %fusion.4 = (bf16[2,256,6144]{2,1,0:T(8,128)(2,1)S(1)}, bf16[2,256,6144]{2,1,0:T(8,128)(2,1)S(1)}) fusion(bf16[4,256,6144]{2,1,0:T(8,128)(2,1)} %param.5), kind=kLoop, calls=%fused_computation.59 | loop fusion | bytes 25165824 | tf_op jit(solution)/shard_map/slice | solution.py:116
  5.5 2.8 %copy-done.5 = bf16[6144,1024]{1,0:T(8,128)(2,1)S(1)} copy-done((bf16[6144,1024]{1,0:T(8,128)(2,1)S(1)}, bf16[6144,1024]{1,0:T(8,128)(2,1)}, u32[]{:S(2)}) %copy-start.5) | copy-done | bytes 12582936
  8.3 6.7 %convolution_convert_fusion.1 = bf16[512,1024]{1,0:T(8,128)(2,1)S(1)} fusion(bf16[512,6144]{1,0:T(8,128)(2,1)S(1)} %bitcast.24, bf16[6144,1024]{1,0:T(8,128)(2,1)S(1)} %copy-done.5), kind=kOutput, calls=%fused_computation.4 | convolution fusion | flops 6442975232 | bytes 19922944 | tf_op jit(solution)/shard_map/dot_general | solution.py:117
  15.0 1.0 %broadcast_select_fusion.3 = bf16[512,512]{1,0:T(8,128)(2,1)} fusion(pred[]{:T(512)S(6)} %eq.9, bf16[512,1024]{1,0:T(8,128)(2,1)S(1)} %convolution_convert_fusion.1), kind=kLoop, calls=%fused_computation.23 | loop fusion | flops 262144 | bytes 1572865 | tf_op jit(solution)/shard_map/jit(_where)/select_n | solution.py:22
  16.0 0.5 collective-permute-start.2
  16.4 0.1 slice_bitcast_fusion.6
  16.5 0.4 slice_bitcast_fusion.2
  17.0 0.9 fusion.1
  17.9 2.5 %collective-permute-start = (bf16[256,768]{1,0:T(8,128)(2,1)}, bf16[256,768]{1,0:T(8,128)(2,1)}, u32[]{:S(2)}, u32[]{:S(2)}) collective-permute-start(bf16[256,768]{1,0:T(8,128)(2,1)} %fusion.1), channel_id=1, source_target_pairs={{0,1},{1,0},{2,3},{3,2},{4,5},{5,4},{6,7},{7,6},{8,9},{9,8},{10,11... | collective-permute-start | bytes 1179656 | tf_op jit(solution)/shard_map/ppermute | solution.py:105
  20.4 6.7 %convolution_convert_fusion = bf16[512,1024]{1,0:T(8,128)(2,1)S(1)} fusion(bf16[512,6144]{1,0:T(8,128)(2,1)S(1)} %bitcast.23, bf16[6144,1024]{1,0:T(8,128)(2,1)S(1)} %copy-done.5), kind=kOutput, calls=%fused_computation.3 | convolution fusion | flops 6442975232 | bytes 19922944 | tf_op jit(solution)/shard_map/dot_general | solution.py:117
  27.1 0.9 broadcast_select_fusion.2
  28.0 0.2 collective-permute-start.12
  28.3 0.1 slice.132
  28.3 0.0 copy-start.2
  28.4 0.2 fusion
  28.6 0.3 collective-permute-start.10
  29.0 0.1 pad_maximum_fusion.own_w
  29.1 1.4 %copy-done.2 = f32[4,256,1024]{2,1,0:T(8,128)S(1)} copy-done((f32[4,256,1024]{2,1,0:T(8,128)S(1)}, f32[4,256,1024]{2,1,0:T(8,128)}, u32[]{:S(2)}) %copy-start.2) | copy-done | bytes 4194328
  30.5 2.3 %fusion.5 = (f32[2,256,1024]{2,1,0:T(8,128)}, f32[2,256,1024]{2,1,0:T(8,128)}) fusion(f32[4,256,1024]{2,1,0:T(8,128)S(1)} %copy-done.2), kind=kLoop, calls=%fused_computation.60 | loop fusion | bytes 8388608 | tf_op jit(solution)/shard_map/slice | solution.py:127
  32.9 0.1 pad_maximum_fusion.5.own_w
  33.0 0.3 collective-permute-start.1
  33.3 1.6 %add_convert_fusion.1 = bf16[512,512]{1,0:T(8,128)(2,1)S(1)} fusion(bf16[512,512]{1,0:T(8,128)(2,1)} %collective-permute-done.2, pred[]{:T(512)S(6)} %eq.9, bf16[512,1024]{1,0:T(8,128)(2,1)} %copy-done), kind=kLoop, calls=%fused_computation.8 | loop fusion | flops 1310720 | bytes 2097153 | tf_op jit(solution)/shard_map/convert_element_type | solution.py:122
  34.9 1.6 %collective-permute-start.3 = (bf16[512,256]{1,0:T(8,128)(2,1)S(1)}, bf16[512,256]{1,0:T(8,128)(2,1)S(1)}, u32[]{:S(2)}, u32[]{:S(2)}) collective-permute-start(bf16[512,256]{1,0:T(8,128)(2,1)S(1)} %broadcast_select_fusion.11), channel_id=1, source_target_pairs={{0,4},{2,6},{4,0},{6,2},{8,12},{10,14},{12,8},{14,10},{16,20},{18,... | collective-permute-start | bytes 786440 | tf_op jit(solution)/shard_map/ppermute | solution.py:18
  36.5 0.0 collective-permute-done.12
  36.5 1.7 %add_convert_fusion = bf16[512,512]{1,0:T(8,128)(2,1)S(1)} fusion(bf16[512,512]{1,0:T(8,128)(2,1)} %collective-permute-done.12, pred[]{:T(512)S(6)} %eq.9, bf16[512,1024]{1,0:T(8,128)(2,1)} %copy-done.1), kind=kLoop, calls=%fused_computation.5 | loop fusion | flops 1310720 | bytes 2097153 | tf_op jit(solution)/shard_map/convert_element_type | solution.py:122
  38.3 0.6 collective-permute-start.13
  38.9 5.3 %collective-permute-done.3 = bf16[512,256]{1,0:T(8,128)(2,1)S(1)} collective-permute-done((bf16[512,256]{1,0:T(8,128)(2,1)S(1)}, bf16[512,256]{1,0:T(8,128)(2,1)S(1)}, u32[]{:S(2)}, u32[]{:S(2)}) %collective-permute-start.3) | collective-permute-done | bytes 262176 | tf_op jit(solution)/shard_map/ppermute | solution.py:18
  44.1 0.1 add_convert_fusion.3
  44.2 1.6 %collective-permute-start.4 = (bf16[512,128]{1,0:T(8,128)(2,1)S(1)}, bf16[512,128]{1,0:T(8,128)(2,1)S(1)}, u32[]{:S(2)}, u32[]{:S(2)}) collective-permute-start(bf16[512,128]{1,0:T(8,128)(2,1)S(1)} %broadcast_select_fusion.17), channel_id=1, source_target_pairs={{0,8},{2,10},{4,12},{6,14},{8,0},{10,2},{12,4},{14,6},{16,24},{18,... | collective-permute-start | bytes 393224 | tf_op jit(solution)/shard_map/ppermute | solution.py:18
  45.9 3.1 %collective-permute-done.13 = bf16[512,256]{1,0:T(8,128)(2,1)S(1)} collective-permute-done((bf16[512,256]{1,0:T(8,128)(2,1)S(1)}, bf16[512,256]{1,0:T(8,128)(2,1)S(1)}, u32[]{:S(2)}, u32[]{:S(2)}) %collective-permute-start.13) | collective-permute-done | bytes 262176 | tf_op jit(solution)/shard_map/ppermute | solution.py:18
  49.0 0.1 add_convert_fusion.2
  49.2 1.6 %collective-permute-start.14 = (bf16[512,128]{1,0:T(8,128)(2,1)S(1)}, bf16[512,128]{1,0:T(8,128)(2,1)S(1)}, u32[]{:S(2)}, u32[]{:S(2)}) collective-permute-start(bf16[512,128]{1,0:T(8,128)(2,1)S(1)} %broadcast_select_fusion.16), channel_id=1, source_target_pairs={{0,8},{2,10},{4,12},{6,14},{8,0},{10,2},{12,4},{14,6},{16,24},{18,... | collective-permute-start | bytes 393224 | tf_op jit(solution)/shard_map/ppermute | solution.py:18
  50.8 1.1 %broadcast_select_fusion.9 = (bf16[256,768]{1,0:T(8,128)(2,1)S(1)}, bf16[256,768]{1,0:T(8,128)(2,1)S(1)}) fusion(bf16[256,768]{1,0:T(8,128)(2,1)S(1)} %collective-permute-done.1, bf16[256,768]{1,0:T(8,128)(2,1)} %collective-permute-done, pred[]{:T(512)S(6)} %eq.9), kind=kLoop, calls=%fused_computation.32 | loop fusion | flops 393216 | bytes 1572865 | tf_op jit(solution)/shard_map/jit(_where)/select_n | solution.py:22
  51.9 0.1 pad_maximum_fusion.6.far_w
  51.9 0.1 add_convert_fusion.5
  52.0 2.7 %collective-permute-start.5 = (bf16[512,128]{1,0:T(8,128)(2,1)S(1)}, bf16[512,128]{1,0:T(8,128)(2,1)S(1)}, u32[]{:S(2)}, u32[]{:S(2)}) collective-permute-start(bf16[512,128]{1,0:T(8,128)(2,1)S(1)} %add_convert_fusion.5), channel_id=1, source_target_pairs={{0,16},{2,18},{4,20},{6,22},{8,24},{10,26},{12,28},{14,30},{16,0},... | collective-permute-start | bytes 393224 | tf_op jit(solution)/shard_map/ppermute | solution.py:18
  54.7 0.1 add_convert_fusion.4
  54.7 3.7 %collective-permute-start.15 = (bf16[512,128]{1,0:T(8,128)(2,1)S(1)}, bf16[512,128]{1,0:T(8,128)(2,1)S(1)}, u32[]{:S(2)}, u32[]{:S(2)}) collective-permute-start(bf16[512,128]{1,0:T(8,128)(2,1)S(1)} %add_convert_fusion.4), channel_id=1, source_target_pairs={{0,16},{2,18},{4,20},{6,22},{8,24},{10,26},{12,28},{14,30},{16,0},... | collective-permute-start | bytes 393224 | tf_op jit(solution)/shard_map/ppermute | solution.py:18
  58.4 5.7 %collective-permute-done.5 = bf16[512,128]{1,0:T(8,128)(2,1)S(1)} collective-permute-done((bf16[512,128]{1,0:T(8,128)(2,1)S(1)}, bf16[512,128]{1,0:T(8,128)(2,1)S(1)}, u32[]{:S(2)}, u32[]{:S(2)}) %collective-permute-start.5) | collective-permute-done | bytes 131104 | tf_op jit(solution)/shard_map/ppermute | solution.py:18
  64.1 1.0 %fusion.2 = (bf16[2,256,128]{2,1,0:T(8,128)(2,1)S(1)}, f32[2,256,128]{2,1,0:T(8,128)S(1)}) fusion(f32[2,256,128]{2,1,0:T(8,128)S(1)} %bitcast.26, f32[2,256,1024]{2,1,0:T(8,128)} %get-tuple-element.17, s32[]{:T(128)S(6)} %select_n.163), kind=kLoop, calls=%fused_computation.57 | loop fusion | flops 131072 | bytes 917508 | tf_op jit(solution)/shard_map/convert_element_type | solution.py:129
  65.1 0.6 collective-permute-start.6
  65.8 0.2 collective-permute-done.15
  66.0 1.0 %fusion.3 = (bf16[2,256,128]{2,1,0:T(8,128)(2,1)S(1)}, f32[2,256,128]{2,1,0:T(8,128)S(1)}) fusion(f32[2,256,128]{2,1,0:T(8,128)S(1)} %bitcast.25, f32[2,256,1024]{2,1,0:T(8,128)} %get-tuple-element.18, s32[]{:T(128)S(6)} %select_n.163), kind=kLoop, calls=%fused_computation.58 | loop fusion | flops 131072 | bytes 917508 | tf_op jit(solution)/shard_map/convert_element_type | solution.py:129
  67.0 1.3 %collective-permute-start.16 = (bf16[2,256,128]{2,1,0:T(8,128)(2,1)S(1)}, bf16[2,256,128]{2,1,0:T(8,128)(2,1)S(1)}, u32[]{:S(2)}, u32[]{:S(2)}) collective-permute-start(bf16[2,256,128]{2,1,0:T(8,128)(2,1)S(1)} %get-tuple-element.13), channel_id=1, source_target_pairs={{0,1},{1,0},{2,3},{3,2},{4,5},{5,4},{6,7},{7,6},{8,9},{9,8},{10,11... | collective-permute-start | bytes 393224 | tf_op jit(solution)/shard_map/ppermute | solution.py:129
  68.3 3.1 %collective-permute-done.6.far_r = bf16[2,256,128]{2,1,0:T(8,128)(2,1)S(1)} collective-permute-done((bf16[2,256,128]{2,1,0:T(8,128)(2,1)S(1)}, bf16[2,256,128]{2,1,0:T(8,128)(2,1)S(1)}, u32[]{:S(2)}, u32[]{:S(2)}) %collective-permute-start.6) | collective-permute-done | bytes 131104 | tf_op jit(solution)/shard_map/ppermute | solution.py:129
  71.4 0.9 chain.2
  72.2 0.1 collective-permute-start.7
  72.3 1.3 %broadcast_select_fusion.1 = (bf16[256,1792]{1,0:T(8,128)(2,1)S(1)}, bf16[256,1792]{1,0:T(8,128)(2,1)S(1)}) fusion(bf16[256,1792]{1,0:T(8,128)(2,1)S(1)} %collective-permute-done.11, bf16[256,1792]{1,0:T(8,128)(2,1)} %collective-permute-done.10, pred[]{:T(512)S(6)} %eq.9), kind=kLoop, calls=%fused_computation.15 | loop fusion | flops 917504 | bytes 3670017 | tf_op jit(solution)/shard_map/jit(_where)/select_n | solution.py:22
  73.6 0.1 pad_maximum_fusion.1.far_w
  73.8 2.4 %chain.3 = (bf16[2,256,128]{2,1,0:T(8,128)(2,1)S(1)}, bf16[2048,128]{1,0:T(8,128)(2,1)}) custom-call(s32[1]{0:T(128)} %bitcast.side_ref, bf16[256,3584]{1,0:T(8,128)(2,1)S(1)} %pad_maximum_fusion.own_w, bf16[256,3584]{1,0:T(8,128)(2,1)S(1)} %pad_maximum_fusion.1.far_w, f32[2,256,128]{2,1,0:T(8,128)S(1)} %get-tuple-element.14.own_r, ...), custom_call_target="tpu_custom_call" | custom-call | tf_op jit(solution)/shard_map/chain/pallas_call | solution.py:65
  76.2 2.0 %collective-permute-start.17 = (bf16[2,256,128]{2,1,0:T(8,128)(2,1)S(1)}, bf16[2,256,128]{2,1,0:T(8,128)(2,1)S(1)}, u32[]{:S(2)}, u32[]{:S(2)}) collective-permute-start(bf16[2,256,128]{2,1,0:T(8,128)(2,1)S(1)} %get-tuple-element.10), channel_id=1, source_target_pairs={{0,8},{2,10},{4,12},{6,14},{8,0},{10,2},{12,4},{14,6},{16,24},{18,... | collective-permute-start | bytes 393224 | tf_op jit(solution)/shard_map/ppermute | solution.py:18
  78.2 1.6 %collective-permute-start.8 = (bf16[2,256,256]{2,1,0:T(8,128)(2,1)S(1)}, bf16[2,256,256]{2,1,0:T(8,128)(2,1)S(1)}, u32[]{:S(2)}, u32[]{:S(2)}) collective-permute-start(bf16[2,256,256]{2,1,0:T(8,128)(2,1)S(1)} %pad_maximum_fusion.11), channel_id=1, source_target_pairs={{0,4},{2,6},{4,0},{6,2},{8,12},{10,14},{12,8},{14,10},{16,20},{18,... | collective-permute-start | bytes 786440 | tf_op jit(solution)/shard_map/ppermute | solution.py:18
  79.8 1.3 %collective-permute-done.17 = bf16[2,256,128]{2,1,0:T(8,128)(2,1)S(1)} collective-permute-done((bf16[2,256,128]{2,1,0:T(8,128)(2,1)S(1)}, bf16[2,256,128]{2,1,0:T(8,128)(2,1)S(1)}, u32[]{:S(2)}, u32[]{:S(2)}) %collective-permute-start.17) | collective-permute-done | bytes 131104 | tf_op jit(solution)/shard_map/ppermute | solution.py:18
  81.2 1.6 %collective-permute-start.18 = (bf16[2,256,256]{2,1,0:T(8,128)(2,1)S(1)}, bf16[2,256,256]{2,1,0:T(8,128)(2,1)S(1)}, u32[]{:S(2)}, u32[]{:S(2)}) collective-permute-start(bf16[2,256,256]{2,1,0:T(8,128)(2,1)S(1)} %pad_maximum_fusion.12), channel_id=1, source_target_pairs={{0,4},{2,6},{4,0},{6,2},{8,12},{10,14},{12,8},{14,10},{16,20},{18,... | collective-permute-start | bytes 786440 | tf_op jit(solution)/shard_map/ppermute | solution.py:18
  82.8 4.1 %collective-permute-done.8 = bf16[2,256,256]{2,1,0:T(8,128)(2,1)S(1)} collective-permute-done((bf16[2,256,256]{2,1,0:T(8,128)(2,1)S(1)}, bf16[2,256,256]{2,1,0:T(8,128)(2,1)S(1)}, u32[]{:S(2)}, u32[]{:S(2)}) %collective-permute-start.8) | collective-permute-done | bytes 262176 | tf_op jit(solution)/shard_map/ppermute | solution.py:18
  86.8 0.1 broadcast_select_fusion.15
  87.0 0.1 collective-permute-start.9
  87.1 2.6 %collective-permute-done.18 = bf16[2,256,256]{2,1,0:T(8,128)(2,1)S(1)} collective-permute-done((bf16[2,256,256]{2,1,0:T(8,128)(2,1)S(1)}, bf16[2,256,256]{2,1,0:T(8,128)(2,1)S(1)}, u32[]{:S(2)}, u32[]{:S(2)}) %collective-permute-start.18) | collective-permute-done | bytes 262176 | tf_op jit(solution)/shard_map/ppermute | solution.py:18
  89.7 0.1 broadcast_select_fusion.13
  89.8 0.1 collective-permute-start.19
  89.9 0.2 broadcast_select_fusion.7
  90.1 1.7 %collective-permute-done.19 = bf16[2,256,512]{2,1,0:T(8,128)(2,1)S(1)} collective-permute-done((bf16[2,256,512]{2,1,0:T(8,128)(2,1)S(1)}, bf16[2,256,512]{2,1,0:T(8,128)(2,1)S(1)}, u32[]{:S(2)}, u32[]{:S(2)}) %collective-permute-start.19) | collective-permute-done | bytes 524320 | tf_op jit(solution)/shard_map/ppermute | solution.py:18
  91.8 0.2 broadcast_select_fusion.5
  92.0 1.6 %maximum_maximum_fusion = bf16[4,256,1024]{2,1,0:T(8,128)(2,1)} fusion(bf16[2,256,512]{2,1,0:T(8,128)(2,1)S(1)} %get-tuple-element.27, bf16[2,256,512]{2,1,0:T(8,128)(2,1)S(1)} %get-tuple-element.26, bf16[2,256,512]{2,1,0:T(8,128)(2,1)S(1)} %get-tuple-element.25, bf16[2,256,512]{2,1,0:T(8,128)(2,1)S(1)} %get-tuple-element.24), kind=kLoop, calls=%fused_computation | loop fusion | flops 8388608 | bytes 4194304 | tf_op jit(solution)/shard_map/concatenate | solution.py:139
  (34 shorter events, 0.4 us)
Async XLA Ops:
  0.0 8.3 %copy-start.5 = (bf16[6144,1024]{1,0:T(8,128)(2,1)S(1)}, bf16[6144,1024]{1,0:T(8,128)(2,1)}, u32[]{:S(2)}) copy-start(bf16[6144,1024]{1,0:T(8,128)(2,1)} %param.6) | copy-start | bytes 37748740
  8.3 8.2 %copy-start.4 = (bf16[4,256,512]{2,1,0:T(8,128)(2,1)S(1)}, bf16[4,256,512]{2,1,0:T(8,128)(2,1)}, u32[]{:S(2)}) copy-start(bf16[4,256,512]{2,1,0:T(8,128)(2,1)} %param.9) | copy-start | bytes 3145732
  8.3 8.2 %copy-start.3 = (bf16[4,256,2048]{2,1,0:T(8,128)(2,1)S(1)}, bf16[4,256,2048]{2,1,0:T(8,128)(2,1)}, u32[]{:S(2)}) copy-start(bf16[4,256,2048]{2,1,0:T(8,128)(2,1)} %param.8) | copy-start | bytes 12582916
  15.0 1.9 %copy-start = (bf16[512,1024]{1,0:T(8,128)(2,1)}, bf16[512,1024]{1,0:T(8,128)(2,1)S(1)}, u32[]{:S(2)}) copy-start(bf16[512,1024]{1,0:T(8,128)(2,1)S(1)} %convolution_convert_fusion.1) | copy-start | bytes 3145732
  16.0 17.3 %collective-permute-start.2 = (bf16[512,512]{1,0:T(8,128)(2,1)}, bf16[512,512]{1,0:T(8,128)(2,1)}, u32[]{:S(2)}, u32[]{:S(2)}) collective-permute-start(bf16[512,512]{1,0:T(8,128)(2,1)} %broadcast_select_fusion.3), channel_id=1, source_target_pairs={{0,2},{2,0},{4,6},{6,4},{8,10},{10,8},{12,14},{14,12},{16,18},{18,... | collective-permute-start | bytes 1572872 | tf_op jit(solution)/shard_map/ppermute | solution.py:18
  17.9 15.1 %collective-permute-start = (bf16[256,768]{1,0:T(8,128)(2,1)}, bf16[256,768]{1,0:T(8,128)(2,1)}, u32[]{:S(2)}, u32[]{:S(2)}) collective-permute-start(bf16[256,768]{1,0:T(8,128)(2,1)} %fusion.1), channel_id=1, source_target_pairs={{0,1},{1,0},{2,3},{3,2},{4,5},{5,4},{6,7},{7,6},{8,9},{9,8},{10,11... | collective-permute-start | bytes 1179656 | tf_op jit(solution)/shard_map/ppermute | solution.py:105
  27.1 2.0 %copy-start.1 = (bf16[512,1024]{1,0:T(8,128)(2,1)}, bf16[512,1024]{1,0:T(8,128)(2,1)S(1)}, u32[]{:S(2)}) copy-start(bf16[512,1024]{1,0:T(8,128)(2,1)S(1)} %convolution_convert_fusion) | copy-start | bytes 3145732
  28.0 8.5 %collective-permute-start.12 = (bf16[512,512]{1,0:T(8,128)(2,1)}, bf16[512,512]{1,0:T(8,128)(2,1)}, u32[]{:S(2)}, u32[]{:S(2)}) collective-permute-start(bf16[512,512]{1,0:T(8,128)(2,1)} %broadcast_select_fusion.2), channel_id=1, source_target_pairs={{0,2},{2,0},{4,6},{6,4},{8,10},{10,8},{12,14},{14,12},{16,18},{18,... | collective-permute-start | bytes 1572872 | tf_op jit(solution)/shard_map/ppermute | solution.py:18
  28.3 2.2 %copy-start.2 = (f32[4,256,1024]{2,1,0:T(8,128)S(1)}, f32[4,256,1024]{2,1,0:T(8,128)}, u32[]{:S(2)}) copy-start(f32[4,256,1024]{2,1,0:T(8,128)} %param.7) | copy-start | bytes 12582916
  28.6 29.7 %collective-permute-start.10 = (bf16[256,1792]{1,0:T(8,128)(2,1)S(1)}, bf16[256,1792]{1,0:T(8,128)(2,1)}, u32[]{:S(2)}, u32[]{:S(2)}) collective-permute-start(bf16[256,1792]{1,0:T(8,128)(2,1)S(1)} %fusion), channel_id=1, source_target_pairs={{0,1},{1,0},{2,3},{3,2},{4,5},{5,4},{6,7},{7,6},{8,9},{9,8},{10,11... | collective-permute-start | bytes 2752520 | tf_op jit(solution)/shard_map/ppermute | solution.py:105
  33.0 17.8 %collective-permute-start.1 = (bf16[256,768]{1,0:T(8,128)(2,1)}, bf16[256,768]{1,0:T(8,128)(2,1)S(1)}, u32[]{:S(2)}, u32[]{:S(2)}) collective-permute-start(bf16[256,768]{1,0:T(8,128)(2,1)} %collective-permute-done), channel_id=1, source_target_pairs={{0,2},{2,0},{4,6},{6,4},{8,10},{10,8},{12,14},{14,12},{16,18},{18,... | collective-permute-start | bytes 1179656 | tf_op jit(solution)/shard_map/ppermute | solution.py:18
  34.9 9.2 %collective-permute-start.3 = (bf16[512,256]{1,0:T(8,128)(2,1)S(1)}, bf16[512,256]{1,0:T(8,128)(2,1)S(1)}, u32[]{:S(2)}, u32[]{:S(2)}) collective-permute-start(bf16[512,256]{1,0:T(8,128)(2,1)S(1)} %broadcast_select_fusion.11), channel_id=1, source_target_pairs={{0,4},{2,6},{4,0},{6,2},{8,12},{10,14},{12,8},{14,10},{16,20},{18,... | collective-permute-start | bytes 786440 | tf_op jit(solution)/shard_map/ppermute | solution.py:18
  38.3 10.8 %collective-permute-start.13 = (bf16[512,256]{1,0:T(8,128)(2,1)S(1)}, bf16[512,256]{1,0:T(8,128)(2,1)S(1)}, u32[]{:S(2)}, u32[]{:S(2)}) collective-permute-start(bf16[512,256]{1,0:T(8,128)(2,1)S(1)} %broadcast_select_fusion.10), channel_id=1, source_target_pairs={{0,4},{2,6},{4,0},{6,2},{8,12},{10,14},{12,8},{14,10},{16,20},{18,... | collective-permute-start | bytes 786440 | tf_op jit(solution)/shard_map/ppermute | solution.py:18
  44.2 7.7 %collective-permute-start.4 = (bf16[512,128]{1,0:T(8,128)(2,1)S(1)}, bf16[512,128]{1,0:T(8,128)(2,1)S(1)}, u32[]{:S(2)}, u32[]{:S(2)}) collective-permute-start(bf16[512,128]{1,0:T(8,128)(2,1)S(1)} %broadcast_select_fusion.17), channel_id=1, source_target_pairs={{0,8},{2,10},{4,12},{6,14},{8,0},{10,2},{12,4},{14,6},{16,24},{18,... | collective-permute-start | bytes 393224 | tf_op jit(solution)/shard_map/ppermute | solution.py:18
  49.2 5.5 %collective-permute-start.14 = (bf16[512,128]{1,0:T(8,128)(2,1)S(1)}, bf16[512,128]{1,0:T(8,128)(2,1)S(1)}, u32[]{:S(2)}, u32[]{:S(2)}) collective-permute-start(bf16[512,128]{1,0:T(8,128)(2,1)S(1)} %broadcast_select_fusion.16), channel_id=1, source_target_pairs={{0,8},{2,10},{4,12},{6,14},{8,0},{10,2},{12,4},{14,6},{16,24},{18,... | collective-permute-start | bytes 393224 | tf_op jit(solution)/shard_map/ppermute | solution.py:18
  52.0 12.1 %collective-permute-start.5 = (bf16[512,128]{1,0:T(8,128)(2,1)S(1)}, bf16[512,128]{1,0:T(8,128)(2,1)S(1)}, u32[]{:S(2)}, u32[]{:S(2)}) collective-permute-start(bf16[512,128]{1,0:T(8,128)(2,1)S(1)} %add_convert_fusion.5), channel_id=1, source_target_pairs={{0,16},{2,18},{4,20},{6,22},{8,24},{10,26},{12,28},{14,30},{16,0},... | collective-permute-start | bytes 393224 | tf_op jit(solution)/shard_map/ppermute | solution.py:18
  54.7 11.3 %collective-permute-start.15 = (bf16[512,128]{1,0:T(8,128)(2,1)S(1)}, bf16[512,128]{1,0:T(8,128)(2,1)S(1)}, u32[]{:S(2)}, u32[]{:S(2)}) collective-permute-start(bf16[512,128]{1,0:T(8,128)(2,1)S(1)} %add_convert_fusion.4), channel_id=1, source_target_pairs={{0,16},{2,18},{4,20},{6,22},{8,24},{10,26},{12,28},{14,30},{16,0},... | collective-permute-start | bytes 393224 | tf_op jit(solution)/shard_map/ppermute | solution.py:18
  58.4 14.0 %collective-permute-start.11 = (bf16[256,1792]{1,0:T(8,128)(2,1)}, bf16[256,1792]{1,0:T(8,128)(2,1)S(1)}, u32[]{:S(2)}, u32[]{:S(2)}) collective-permute-start(bf16[256,1792]{1,0:T(8,128)(2,1)} %collective-permute-done.10), channel_id=1, source_target_pairs={{0,2},{2,0},{4,6},{6,4},{8,10},{10,8},{12,14},{14,12},{16,18},{18,... | collective-permute-start | bytes 2752520 | tf_op jit(solution)/shard_map/ppermute | solution.py:18
  65.1 6.3 %collective-permute-start.6 = (bf16[2,256,128]{2,1,0:T(8,128)(2,1)S(1)}, bf16[2,256,128]{2,1,0:T(8,128)(2,1)S(1)}, u32[]{:S(2)}, u32[]{:S(2)}) collective-permute-start(bf16[2,256,128]{2,1,0:T(8,128)(2,1)S(1)} %get-tuple-element.11), channel_id=1, source_target_pairs={{0,1},{1,0},{2,3},{3,2},{4,5},{5,4},{6,7},{7,6},{8,9},{9,8},{10,11... | collective-permute-start | bytes 393224 | tf_op jit(solution)/shard_map/ppermute | solution.py:129
  67.0 6.7 %collective-permute-start.16 = (bf16[2,256,128]{2,1,0:T(8,128)(2,1)S(1)}, bf16[2,256,128]{2,1,0:T(8,128)(2,1)S(1)}, u32[]{:S(2)}, u32[]{:S(2)}) collective-permute-start(bf16[2,256,128]{2,1,0:T(8,128)(2,1)S(1)} %get-tuple-element.13), channel_id=1, source_target_pairs={{0,1},{1,0},{2,3},{3,2},{4,5},{5,4},{6,7},{7,6},{8,9},{9,8},{10,11... | collective-permute-start | bytes 393224 | tf_op jit(solution)/shard_map/ppermute | solution.py:129
  72.2 5.9 %collective-permute-start.7 = (bf16[2,256,128]{2,1,0:T(8,128)(2,1)S(1)}, bf16[2,256,128]{2,1,0:T(8,128)(2,1)S(1)}, u32[]{:S(2)}, u32[]{:S(2)}) collective-permute-start(bf16[2,256,128]{2,1,0:T(8,128)(2,1)S(1)} %get-tuple-element.8), channel_id=1, source_target_pairs={{0,8},{2,10},{4,12},{6,14},{8,0},{10,2},{12,4},{14,6},{16,24},{18,... | collective-permute-start | bytes 393224 | tf_op jit(solution)/shard_map/ppermute | solution.py:18
  76.2 5.0 %collective-permute-start.17 = (bf16[2,256,128]{2,1,0:T(8,128)(2,1)S(1)}, bf16[2,256,128]{2,1,0:T(8,128)(2,1)S(1)}, u32[]{:S(2)}, u32[]{:S(2)}) collective-permute-start(bf16[2,256,128]{2,1,0:T(8,128)(2,1)S(1)} %get-tuple-element.10), channel_id=1, source_target_pairs={{0,8},{2,10},{4,12},{6,14},{8,0},{10,2},{12,4},{14,6},{16,24},{18,... | collective-permute-start | bytes 393224 | tf_op jit(solution)/shard_map/ppermute | solution.py:18
  78.2 8.6 %collective-permute-start.8 = (bf16[2,256,256]{2,1,0:T(8,128)(2,1)S(1)}, bf16[2,256,256]{2,1,0:T(8,128)(2,1)S(1)}, u32[]{:S(2)}, u32[]{:S(2)}) collective-permute-start(bf16[2,256,256]{2,1,0:T(8,128)(2,1)S(1)} %pad_maximum_fusion.11), channel_id=1, source_target_pairs={{0,4},{2,6},{4,0},{6,2},{8,12},{10,14},{12,8},{14,10},{16,20},{18,... | collective-permute-start | bytes 786440 | tf_op jit(solution)/shard_map/ppermute | solution.py:18
  81.2 8.5 %collective-permute-start.18 = (bf16[2,256,256]{2,1,0:T(8,128)(2,1)S(1)}, bf16[2,256,256]{2,1,0:T(8,128)(2,1)S(1)}, u32[]{:S(2)}, u32[]{:S(2)}) collective-permute-start(bf16[2,256,256]{2,1,0:T(8,128)(2,1)S(1)} %pad_maximum_fusion.12), channel_id=1, source_target_pairs={{0,4},{2,6},{4,0},{6,2},{8,12},{10,14},{12,8},{14,10},{16,20},{18,... | collective-permute-start | bytes 786440 | tf_op jit(solution)/shard_map/ppermute | solution.py:18
  87.0 2.9 %collective-permute-start.9 = (bf16[2,256,512]{2,1,0:T(8,128)(2,1)S(1)}, bf16[2,256,512]{2,1,0:T(8,128)(2,1)S(1)}, u32[]{:S(2)}, u32[]{:S(2)}) collective-permute-start(bf16[2,256,512]{2,1,0:T(8,128)(2,1)S(1)} %pad_maximum_fusion.7), channel_id=1, source_target_pairs={{0,2},{2,0},{4,6},{6,4},{8,10},{10,8},{12,14},{14,12},{16,18},{18,... | collective-permute-start | bytes 1572872 | tf_op jit(solution)/shard_map/ppermute | solution.py:18
  89.8 2.0 %collective-permute-start.19 = (bf16[2,256,512]{2,1,0:T(8,128)(2,1)S(1)}, bf16[2,256,512]{2,1,0:T(8,128)(2,1)S(1)}, u32[]{:S(2)}, u32[]{:S(2)}) collective-permute-start(bf16[2,256,512]{2,1,0:T(8,128)(2,1)S(1)} %pad_maximum_fusion.8), channel_id=1, source_target_pairs={{0,2},{2,0},{4,6},{6,4},{8,10},{10,8},{12,14},{14,12},{16,18},{18,... | collective-permute-start | bytes 1572872 | tf_op jit(solution)/shard_map/ppermute | solution.py:18

commit v2 on v0

v2 whole, which is shorter than its diff:
```python
import functools

import jax
import jax.numpy as jnp
from jax import lax
from jax.experimental import pallas as pl
from jax.experimental.pallas import tpu as pltpu
from jax.sharding import PartitionSpec as P

BF = jnp.bfloat16
F32 = jnp.float32
LANES = 128
MIB = 1 << 20
VMEM = pl.BlockSpec(memory_space=pltpu.VMEM)
SMEM = pl.BlockSpec(memory_space=pltpu.SMEM)
ANY = pl.BlockSpec(memory_space=pl.ANY)


def swap(value, axis, size, mask):
    return lax.ppermute(value, axis, [(i, i ^ mask) for i in range(size)])


def pick(flag, when_set, when_clear):
    return jnp.where(flag, when_set, when_clear)


def cost(flops, moved):
    return pl.CostEstimate(flops=flops, bytes_accessed=moved, transcendentals=0)


def in_hbm(value):
    return pltpu.with_memory_space_constraint(value, pltpu.HBM)


def params(mib):
    return pltpu.CompilerParams(vmem_limit_bytes=mib * MIB)


def halve(value, flag, send, keep):
    mid = send.shape[1]
    low, high = value[:, :mid], value[:, mid:]
    send[...] = jnp.where(flag, low, high).astype(send.dtype)
    keep[...] = jnp.where(flag, high, low).astype(keep.dtype)


def gemm_kernel(first, cuts, flag_ref, panel, solved, after, send, keep, rows, held, acc, sem_p, sem_s):
    del after
    count, half, _ = rows.shape
    start = 0
    copies = []
    for index, cut in enumerate(cuts):
        span = slice(start, start + cut)
        start += cut
        copy_p = pltpu.make_async_copy(panel.at[first : first + count, :, span], rows.at[:, :, span], sem_p.at[index])
        copy_s = pltpu.make_async_copy(solved.at[span], held.at[span], sem_s.at[index])
        copy_p.start()
        copy_s.start()
        copies.append((span, copy_p, copy_s))
    flag = flag_ref[0] == 1
    for index, (span, copy_p, copy_s) in enumerate(copies):
        copy_p.wait()
        copy_s.wait()
        part = jnp.dot(
            rows[:, :, span].reshape(count * half, cuts[index]), held[span, :], preferred_element_type=F32
        )
        if index:
            part = part + acc[...]
        if index + 1 < len(cuts):
            acc[...] = part
        else:
            halve(part, flag, send, keep)


def gemm(flag, panel, solved, steps, after):
    _, half, depth = panel.shape
    rhs = solved.shape[1]
    count = len(steps)
    pieces = next(p for p in (6, 8, 4, 3, 2, 1) if depth % (p * LANES) == 0)
    cuts = (depth // pieces,) * pieces
    rows = count * half
    return pl.pallas_call(
        functools.partial(gemm_kernel, steps[0], cuts),
        in_specs=[SMEM, ANY, ANY, ANY],
        out_specs=[VMEM] * 2,
        out_shape=[
            jax.ShapeDtypeStruct((rows, rhs // 2), BF),
            jax.ShapeDtypeStruct((rows, rhs // 2), BF),
        ],
        scratch_shapes=[
            pltpu.VMEM((count, half, depth), BF),
            pltpu.VMEM((depth, rhs), BF),
            pltpu.VMEM((rows, rhs), F32),
            pltpu.SemaphoreType.DMA((pieces,)),
            pltpu.SemaphoreType.DMA((pieces,)),
        ],
        compiler_params=params(30),
        cost_estimate=cost(1, 1),
        name="gemm",
    )(flag, in_hbm(panel), in_hbm(solved), after)


def split_kernel(at_ref, keep, got, *pieces):
    width = pieces[0].shape[1]
    for index, piece in enumerate(pieces):
        span = pl.ds(pl.multiple_of(at_ref[index] * width, width), width)
        piece[...] = (keep[:, span].astype(F32) + got[:, span].astype(F32)).astype(piece.dtype)


def split(at, keep, got, count):
    rows, cols = keep.shape
    return pl.pallas_call(
        split_kernel,
        in_specs=[SMEM, VMEM, VMEM],
        out_specs=[VMEM] * count,
        out_shape=[jax.ShapeDtypeStruct((rows, cols // count), BF if i else F32) for i in range(count)],
        compiler_params=params(16),
        name="split",
    )(at, keep, got)


def far_units(step_count):
    units = []
    for step in range(step_count):
        if step + 1 < step_count:
            units += [("inverses", step, piece) for piece in range(2)]
        units += [("window", step, piece) for piece in range(2 * step)]
    return units


def pack_kernel(flag_ref, inverses, window, out, sems):
    half = out.shape[1]
    sources = {"inverses": inverses, "window": window}
    units = far_units(inverses.shape[0])
    mid = out.shape[0]
    for core in range(2):

        @pl.when(flag_ref[0] == core)
        def _():
            copies = []
            for index, (name, step, piece) in enumerate(units[core * mid : (core + 1) * mid]):
                span = slice(piece * half, (piece + 1) * half)
                copy = pltpu.make_async_copy(sources[name].at[step, :, span], out.at[index], sems.at[index])
                copy.start()
                copies.append(copy)
            for copy in copies:
                copy.wait()


def pack(flag, inverses, window):
    step_count, half, _ = inverses.shape
    mid = (len(far_units(step_count)) + 1) // 2
    return pl.pallas_call(
        pack_kernel,
        in_specs=[SMEM, ANY, ANY],
        out_specs=VMEM,
        out_shape=jax.ShapeDtypeStruct((mid, half, half), BF),
        scratch_shapes=[pltpu.SemaphoreType.DMA((mid,))],
        compiler_params=params(4),
        cost_estimate=cost(1, 4 * mid * half * half),
        name="pack",
    )(flag, in_hbm(inverses), in_hbm(window))


def unpack_kernel(flag_ref, here, there, out, sems):
    mid = here.shape[0]
    flag = flag_ref[0]
    copies = [
        pltpu.make_async_copy(here, out.at[pl.ds(flag * mid, mid)], sems.at[0]),
        pltpu.make_async_copy(there, out.at[pl.ds((1 - flag) * mid, mid)], sems.at[1]),
    ]
    for copy in copies:
        copy.start()
    for copy in copies:
        copy.wait()


def unpack(flag, here, there):
    mid, half, _ = here.shape
    return pl.pallas_call(
        unpack_kernel,
        in_specs=[SMEM, ANY, ANY],
        out_specs=VMEM,
        out_shape=jax.ShapeDtypeStruct((2 * mid, half, half), BF),
        scratch_shapes=[pltpu.SemaphoreType.DMA((2,))],
        compiler_params=params(4),
        cost_estimate=cost(1, 8 * mid * half * half),
        name="unpack",
    )(flag, here, there)


def chain_kernel(steps, side_ref, inverses, window, far_w, own_r, far_r, *rest):
    first = steps[0]
    own_out, solved, right = rest[-3:]
    if first:
        before = rest[0]
        solved[: before.shape[0], :] = before[...]
    step_count, half, block = inverses.shape
    units = far_units(step_count)
    side = side_ref[0]
    near_at = pl.multiple_of(side * half, half)
    far_at = pl.multiple_of((1 - side) * half, half)
    for place, step in enumerate(steps):
        near = own_r[place].astype(F32)
        far = far_r[place].astype(F32)
        if step:
            known = solved[: step * block, :]
            near = near - jnp.dot(window[step, :, : step * block], known, preferred_element_type=F32)
            for piece in range(2 * step):
                known = solved[piece * half : (piece + 1) * half, :]
                tile = far_w[units.index(("window", step, piece))]
                far = far - jnp.dot(tile, known, preferred_element_type=F32)
        right[pl.ds(near_at, half), :] = near.astype(BF)
        right[pl.ds(far_at, half), :] = far.astype(BF)
        near = jnp.dot(inverses[step], right[...], preferred_element_type=F32).astype(BF)
        own_out[place] = near
        if step + 1 < step_count:
            far = jnp.zeros_like(far)
            for piece in range(2):
                tile = far_w[units.index(("inverses", step, piece))]
                far = far + jnp.dot(tile, right[piece * half : (piece + 1) * half, :], preferred_element_type=F32)
            solved[pl.ds(pl.multiple_of(step * block + near_at, half), half), :] = near
            solved[pl.ds(pl.multiple_of(step * block + far_at, half), half), :] = far.astype(BF)


def chain(steps, side, inverses, window, far_w, own_r, far_r, before, after):
    count, half, cols = own_r.shape
    block = 2 * half
    args = [side, inverses, window, far_w, own_r, far_r] + ([before] if steps[0] else [])
    return pl.pallas_call(
        functools.partial(chain_kernel, steps),
        in_specs=[SMEM] + [VMEM] * (len(args) - 1) + [ANY] * len(after),
        out_specs=[VMEM, VMEM],
        out_shape=[
            jax.ShapeDtypeStruct((count, half, cols), BF),
            jax.ShapeDtypeStruct((min(steps[-1] + 1, inverses.shape[0] - 1) * block, cols), BF),
        ],
        scratch_shapes=[pltpu.VMEM((block, cols), BF)],
        compiler_params=params(20),
        name="chain",
    )(*args, *after)


def anchor_kernel(*refs):
    del refs


def anchor(value, after):
    return pl.pallas_call(
        anchor_kernel,
        in_specs=[ANY] * (1 + len(after)),
        out_specs=ANY,
        out_shape=jax.ShapeDtypeStruct(value.shape, value.dtype),
        input_output_aliases={0: 0},
        compiler_params=params(1),
        cost_estimate=cost(1, 1),
        name="anchor",
    )(value, *after)


def put_kernel(firsts, at_ref, *refs):
    out, sems = refs[-2:]
    pieces = refs[:-2]
    per = len(pieces) // len(firsts)
    copies = []
    for index, piece in enumerate(pieces):
        count, _, cols = piece.shape
        first = firsts[index // per]
        span = pl.ds(pl.multiple_of(at_ref[index % per] * cols, cols), cols)
        copy = pltpu.make_async_copy(piece, out.at[first : first + count, :, span], sems.at[index])
        copy.start()
        copies.append(copy)
    for copy in copies:
        copy.wait()


def put(firsts, shape, at, pieces):
    return pl.pallas_call(
        functools.partial(put_kernel, firsts),
        in_specs=[SMEM] + [VMEM] * len(pieces),
        out_specs=ANY,
        out_shape=jax.ShapeDtypeStruct(shape, BF),
        scratch_shapes=[pltpu.SemaphoreType.DMA((len(pieces),))],
        compiler_params=params(16),
        name="put",
    )(at, *pieces)


def cut_kernel(at_ref, loads, after, *refs):
    del after
    outs, sems = refs[:-1], refs[-1]
    cols = outs[0].shape[2]
    span = pl.ds(pl.multiple_of(at_ref[0] * cols, cols), cols)
    copies = []
    first = 0
    for index, out in enumerate(outs):
        copy = pltpu.make_async_copy(loads.at[first : first + out.shape[0], :, span], out, sems.at[index])
        first += out.shape[0]
        copy.start()
        copies.append(copy)
    for copy in copies:
        copy.wait()


def cut(at, loads, cols, counts, after):
    half = loads.shape[1]
    return pl.pallas_call(
        cut_kernel,
        in_specs=[SMEM, ANY, ANY],
        out_specs=[VMEM] * len(counts),
        out_shape=[jax.ShapeDtypeStruct((count, half, cols), F32) for count in counts],
        scratch_shapes=[pltpu.SemaphoreType.DMA((len(counts),))],
        compiler_params=params(4),
        cost_estimate=cost(1, 1 << 23),
        name="cut",
    )(at, in_hbm(loads), after)


def shards(size, panel, solved, loads, window, inverses):
    me = lax.axis_index("blk")
    side = lax.axis_index("rows").astype(jnp.int32)[None]
    bits = size.bit_length() - 1
    flags = [(me >> bit) & 1 for bit in range(bits)]
    step_count, half, _ = panel.shape
    block = inverses.shape[2]
    rhs = solved.shape[1]

    halvings = 1
    while halvings < bits and (rhs >> halvings) % (2 * LANES) == 0:
        halvings += 1
    inner = halvings - 1
    cols = rhs >> halvings
    blocks = 1 << halvings
    mine = sum(flags[bit] << (inner - bit) for bit in range(halvings))
    reverse = [sum(((mask >> bit) & 1) << (inner - bit) for bit in range(halvings)) for mask in range(blocks)]
    cross = [2 * mask for mask in range(1 << inner)]
    split_at = jnp.stack([(mine ^ reverse[mask]) & ((1 << inner) - 1) for mask in cross]).astype(jnp.int32)
    put_at = jnp.stack([mine ^ reverse[mask] for mask in cross + [mask + 1 for mask in cross]]).astype(jnp.int32)
    core = flags[0].astype(jnp.int32)[None]

    pair = [(0, 1), (1, 0)]
    sent = pack(core, inverses, window)
    here = lax.ppermute(sent, "rows", pair)

    first_count = (step_count + 1) // 2
    steps_a, steps_b = tuple(range(first_count)), tuple(range(first_count, step_count))
    shape = (step_count, half, rhs)
    together = lax.optimization_barrier

    def scatter(send, keep):
        pieces = split(split_at, keep, swap(send, "blk", size, 1), len(cross))
        return pieces[0], [swap(piece, "blk", size, mask) for mask, piece in zip(cross[1:], pieces[1:])], pieces[1]

    def collect(own, got):
        for piece in got:
            own = own + piece.astype(F32)
        part = own.astype(BF)
        for bit in range(halvings, bits - 1):
            part = (part.astype(F32) + swap(part, "blk", size, 1 << bit).astype(F32)).astype(BF)
        return part, swap(part, "blk", size, 1 << (bits - 1))

    def remain(load, part, got):
        return load - (part.astype(F32) + got.astype(F32)).reshape(load.shape)

    def spread(answer):
        return [swap(answer, "blk", size, mask) for mask in cross[1:]]

    def forward(answer, got):
        pieces = [answer] + got
        return pieces + [swap(piece, "blk", size, 1) for piece in pieces]

    send, keep = gemm(core, panel, solved, steps_a, sent)
    own_a, got_a, after = scatter(send, keep)
    send, keep = gemm(core, panel, solved, steps_b, after)
    send, got_a = together((send, got_a))
    own_b, got_b, after = scatter(send, keep)
    load_a, load_b = cut(mine.astype(jnp.int32)[None], loads, cols, (len(steps_a), len(steps_b)), after)
    part_a, half_a = collect(own_a, got_a)
    half_a = anchor(half_a, [after])
    got_b[-1] = anchor(got_b[-1], [half_a])
    part_b, half_b = collect(own_b, got_b)
    left_a = remain(load_a, part_a, half_a)
    far_a = lax.ppermute(left_a.astype(BF), "rows", pair)
    there = swap(here, "blk", size, 1)
    far_w = unpack(core, here, there)
    answer_a, known = chain(steps_a, side, inverses, window, far_w, left_a, far_a, None, [])
    got_a = spread(answer_a)
    left_b = remain(load_b, part_b, anchor(half_b, [known]))
    far_b = lax.ppermute(left_b.astype(BF), "rows", pair)
    answer_b, _ = chain(steps_b, side, inverses, window, far_w, left_b, far_b, known, [got_a[0]])
    got_b = spread(answer_b)
    return put((steps_a[0], steps_b[0]), shape, put_at, forward(answer_a, got_a) + forward(answer_b, got_b))


def solution(mesh):
    placed = (
        P(None, "rows", "blk"),
        P("blk", None),
        P(None, "rows", None),
        P(None, "rows", None),
        P(None, "rows", None),
    )
    return jax.shard_map(
        functools.partial(shards, mesh.shape["blk"]),
        mesh=mesh,
        in_specs=placed,
        out_specs=P(None, "rows", None),
        check_vma=False,
    )
```

time: 193 us -> 75.7 us (0.39)
  waiting for transfers between devices: 112 us -> 16.9 us
  blocking collectives: 32.2 us -> 0 us
  Pallas kernels: 0 us -> 28.9 us
  matrix products: 24.9 us -> 0 us
  starting transfers between devices: 0.04 us -> 24.8 us
  between operations: 13.5 us -> 0.39 us
  local copies, waits for them, and re-layouts: 7.45 us -> 1.75 us
    reduce_scatter x1 -> x0, waiting for transfers between devices: 71.7 us -> none  [shards(): lax.psum_scatter(partial_value, 'blk', scatter_dimension=2, tiled=True)]
    all_gather x1 -> x0, waiting for transfers between devices: 40.7 us -> none  [shards(): result = lax.all_gather(result, 'blk', axis=2, tiled=True)]
    all_gather x7 -> x0, blocking collectives: 32.2 us -> none  [the longest x4 18.5 us: shards(): lax.all_gather(residual, 'rows', axis=0, tiled=True)]
    pallas_call x0 -> x13, Pallas kernels: none -> 28.9 us  [the longest x2 18.7 us: gemm(): pl.pallas_call(functools.partial(gemm_kernel, steps[0], cuts), in_specs=[...]
    dot_general x11 -> x0, matrix products: 24.9 us -> none  [the longest x1 19.1 us: shards(): jnp.einsum('ksc,cr->ksr', panel, solved, preferred_element_type=jnp.float32)]
    ppermute x0 -> x28, starting transfers between devices: none -> 24.8 us  [the longest x25 18.7 us: swap(): return lax.ppermute(value, axis, [(i, i ^ mask) for i in range(size)])]
    ppermute x0 -> x28, waiting for transfers between devices: none -> 16.9 us  [the longest x25 15.7 us: swap(): return lax.ppermute(value, axis, [(i, i ^ mask) for i in range(size)])]
    all_gather x1 -> x0, local copies, waits for them, and re-layouts: 3.94 us -> none  [shards(): result = lax.all_gather(result, 'blk', axis=2, tiled=True)]
  transfers between devices with their start and end apart: 2 -> 28, of which waited for: 2 -> 14; matrix products, arithmetic and copies ran while one was open for 2% -> 4% of each run, Pallas kernels for 0% -> 34%
where the time goes in v2:
time: 75.7 us; the launch traced here: 75.5 us
  Pallas kernels  28.9 us (38%)
  starting transfers between devices  24.8 us (33%)
  waiting for transfers between devices  16.9 us (22%)
  other arithmetic  2.64 us (3%)
  local copies, waits for them, and re-layouts  1.75 us (2%)
    ppermute x25, starting transfers between devices, swap(): return lax.ppermute(value, axis, [(i, i ^ mask) for i in range(size)])  18.7 us
    pallas_call x2, Pallas kernels, gemm(): pl.pallas_call(functools.partial(gemm_kernel, steps[0], cuts), in_specs=[...  18.7 us
    ppermute x25, waiting for transfers between devices, swap(): return lax.ppermute(value, axis, [(i, i ^ mask) for i in range(size)])  15.7 us
    pallas_call x2, Pallas kernels, chain(): pl.pallas_call(functools.partial(chain_kernel, steps), in_specs=[SMEM] +...  3.89 us
    ppermute x1, starting transfers between devices, shards(): here = lax.ppermute(sent, 'rows', pair)  3 us
    pallas_call x1, Pallas kernels, put(): pl.pallas_call(functools.partial(put_kernel, firsts), in_specs=[SMEM] + [...  1.98 us
    unnamed x10, local copies, waits for them, and re-layouts  1.67 us
    ppermute x1, starting transfers between devices, shards(): far_b = lax.ppermute(left_b.astype(BF), 'rows', pair)  1.56 us
  transfers between devices with their start and end apart: 28, of which 14 were waited for; matrix products, arithmetic and copies ran while one was open for 4% of the time, Pallas kernels for 34%

profile of v2, /device:TPU:0, one launch (start us, length us, event | category | flops | bytes accessed | tf_op | source)
XLA Modules:
  0.0 75.5 jit_solution(12754365309898825383)
XLA Ops:
  0.0 1.4 %pack.1.after = bf16[9,256,256]{2,1,0:T(8,128)(2,1)S(1)} custom-call(s32[1]{0:T(128)} %bitcast.9.flag_ref, bf16[4,256,512]{2,1,0:T(8,128)(2,1)} %inverses.5, bf16[4,256,2048]{2,1,0:T(8,128)(2,1)} %window.5), custom_call_target="tpu_custom_call" | custom-call | flops 1 | bytes 2359296 | tf_op jit(solution)/shard_map/pack/pallas_call | solution.py:152
  1.4 3.0 %collective-permute-start = (bf16[9,256,256]{2,1,0:T(8,128)(2,1)S(1)}, bf16[9,256,256]{2,1,0:T(8,128)(2,1)S(1)}, u32[]{:S(2)}, u32[]{:S(2)}) collective-permute-start(bf16[9,256,256]{2,1,0:T(8,128)(2,1)S(1)} %pack.1.after), channel_id=1, source_target_pairs={{0,1},{1,0},{2,3},{3,2},{4,5},{5,4},{6,7},{7,6},{8,9},{9,8},{10,11... | collective-permute-start | bytes 3538952 | tf_op jit(solution)/shard_map/ppermute | solution.py:342
  4.4 9.8 %gemm.2 = (bf16[512,512]{1,0:T(8,128)(2,1)}, bf16[512,512]{1,0:T(8,128)(2,1)S(1)}) custom-call(s32[1]{0:T(128)} %bitcast.9.flag_ref, bf16[4,256,6144]{2,1,0:T(8,128)(2,1)} %panel.3, bf16[6144,1024]{1,0:T(8,128)(2,1)} %solved.3, bf16[9,256,256]{2,1,0:T(8,128)(2,1)S(1)} %pack.1.after), custom_call_target="tpu_custom_call" | custom-call | flops 1 | bytes 1 | tf_op jit(solution)/shard_map/gemm/pallas_call | solution.py:81
  14.2 0.1 collective-permute-start.2
  14.3 0.1 pad_add_fusion.at_ref
  14.4 2.0 %collective-permute-done.2.got = bf16[512,512]{1,0:T(8,128)(2,1)S(1)} collective-permute-done((bf16[512,512]{1,0:T(8,128)(2,1)}, bf16[512,512]{1,0:T(8,128)(2,1)S(1)}, u32[]{:S(2)}, u32[]{:S(2)}) %collective-permute-start.2) | collective-permute-done | bytes 524320 | tf_op jit(solution)/shard_map/ppermute | solution.py:20
  16.4 0.7 split.2
  17.1 1.6 %collective-permute-start.4 = (bf16[512,128]{1,0:T(8,128)(2,1)S(1)}, bf16[512,128]{1,0:T(8,128)(2,1)S(1)}, u32[]{:S(2)}, u32[]{:S(2)}) collective-permute-start(bf16[512,128]{1,0:T(8,128)(2,1)S(1)} %get-tuple-element.31), channel_id=1, source_target_pairs={{0,8},{2,10},{4,12},{6,14},{8,0},{10,2},{12,4},{14,6},{16,24},{18,... | collective-permute-start | bytes 393224 | tf_op jit(solution)/shard_map/ppermute | solution.py:20
  18.7 1.4 %collective-permute-start.5 = (bf16[512,128]{1,0:T(8,128)(2,1)S(1)}, bf16[512,128]{1,0:T(8,128)(2,1)S(1)}, u32[]{:S(2)}, u32[]{:S(2)}) collective-permute-start(bf16[512,128]{1,0:T(8,128)(2,1)S(1)} %get-tuple-element.32), channel_id=1, source_target_pairs={{0,12},{2,14},{4,8},{6,10},{8,4},{10,6},{12,0},{14,2},{16,28},{18,... | collective-permute-start | bytes 393224 | tf_op jit(solution)/shard_map/ppermute | solution.py:20
  20.1 0.5 collective-permute-start.3
  20.6 9.0 %gemm.3 = (bf16[512,512]{1,0:T(8,128)(2,1)S(1)}, bf16[512,512]{1,0:T(8,128)(2,1)S(1)}) custom-call(s32[1]{0:T(128)} %bitcast.9.flag_ref, bf16[4,256,6144]{2,1,0:T(8,128)(2,1)} %panel.3, bf16[6144,1024]{1,0:T(8,128)(2,1)} %solved.3, bf16[512,128]{1,0:T(8,128)(2,1)S(1)} %get-tuple-element.28.after), custom_call_target="tpu_custom_call" | custom-call | flops 1 | bytes 1 | tf_op jit(solution)/shard_map/gemm/pallas_call | solution.py:81
  29.6 0.0 collective-permute-done.3
  29.6 0.1 collective-permute-start.6
  29.7 0.7 collective-permute-done.here
  30.4 0.1 add_convert_fusion.1
  30.5 2.9 %collective-permute-start.7 = (bf16[512,128]{1,0:T(8,128)(2,1)S(1)}, bf16[512,128]{1,0:T(8,128)(2,1)S(1)}, u32[]{:S(2)}, u32[]{:S(2)}) collective-permute-start(bf16[512,128]{1,0:T(8,128)(2,1)S(1)} %add_convert_fusion.1), channel_id=1, source_target_pairs={{0,16},{2,18},{4,20},{6,22},{8,24},{10,26},{12,28},{14,30},{16,0},... | collective-permute-start | bytes 393224 | tf_op jit(solution)/shard_map/ppermute | solution.py:20
  33.4 0.7 split.3
  34.1 1.6 %collective-permute-start.17 = (bf16[512,128]{1,0:T(8,128)(2,1)S(1)}, bf16[512,128]{1,0:T(8,128)(2,1)S(1)}, u32[]{:S(2)}, u32[]{:S(2)}) collective-permute-start(bf16[512,128]{1,0:T(8,128)(2,1)S(1)} %get-tuple-element.43), channel_id=1, source_target_pairs={{0,8},{2,10},{4,12},{6,14},{8,0},{10,2},{12,4},{14,6},{16,24},{18,... | collective-permute-start | bytes 393224 | tf_op jit(solution)/shard_map/ppermute | solution.py:20
  35.7 1.4 %collective-permute-start.18 = (bf16[512,128]{1,0:T(8,128)(2,1)S(1)}, bf16[512,128]{1,0:T(8,128)(2,1)S(1)}, u32[]{:S(2)}, u32[]{:S(2)}) collective-permute-start(bf16[512,128]{1,0:T(8,128)(2,1)S(1)} %get-tuple-element.44), channel_id=1, source_target_pairs={{0,12},{2,14},{4,8},{6,10},{8,4},{10,6},{12,0},{14,2},{16,28},{18,... | collective-permute-start | bytes 393224 | tf_op jit(solution)/shard_map/ppermute | solution.py:20
  37.1 0.5 collective-permute-start.16
  37.6 1.0 %cut.1 = (f32[2,256,128]{2,1,0:T(8,128)S(1)}, f32[2,256,128]{2,1,0:T(8,128)S(1)}) custom-call(s32[1]{0:T(128)} %bitcast.at_ref, f32[4,256,1024]{2,1,0:T(8,128)} %loads.1, bf16[512,128]{1,0:T(8,128)(2,1)S(1)} %get-tuple-element.34.after.refs_1_), custom_call_target="tpu_custom_call" | custom-call | flops 1 | bytes 8388608 | tf_op jit(solution)/shard_map/cut/pallas_call | solution.py:306
  38.7 1.8 %collective-permute-done.7.refs_0_ = bf16[512,128]{1,0:T(8,128)(2,1)S(1)} collective-permute-done((bf16[512,128]{1,0:T(8,128)(2,1)S(1)}, bf16[512,128]{1,0:T(8,128)(2,1)S(1)}, u32[]{:S(2)}, u32[]{:S(2)}) %collective-permute-start.7) | collective-permute-done | bytes 131104 | tf_op jit(solution)/shard_map/ppermute | solution.py:20
  40.5 0.8 %fusion.1 = (bf16[2,256,128]{2,1,0:T(8,128)(2,1)}, f32[2,256,128]{2,1,0:T(8,128)}) fusion(f32[2,256,128]{2,1,0:T(8,128)S(1)} %get-tuple-element.35, f32[2,256,128]{2,1,0:T(8,128)S(1)} %bitcast.17), kind=kLoop, calls=%fused_computation.6 | loop fusion | flops 131072 | bytes 917504 | tf_op jit(solution)/shard_map/convert_element_type | solution.py:382
  41.3 1.5 %collective-permute-start.8 = (bf16[2,256,128]{2,1,0:T(8,128)(2,1)}, bf16[2,256,128]{2,1,0:T(8,128)(2,1)}, u32[]{:S(2)}, u32[]{:S(2)}) collective-permute-start(bf16[2,256,128]{2,1,0:T(8,128)(2,1)} %get-tuple-element.49), channel_id=1, source_target_pairs={{0,1},{1,0},{2,3},{3,2},{4,5},{5,4},{6,7},{7,6},{8,9},{9,8},{10,11... | collective-permute-start | bytes 393224 | tf_op jit(solution)/shard_map/ppermute | solution.py:382
  42.8 2.4 %collective-permute-done.18.refs_0_ = bf16[512,128]{1,0:T(8,128)(2,1)S(1)} collective-permute-done((bf16[512,128]{1,0:T(8,128)(2,1)S(1)}, bf16[512,128]{1,0:T(8,128)(2,1)S(1)}, u32[]{:S(2)}, u32[]{:S(2)}) %collective-permute-start.18) | collective-permute-done | bytes 131104 | tf_op jit(solution)/shard_map/ppermute | solution.py:20
  45.2 0.0 collective-permute-done.17
  45.2 0.0 collective-permute-done.16
  45.2 0.7 add_convert_fusion
  46.0 0.6 collective-permute-start.19
  46.5 0.5 unpack.1.far_w
  47.1 0.0 collective-permute-done.8.far_r
  47.1 1.6 %copy-done = bf16[4,256,2048]{2,1,0:T(8,128)(2,1)S(1)} copy-done((bf16[4,256,2048]{2,1,0:T(8,128)(2,1)S(1)}, bf16[4,256,2048]{2,1,0:T(8,128)(2,1)}, u32[]{:S(2)}) %copy-start) | copy-done | bytes 4194328
  48.7 0.0 copy-done.2
  48.7 1.8 %chain.2 = (bf16[2,256,128]{2,1,0:T(8,128)(2,1)S(1)}, bf16[1024,128]{1,0:T(8,128)(2,1)S(1)}) custom-call(s32[1]{0:T(128)} %bitcast.8.side_ref, bf16[4,256,512]{2,1,0:T(8,128)(2,1)S(1)} %copy-done.1, bf16[4,256,2048]{2,1,0:T(8,128)(2,1)S(1)} %copy-done, bf16[18,256,256]{2,1,0:T(8,128)(2,1)S(1)} %unpack.1.far_w, f32[2,256,128]{2,1,0:T(8,128)S(1)} %copy-done.2, ...), custom_call_target="tpu_custom_call" | custom-call | tf_op jit(solution)/shard_map/chain/pallas_call | solution.py:229
  50.6 2.8 %collective-permute-start.11 = (bf16[2,256,128]{2,1,0:T(8,128)(2,1)S(1)}, bf16[2,256,128]{2,1,0:T(8,128)(2,1)S(1)}, u32[]{:S(2)}, u32[]{:S(2)}) collective-permute-start(bf16[2,256,128]{2,1,0:T(8,128)(2,1)S(1)} %get-tuple-element.40.refs_0_), channel_id=1, source_target_pairs={{0,12},{2,14},{4,8},{6,10},{8,4},{10,6},{12,0},{14,2},{16,28},{18,... | collective-permute-start | bytes 393224 | tf_op jit(solution)/shard_map/ppermute | solution.py:20
  53.4 0.1 collective-permute-start.10
  53.5 1.3 %collective-permute-done.19.refs_0_ = bf16[512,128]{1,0:T(8,128)(2,1)S(1)} collective-permute-done((bf16[512,128]{1,0:T(8,128)(2,1)}, bf16[512,128]{1,0:T(8,128)(2,1)S(1)}, u32[]{:S(2)}, u32[]{:S(2)}) %collective-permute-start.19) | collective-permute-done | bytes 131104 | tf_op jit(solution)/shard_map/ppermute | solution.py:20
  54.8 0.9 %convert_add_fusion = f32[512,128]{1,0:T(8,128)S(1)} fusion(bf16[512,128]{1,0:T(8,128)(2,1)S(1)} %anchor.5, bf16[512,128]{1,0:T(8,128)(2,1)} %add_convert_fusion), kind=kLoop, calls=%fused_computation | loop fusion | flops 196608 | bytes 524288 | tf_op jit(solution)/shard_map/add | solution.py:362
  55.8 1.6 %collective-permute-start.20 = (bf16[2,256,128]{2,1,0:T(8,128)(2,1)S(1)}, bf16[2,256,128]{2,1,0:T(8,128)(2,1)S(1)}, u32[]{:S(2)}, u32[]{:S(2)}) collective-permute-start(bf16[2,256,128]{2,1,0:T(8,128)(2,1)S(1)} %get-tuple-element.47), channel_id=1, source_target_pairs={{0,1},{1,0},{2,3},{3,2},{4,5},{5,4},{6,7},{7,6},{8,9},{9,8},{10,11... | collective-permute-start | bytes 393224 | tf_op jit(solution)/shard_map/ppermute | solution.py:388
  57.3 0.5 collective-permute-start.9
  57.9 0.1 collective-permute-done.11.refs_3_
  58.0 0.4 collective-permute-start.15
  58.4 1.9 %collective-permute-done.10.refs_2_ = bf16[2,256,128]{2,1,0:T(8,128)(2,1)S(1)} collective-permute-done((bf16[2,256,128]{2,1,0:T(8,128)(2,1)S(1)}, bf16[2,256,128]{2,1,0:T(8,128)(2,1)S(1)}, u32[]{:S(2)}, u32[]{:S(2)}) %collective-permute-start.10) | collective-permute-done | bytes 131104 | tf_op jit(solution)/shard_map/ppermute | solution.py:20
  60.3 0.0 collective-permute-start.14
  60.3 0.5 collective-permute-done.20.far_r
  60.8 1.5 %collective-permute-done.9.rest_1_.refs_1_ = bf16[2,256,128]{2,1,0:T(8,128)(2,1)S(1)} collective-permute-done((bf16[2,256,128]{2,1,0:T(8,128)(2,1)S(1)}, bf16[2,256,128]{2,1,0:T(8,128)(2,1)S(1)}, u32[]{:S(2)}, u32[]{:S(2)}) %collective-permute-start.9) | collective-permute-done | bytes 131104 | tf_op jit(solution)/shard_map/ppermute | solution.py:20
  62.3 2.1 %chain.3 = (bf16[2,256,128]{2,1,0:T(8,128)(2,1)S(1)}, bf16[1536,128]{1,0:T(8,128)(2,1)}) custom-call(s32[1]{0:T(128)} %bitcast.8.side_ref, bf16[4,256,512]{2,1,0:T(8,128)(2,1)S(1)} %copy-done.1, bf16[4,256,2048]{2,1,0:T(8,128)(2,1)S(1)} %copy-done, bf16[18,256,256]{2,1,0:T(8,128)(2,1)S(1)} %unpack.1.far_w, f32[2,256,128]{2,1,0:T(8,128)S(1)} %get-tuple-element.48.own_r, ...), custom_call_target="tpu_custom_call" | custom-call | tf_op jit(solution)/shard_map/chain/pallas_call | solution.py:229
  64.4 1.2 %collective-permute-start.23 = (bf16[2,256,128]{2,1,0:T(8,128)(2,1)S(1)}, bf16[2,256,128]{2,1,0:T(8,128)(2,1)S(1)}, u32[]{:S(2)}, u32[]{:S(2)}) collective-permute-start(bf16[2,256,128]{2,1,0:T(8,128)(2,1)S(1)} %get-tuple-element.46.refs_8_), channel_id=1, source_target_pairs={{0,12},{2,14},{4,8},{6,10},{8,4},{10,6},{12,0},{14,2},{16,28},{18,... | collective-permute-start | bytes 393224 | tf_op jit(solution)/shard_map/ppermute | solution.py:20
  65.6 0.7 collective-permute-start.22
  66.3 0.0 collective-permute-done.12.refs_4_
  66.3 1.5 %collective-permute-start.21 = (bf16[2,256,128]{2,1,0:T(8,128)(2,1)S(1)}, bf16[2,256,128]{2,1,0:T(8,128)(2,1)S(1)}, u32[]{:S(2)}, u32[]{:S(2)}) collective-permute-start(bf16[2,256,128]{2,1,0:T(8,128)(2,1)S(1)} %get-tuple-element.46.refs_8_), channel_id=1, source_target_pairs={{0,4},{2,6},{4,0},{6,2},{8,12},{10,14},{12,8},{14,10},{16,20},{18,... | collective-permute-start | bytes 393224 | tf_op jit(solution)/shard_map/ppermute | solution.py:20
  67.9 0.0 collective-permute-done.15.refs_7_
  67.9 0.5 collective-permute-start.13
  68.4 2.3 %collective-permute-done.23.refs_11_ = bf16[2,256,128]{2,1,0:T(8,128)(2,1)S(1)} collective-permute-done((bf16[2,256,128]{2,1,0:T(8,128)(2,1)S(1)}, bf16[2,256,128]{2,1,0:T(8,128)(2,1)S(1)}, u32[]{:S(2)}, u32[]{:S(2)}) %collective-permute-start.23) | collective-permute-done | bytes 131104 | tf_op jit(solution)/shard_map/ppermute | solution.py:20
  70.7 0.4 collective-permute-done.22.refs_10_
  71.0 0.1 collective-permute-start.26
  71.2 0.8 %collective-permute-done.21.refs_9_ = bf16[2,256,128]{2,1,0:T(8,128)(2,1)S(1)} collective-permute-done((bf16[2,256,128]{2,1,0:T(8,128)(2,1)S(1)}, bf16[2,256,128]{2,1,0:T(8,128)(2,1)S(1)}, u32[]{:S(2)}, u32[]{:S(2)}) %collective-permute-start.21) | collective-permute-done | bytes 131104 | tf_op jit(solution)/shard_map/ppermute | solution.py:20
  72.0 0.0 collective-permute-start.25
  72.0 0.1 stack.50.at_ref
  72.1 0.0 collective-permute-done.24.refs_12_
  72.1 0.0 collective-permute-done.13.refs_5_
  72.1 0.3 collective-permute-done.26.refs_14_
  72.4 1.0 %collective-permute-done.25.refs_13_ = bf16[2,256,128]{2,1,0:T(8,128)(2,1)S(1)} collective-permute-done((bf16[2,256,128]{2,1,0:T(8,128)(2,1)S(1)}, bf16[2,256,128]{2,1,0:T(8,128)(2,1)S(1)}, u32[]{:S(2)}, u32[]{:S(2)}) %collective-permute-start.25) | collective-permute-done | bytes 131104 | tf_op jit(solution)/shard_map/ppermute | solution.py:20
  73.3 2.0 %put.1 = bf16[4,256,1024]{2,1,0:T(8,128)(2,1)} custom-call(s32[8]{0:T(128)S(1)} %stack.50.at_ref, bf16[2,256,128]{2,1,0:T(8,128)(2,1)S(1)} %get-tuple-element.40.refs_0_, bf16[2,256,128]{2,1,0:T(8,128)(2,1)S(1)} %collective-permute-done.9.rest_1_.refs_1_, bf16[2,256,128]{2,1,0:T(8,128)(2,1)S(1)} %collective-permute-done.10.refs_2_, ...), custom_call_target="tpu_custom_call" | custom-call | tf_op jit(solution)/shard_map/put/pallas_call | solution.py:277
  (23 shorter events, 0.1 us)
Async XLA Ops:
  1.4 29.0 %collective-permute-start = (bf16[9,256,256]{2,1,0:T(8,128)(2,1)S(1)}, bf16[9,256,256]{2,1,0:T(8,128)(2,1)S(1)}, u32[]{:S(2)}, u32[]{:S(2)}) collective-permute-start(bf16[9,256,256]{2,1,0:T(8,128)(2,1)S(1)} %pack.1.after), channel_id=1, source_target_pairs={{0,1},{1,0},{2,3},{3,2},{4,5},{5,4},{6,7},{7,6},{8,9},{9,8},{10,11... | collective-permute-start | bytes 3538952 | tf_op jit(solution)/shard_map/ppermute | solution.py:342
  14.2 2.2 %collective-permute-start.2 = (bf16[512,512]{1,0:T(8,128)(2,1)}, bf16[512,512]{1,0:T(8,128)(2,1)S(1)}, u32[]{:S(2)}, u32[]{:S(2)}) collective-permute-start(bf16[512,512]{1,0:T(8,128)(2,1)} %get-tuple-element.27), channel_id=1, source_target_pairs={{0,2},{2,0},{4,6},{6,4},{8,10},{10,8},{12,14},{14,12},{16,18},{18,... | collective-permute-start | bytes 1572872 | tf_op jit(solution)/shard_map/ppermute | solution.py:20
  17.1 12.5 %collective-permute-start.4 = (bf16[512,128]{1,0:T(8,128)(2,1)S(1)}, bf16[512,128]{1,0:T(8,128)(2,1)S(1)}, u32[]{:S(2)}, u32[]{:S(2)}) collective-permute-start(bf16[512,128]{1,0:T(8,128)(2,1)S(1)} %get-tuple-element.31), channel_id=1, source_target_pairs={{0,8},{2,10},{4,12},{6,14},{8,0},{10,2},{12,4},{14,6},{16,24},{18,... | collective-permute-start | bytes 393224 | tf_op jit(solution)/shard_map/ppermute | solution.py:20
  18.7 10.9 %collective-permute-start.5 = (bf16[512,128]{1,0:T(8,128)(2,1)S(1)}, bf16[512,128]{1,0:T(8,128)(2,1)S(1)}, u32[]{:S(2)}, u32[]{:S(2)}) collective-permute-start(bf16[512,128]{1,0:T(8,128)(2,1)S(1)} %get-tuple-element.32), channel_id=1, source_target_pairs={{0,12},{2,14},{4,8},{6,10},{8,4},{10,6},{12,0},{14,2},{16,28},{18,... | collective-permute-start | bytes 393224 | tf_op jit(solution)/shard_map/ppermute | solution.py:20
  20.1 9.5 %collective-permute-start.3 = (bf16[512,128]{1,0:T(8,128)(2,1)S(1)}, bf16[512,128]{1,0:T(8,128)(2,1)S(1)}, u32[]{:S(2)}, u32[]{:S(2)}) collective-permute-start(bf16[512,128]{1,0:T(8,128)(2,1)S(1)} %get-tuple-element.28.after), channel_id=1, source_target_pairs={{0,4},{2,6},{4,0},{6,2},{8,12},{10,14},{12,8},{14,10},{16,20},{18,... | collective-permute-start | bytes 393224 | tf_op jit(solution)/shard_map/ppermute | solution.py:20
  29.6 3.8 %collective-permute-start.6 = (bf16[512,512]{1,0:T(8,128)(2,1)S(1)}, bf16[512,512]{1,0:T(8,128)(2,1)S(1)}, u32[]{:S(2)}, u32[]{:S(2)}) collective-permute-start(bf16[512,512]{1,0:T(8,128)(2,1)S(1)} %get-tuple-element.33), channel_id=1, source_target_pairs={{0,2},{2,0},{4,6},{6,4},{8,10},{10,8},{12,14},{14,12},{16,18},{18,... | collective-permute-start | bytes 1572872 | tf_op jit(solution)/shard_map/ppermute | solution.py:20
  30.4 16.1 %collective-permute-start.1 = (bf16[9,256,256]{2,1,0:T(8,128)(2,1)S(1)}, bf16[9,256,256]{2,1,0:T(8,128)(2,1)S(1)}, u32[]{:S(2)}, u32[]{:S(2)}) collective-permute-start(bf16[9,256,256]{2,1,0:T(8,128)(2,1)S(1)} %collective-permute-done.here), channel_id=1, source_target_pairs={{0,2},{2,0},{4,6},{6,4},{8,10},{10,8},{12,14},{14,12},{16,18},{18,... | collective-permute-start | bytes 3538952 | tf_op jit(solution)/shard_map/ppermute | solution.py:20
  30.5 10.0 %collective-permute-start.7 = (bf16[512,128]{1,0:T(8,128)(2,1)S(1)}, bf16[512,128]{1,0:T(8,128)(2,1)S(1)}, u32[]{:S(2)}, u32[]{:S(2)}) collective-permute-start(bf16[512,128]{1,0:T(8,128)(2,1)S(1)} %add_convert_fusion.1), channel_id=1, source_target_pairs={{0,16},{2,18},{4,20},{6,22},{8,24},{10,26},{12,28},{14,30},{16,0},... | collective-permute-start | bytes 393224 | tf_op jit(solution)/shard_map/ppermute | solution.py:20
  34.1 11.2 %collective-permute-start.17 = (bf16[512,128]{1,0:T(8,128)(2,1)S(1)}, bf16[512,128]{1,0:T(8,128)(2,1)S(1)}, u32[]{:S(2)}, u32[]{:S(2)}) collective-permute-start(bf16[512,128]{1,0:T(8,128)(2,1)S(1)} %get-tuple-element.43), channel_id=1, source_target_pairs={{0,8},{2,10},{4,12},{6,14},{8,0},{10,2},{12,4},{14,6},{16,24},{18,... | collective-permute-start | bytes 393224 | tf_op jit(solution)/shard_map/ppermute | solution.py:20
  35.7 9.5 %collective-permute-start.18 = (bf16[512,128]{1,0:T(8,128)(2,1)S(1)}, bf16[512,128]{1,0:T(8,128)(2,1)S(1)}, u32[]{:S(2)}, u32[]{:S(2)}) collective-permute-start(bf16[512,128]{1,0:T(8,128)(2,1)S(1)} %get-tuple-element.44), channel_id=1, source_target_pairs={{0,12},{2,14},{4,8},{6,10},{8,4},{10,6},{12,0},{14,2},{16,28},{18,... | collective-permute-start | bytes 393224 | tf_op jit(solution)/shard_map/ppermute | solution.py:20
  37.1 8.1 %collective-permute-start.16 = (bf16[512,128]{1,0:T(8,128)(2,1)S(1)}, bf16[512,128]{1,0:T(8,128)(2,1)S(1)}, u32[]{:S(2)}, u32[]{:S(2)}) collective-permute-start(bf16[512,128]{1,0:T(8,128)(2,1)S(1)} %get-tuple-element.34.after.refs_1_), channel_id=1, source_target_pairs={{0,4},{2,6},{4,0},{6,2},{8,12},{10,14},{12,8},{14,10},{16,20},{18,... | collective-permute-start | bytes 393224 | tf_op jit(solution)/shard_map/ppermute | solution.py:20
  38.7 7.3 %copy-start.3 = (f32[2,256,128]{2,1,0:T(8,128)}, f32[2,256,128]{2,1,0:T(8,128)S(1)}, u32[]{:S(2)}) copy-start(f32[2,256,128]{2,1,0:T(8,128)S(1)} %get-tuple-element.41) | copy-start | bytes 786436
  41.3 5.8 %collective-permute-start.8 = (bf16[2,256,128]{2,1,0:T(8,128)(2,1)}, bf16[2,256,128]{2,1,0:T(8,128)(2,1)}, u32[]{:S(2)}, u32[]{:S(2)}) collective-permute-start(bf16[2,256,128]{2,1,0:T(8,128)(2,1)} %get-tuple-element.49), channel_id=1, source_target_pairs={{0,1},{1,0},{2,3},{3,2},{4,5},{5,4},{6,7},{7,6},{8,9},{9,8},{10,11... | collective-permute-start | bytes 393224 | tf_op jit(solution)/shard_map/ppermute | solution.py:382
  45.2 1.8 %copy-start.1 = (bf16[4,256,512]{2,1,0:T(8,128)(2,1)S(1)}, bf16[4,256,512]{2,1,0:T(8,128)(2,1)}, u32[]{:S(2)}) copy-start(bf16[4,256,512]{2,1,0:T(8,128)(2,1)} %inverses.5) | copy-start | bytes 3145732
  46.0 8.8 %collective-permute-start.19 = (bf16[512,128]{1,0:T(8,128)(2,1)}, bf16[512,128]{1,0:T(8,128)(2,1)S(1)}, u32[]{:S(2)}, u32[]{:S(2)}) collective-permute-start(bf16[512,128]{1,0:T(8,128)(2,1)} %add_convert_fusion), channel_id=1, source_target_pairs={{0,16},{2,18},{4,20},{6,22},{8,24},{10,26},{12,28},{14,30},{16,0},... | collective-permute-start | bytes 393224 | tf_op jit(solution)/shard_map/ppermute | solution.py:20
  46.5 2.2 %copy-start = (bf16[4,256,2048]{2,1,0:T(8,128)(2,1)S(1)}, bf16[4,256,2048]{2,1,0:T(8,128)(2,1)}, u32[]{:S(2)}) copy-start(bf16[4,256,2048]{2,1,0:T(8,128)(2,1)} %window.5) | copy-start | bytes 12582916
  46.5 2.2 %copy-start.2 = (f32[2,256,128]{2,1,0:T(8,128)S(1)}, f32[2,256,128]{2,1,0:T(8,128)}, u32[]{:S(2)}) copy-start(f32[2,256,128]{2,1,0:T(8,128)} %get-tuple-element.50.own_r) | copy-start | bytes 786436
  48.7 7.0 %copy-start.4 = (f32[2,256,128]{2,1,0:T(8,128)S(1)}, f32[2,256,128]{2,1,0:T(8,128)}, u32[]{:S(2)}) copy-start(f32[2,256,128]{2,1,0:T(8,128)} %copy-done.3) | copy-start | bytes 786436
  50.6 7.4 %collective-permute-start.11 = (bf16[2,256,128]{2,1,0:T(8,128)(2,1)S(1)}, bf16[2,256,128]{2,1,0:T(8,128)(2,1)S(1)}, u32[]{:S(2)}, u32[]{:S(2)}) collective-permute-start(bf16[2,256,128]{2,1,0:T(8,128)(2,1)S(1)} %get-tuple-element.40.refs_0_), channel_id=1, source_target_pairs={{0,12},{2,14},{4,8},{6,10},{8,4},{10,6},{12,0},{14,2},{16,28},{18,... | collective-permute-start | bytes 393224 | tf_op jit(solution)/shard_map/ppermute | solution.py:20
  53.4 6.9 %collective-permute-start.10 = (bf16[2,256,128]{2,1,0:T(8,128)(2,1)S(1)}, bf16[2,256,128]{2,1,0:T(8,128)(2,1)S(1)}, u32[]{:S(2)}, u32[]{:S(2)}) collective-permute-start(bf16[2,256,128]{2,1,0:T(8,128)(2,1)S(1)} %get-tuple-element.40.refs_0_), channel_id=1, source_target_pairs={{0,8},{2,10},{4,12},{6,14},{8,0},{10,2},{12,4},{14,6},{16,24},{18,... | collective-permute-start | bytes 393224 | tf_op jit(solution)/shard_map/ppermute | solution.py:20
  55.8 5.0 %collective-permute-start.20 = (bf16[2,256,128]{2,1,0:T(8,128)(2,1)S(1)}, bf16[2,256,128]{2,1,0:T(8,128)(2,1)S(1)}, u32[]{:S(2)}, u32[]{:S(2)}) collective-permute-start(bf16[2,256,128]{2,1,0:T(8,128)(2,1)S(1)} %get-tuple-element.47), channel_id=1, source_target_pairs={{0,1},{1,0},{2,3},{3,2},{4,5},{5,4},{6,7},{7,6},{8,9},{9,8},{10,11... | collective-permute-start | bytes 393224 | tf_op jit(solution)/shard_map/ppermute | solution.py:388
  57.3 5.0 %collective-permute-start.9 = (bf16[2,256,128]{2,1,0:T(8,128)(2,1)S(1)}, bf16[2,256,128]{2,1,0:T(8,128)(2,1)S(1)}, u32[]{:S(2)}, u32[]{:S(2)}) collective-permute-start(bf16[2,256,128]{2,1,0:T(8,128)(2,1)S(1)} %get-tuple-element.40.refs_0_), channel_id=1, source_target_pairs={{0,4},{2,6},{4,0},{6,2},{8,12},{10,14},{12,8},{14,10},{16,20},{18,... | collective-permute-start | bytes 393224 | tf_op jit(solution)/shard_map/ppermute | solution.py:20
  57.8 8.5 %collective-permute-start.12 = (bf16[2,256,128]{2,1,0:T(8,128)(2,1)S(1)}, bf16[2,256,128]{2,1,0:T(8,128)(2,1)S(1)}, u32[]{:S(2)}, u32[]{:S(2)}) collective-permute-start(bf16[2,256,128]{2,1,0:T(8,128)(2,1)S(1)} %get-tuple-element.40.refs_0_), channel_id=1, source_target_pairs={{0,2},{2,0},{4,6},{6,4},{8,10},{10,8},{12,14},{14,12},{16,18},{18,... | collective-permute-start | bytes 393224 | tf_op jit(solution)/shard_map/ppermute | solution.py:20
  58.0 9.9 %collective-permute-start.15 = (bf16[2,256,128]{2,1,0:T(8,128)(2,1)S(1)}, bf16[2,256,128]{2,1,0:T(8,128)(2,1)S(1)}, u32[]{:S(2)}, u32[]{:S(2)}) collective-permute-start(bf16[2,256,128]{2,1,0:T(8,128)(2,1)S(1)} %collective-permute-done.11.refs_3_), channel_id=1, source_target_pairs={{0,2},{2,0},{4,6},{6,4},{8,10},{10,8},{12,14},{14,12},{16,18},{18,... | collective-permute-start | bytes 393224 | tf_op jit(solution)/shard_map/ppermute | solution.py:20
  60.3 7.6 %collective-permute-start.14 = (bf16[2,256,128]{2,1,0:T(8,128)(2,1)S(1)}, bf16[2,256,128]{2,1,0:T(8,128)(2,1)S(1)}, u32[]{:S(2)}, u32[]{:S(2)}) collective-permute-start(bf16[2,256,128]{2,1,0:T(8,128)(2,1)S(1)} %collective-permute-done.10.refs_2_), channel_id=1, source_target_pairs={{0,2},{2,0},{4,6},{6,4},{8,10},{10,8},{12,14},{14,12},{16,18},{18,... | collective-permute-start | bytes 393224 | tf_op jit(solution)/shard_map/ppermute | solution.py:20
  64.4 6.3 %collective-permute-start.23 = (bf16[2,256,128]{2,1,0:T(8,128)(2,1)S(1)}, bf16[2,256,128]{2,1,0:T(8,128)(2,1)S(1)}, u32[]{:S(2)}, u32[]{:S(2)}) collective-permute-start(bf16[2,256,128]{2,1,0:T(8,128)(2,1)S(1)} %get-tuple-element.46.refs_8_), channel_id=1, source_target_pairs={{0,12},{2,14},{4,8},{6,10},{8,4},{10,6},{12,0},{14,2},{16,28},{18,... | collective-permute-start | bytes 393224 | tf_op jit(solution)/shard_map/ppermute | solution.py:20
  65.6 5.4 %collective-permute-start.22 = (bf16[2,256,128]{2,1,0:T(8,128)(2,1)S(1)}, bf16[2,256,128]{2,1,0:T(8,128)(2,1)S(1)}, u32[]{:S(2)}, u32[]{:S(2)}) collective-permute-start(bf16[2,256,128]{2,1,0:T(8,128)(2,1)S(1)} %get-tuple-element.46.refs_8_), channel_id=1, source_target_pairs={{0,8},{2,10},{4,12},{6,14},{8,0},{10,2},{12,4},{14,6},{16,24},{18,... | collective-permute-start | bytes 393224 | tf_op jit(solution)/shard_map/ppermute | solution.py:20
  66.3 5.7 %collective-permute-start.21 = (bf16[2,256,128]{2,1,0:T(8,128)(2,1)S(1)}, bf16[2,256,128]{2,1,0:T(8,128)(2,1)S(1)}, u32[]{:S(2)}, u32[]{:S(2)}) collective-permute-start(bf16[2,256,128]{2,1,0:T(8,128)(2,1)S(1)} %get-tuple-element.46.refs_8_), channel_id=1, source_target_pairs={{0,4},{2,6},{4,0},{6,2},{8,12},{10,14},{12,8},{14,10},{16,20},{18,... | collective-permute-start | bytes 393224 | tf_op jit(solution)/shard_map/ppermute | solution.py:20
  67.9 4.2 %collective-permute-start.24 = (bf16[2,256,128]{2,1,0:T(8,128)(2,1)S(1)}, bf16[2,256,128]{2,1,0:T(8,128)(2,1)S(1)}, u32[]{:S(2)}, u32[]{:S(2)}) collective-permute-start(bf16[2,256,128]{2,1,0:T(8,128)(2,1)S(1)} %get-tuple-element.46.refs_8_), channel_id=1, source_target_pairs={{0,2},{2,0},{4,6},{6,4},{8,10},{10,8},{12,14},{14,12},{16,18},{18,... | collective-permute-start | bytes 393224 | tf_op jit(solution)/shard_map/ppermute | solution.py:20
  67.9 4.2 %collective-permute-start.13 = (bf16[2,256,128]{2,1,0:T(8,128)(2,1)S(1)}, bf16[2,256,128]{2,1,0:T(8,128)(2,1)S(1)}, u32[]{:S(2)}, u32[]{:S(2)}) collective-permute-start(bf16[2,256,128]{2,1,0:T(8,128)(2,1)S(1)} %collective-permute-done.9.rest_1_.refs_1_), channel_id=1, source_target_pairs={{0,2},{2,0},{4,6},{6,4},{8,10},{10,8},{12,14},{14,12},{16,18},{18,... | collective-permute-start | bytes 393224 | tf_op jit(solution)/shard_map/ppermute | solution.py:20
  70.7 1.4 %collective-permute-start.27 = (bf16[2,256,128]{2,1,0:T(8,128)(2,1)S(1)}, bf16[2,256,128]{2,1,0:T(8,128)(2,1)S(1)}, u32[]{:S(2)}, u32[]{:S(2)}) collective-permute-start(bf16[2,256,128]{2,1,0:T(8,128)(2,1)S(1)} %collective-permute-done.23.refs_11_), channel_id=1, source_target_pairs={{0,2},{2,0},{4,6},{6,4},{8,10},{10,8},{12,14},{14,12},{16,18},{18,... | collective-permute-start | bytes 393224 | tf_op jit(solution)/shard_map/ppermute | solution.py:20
  71.0 1.3 %collective-permute-start.26 = (bf16[2,256,128]{2,1,0:T(8,128)(2,1)S(1)}, bf16[2,256,128]{2,1,0:T(8,128)(2,1)S(1)}, u32[]{:S(2)}, u32[]{:S(2)}) collective-permute-start(bf16[2,256,128]{2,1,0:T(8,128)(2,1)S(1)} %collective-permute-done.22.refs_10_), channel_id=1, source_target_pairs={{0,2},{2,0},{4,6},{6,4},{8,10},{10,8},{12,14},{14,12},{16,18},{18,... | collective-permute-start | bytes 393224 | tf_op jit(solution)/shard_map/ppermute | solution.py:20
  72.0 1.3 %collective-permute-start.25 = (bf16[2,256,128]{2,1,0:T(8,128)(2,1)S(1)}, bf16[2,256,128]{2,1,0:T(8,128)(2,1)S(1)}, u32[]{:S(2)}, u32[]{:S(2)}) collective-permute-start(bf16[2,256,128]{2,1,0:T(8,128)(2,1)S(1)} %collective-permute-done.21.refs_9_), channel_id=1, source_target_pairs={{0,2},{2,0},{4,6},{6,4},{8,10},{10,8},{12,14},{14,12},{16,18},{18,... | collective-permute-start | bytes 393224 | tf_op jit(solution)/shard_map/ppermute | solution.py:20

commit v3 on v2

--- a/solution.py
+++ b/solution.py
@@ -43,8 +43,8 @@
     keep[...] = jnp.where(flag, high, low).astype(keep.dtype)
 
 
-def gemm_kernel(first, cuts, flag_ref, panel, solved, after, send, keep, rows, held, acc, sem_p, sem_s):
-    del after
+def gemm_kernel(first, cuts, flag_ref, panel, solved, *refs):
+    send, keep, rows, held, acc, sem_p, sem_s = refs[-7:]
     count, half, _ = rows.shape
     start = 0
     copies = []
@@ -77,10 +77,12 @@
     count = len(steps)
     pieces = next(p for p in (6, 8, 4, 3, 2, 1) if depth % (p * LANES) == 0)
     cuts = (depth // pieces,) * pieces
+    if cuts[-1] % (2 * LANES) == 0:
+        cuts = cuts[:-1] + (cuts[-1] // 2,) * 2
     rows = count * half
     return pl.pallas_call(
         functools.partial(gemm_kernel, steps[0], cuts),
-        in_specs=[SMEM, ANY, ANY, ANY],
+        in_specs=[SMEM, ANY, ANY] + [ANY] * len(after),
         out_specs=[VMEM] * 2,
         out_shape=[
             jax.ShapeDtypeStruct((rows, rhs // 2), BF),
@@ -90,13 +92,13 @@
             pltpu.VMEM((count, half, depth), BF),
             pltpu.VMEM((depth, rhs), BF),
             pltpu.VMEM((rows, rhs), F32),
-            pltpu.SemaphoreType.DMA((pieces,)),
-            pltpu.SemaphoreType.DMA((pieces,)),
+            pltpu.SemaphoreType.DMA((len(cuts),)),
+            pltpu.SemaphoreType.DMA((len(cuts),)),
         ],
         compiler_params=params(30),
         cost_estimate=cost(1, 1),
         name="gemm",
-    )(flag, in_hbm(panel), in_hbm(solved), after)
+    )(flag, in_hbm(panel), in_hbm(solved), *after)
 
 
 def split_kernel(at_ref, keep, got, *pieces):
@@ -118,19 +120,20 @@
     )(at, keep, got)
 
 
-def far_units(step_count):
+def far_units(groups):
     units = []
-    for step in range(step_count):
-        if step + 1 < step_count:
-            units += [("inverses", step, piece) for piece in range(2)]
-        units += [("window", step, piece) for piece in range(2 * step)]
+    for steps in groups:
+        for step in steps:
+            if step != groups[-1][-1]:
+                units += [("inverses", step, piece) for piece in range(2)]
+            units += [("window", step, piece) for piece in range(2 * steps[0], 2 * step)]
     return units
 
 
-def pack_kernel(flag_ref, inverses, window, out, sems):
+def pack_kernel(units, flag_ref, inverses, window, after, out, sems):
+    del after
     half = out.shape[1]
     sources = {"inverses": inverses, "window": window}
-    units = far_units(inverses.shape[0])
     mid = out.shape[0]
     for core in range(2):
 
@@ -146,19 +149,19 @@
                 copy.wait()
 
 
-def pack(flag, inverses, window):
-    step_count, half, _ = inverses.shape
-    mid = (len(far_units(step_count)) + 1) // 2
-    return pl.pallas_call(
-        pack_kernel,
-        in_specs=[SMEM, ANY, ANY],
+def pack(units, flag, inverses, window, after):
+    half = inverses.shape[1]
+    mid = (len(units) + 1) // 2
+    return pl.pallas_call(
+        functools.partial(pack_kernel, units),
+        in_specs=[SMEM, ANY, ANY, ANY],
         out_specs=VMEM,
         out_shape=jax.ShapeDtypeStruct((mid, half, half), BF),
         scratch_shapes=[pltpu.SemaphoreType.DMA((mid,))],
         compiler_params=params(4),
         cost_estimate=cost(1, 4 * mid * half * half),
         name="pack",
-    )(flag, in_hbm(inverses), in_hbm(window))
+    )(flag, in_hbm(inverses), in_hbm(window), after)
 
 
 def unpack_kernel(flag_ref, here, there, out, sems):
@@ -188,56 +191,70 @@
     )(flag, here, there)
 
 
-def chain_kernel(steps, side_ref, inverses, window, far_w, own_r, far_r, *rest):
-    first = steps[0]
-    own_out, solved, right = rest[-3:]
-    if first:
-        before = rest[0]
-        solved[: before.shape[0], :] = before[...]
-    step_count, half, block = inverses.shape
-    units = far_units(step_count)
+def chain_kernel(units, steps, last, side_ref, inverses, window, far_w, own_r, far_r, *refs):
+    own_out, solved, right = refs[-3:]
+    _, half, block = inverses.shape
+    start = steps[0]
     side = side_ref[0]
     near_at = pl.multiple_of(side * half, half)
     far_at = pl.multiple_of((1 - side) * half, half)
     for place, step in enumerate(steps):
         near = own_r[place].astype(F32)
         far = far_r[place].astype(F32)
-        if step:
-            known = solved[: step * block, :]
-            near = near - jnp.dot(window[step, :, : step * block], known, preferred_element_type=F32)
-            for piece in range(2 * step):
+        if place:
+            known = solved[: place * block, :]
+            near = near - jnp.dot(window[step, :, start * block : step * block], known, preferred_element_type=F32)
+            for piece in range(2 * place):
                 known = solved[piece * half : (piece + 1) * half, :]
-                tile = far_w[units.index(("window", step, piece))]
+                tile = far_w[units.index(("window", step, 2 * start + piece))]
                 far = far - jnp.dot(tile, known, preferred_element_type=F32)
         right[pl.ds(near_at, half), :] = near.astype(BF)
         right[pl.ds(far_at, half), :] = far.astype(BF)
         near = jnp.dot(inverses[step], right[...], preferred_element_type=F32).astype(BF)
         own_out[place] = near
-        if step + 1 < step_count:
+        if step != last:
             far = jnp.zeros_like(far)
             for piece in range(2):
                 tile = far_w[units.index(("inverses", step, piece))]
                 far = far + jnp.dot(tile, right[piece * half : (piece + 1) * half, :], preferred_element_type=F32)
-            solved[pl.ds(pl.multiple_of(step * block + near_at, half), half), :] = near
-            solved[pl.ds(pl.multiple_of(step * block + far_at, half), half), :] = far.astype(BF)
-
-
-def chain(steps, side, inverses, window, far_w, own_r, far_r, before, after):
+            solved[pl.ds(pl.multiple_of(place * block + near_at, half), half), :] = near
+            solved[pl.ds(pl.multiple_of(place * block + far_at, half), half), :] = far.astype(BF)
+
+
+def chain(units, steps, side, inverses, window, far_w, own_r, far_r, after):
     count, half, cols = own_r.shape
     block = 2 * half
-    args = [side, inverses, window, far_w, own_r, far_r] + ([before] if steps[0] else [])
-    return pl.pallas_call(
-        functools.partial(chain_kernel, steps),
+    last = inverses.shape[0] - 1
+    args = [side, inverses, window, far_w, own_r, far_r]
+    return pl.pallas_call(
+        functools.partial(chain_kernel, units, steps, last),
         in_specs=[SMEM] + [VMEM] * (len(args) - 1) + [ANY] * len(after),
         out_specs=[VMEM, VMEM],
         out_shape=[
             jax.ShapeDtypeStruct((count, half, cols), BF),
-            jax.ShapeDtypeStruct((min(steps[-1] + 1, inverses.shape[0] - 1) * block, cols), BF),
+            jax.ShapeDtypeStruct((min(count, last - steps[0]) * block, cols), BF),
         ],
         scratch_shapes=[pltpu.VMEM((block, cols), BF)],
-        compiler_params=params(20),
+        compiler_params=params(8),
         name="chain",
     )(*args, *after)
+
+
+def couple_kernel(load, window, known, out):
+    count, half, _ = load.shape
+    flat = window[-count:, :, : known.shape[0]].reshape(count * half, known.shape[0])
+    out[...] = load[...] - jnp.dot(flat, known[...], preferred_element_type=F32).reshape(load.shape)
+
+
+def couple(load, window, known):
+    return pl.pallas_call(
+        couple_kernel,
+        in_specs=[VMEM] * 3,
+        out_specs=VMEM,
+        out_shape=jax.ShapeDtypeStruct(load.shape, F32),
+        compiler_params=params(8),
+        name="couple",
+    )(load, window, known)
 
 
 def anchor_kernel(*refs):
@@ -338,12 +355,10 @@
     core = flags[0].astype(jnp.int32)[None]
 
     pair = [(0, 1), (1, 0)]
-    sent = pack(core, inverses, window)
-    here = lax.ppermute(sent, "rows", pair)
-
     first_count = (step_count + 1) // 2
     steps_a, steps_b = tuple(range(first_count)), tuple(range(first_count, step_count))
     shape = (step_count, half, rhs)
+    units = far_units((steps_a, steps_b))
     together = lax.optimization_barrier
 
     def scatter(send, keep):
@@ -368,25 +383,29 @@
         pieces = [answer] + got
         return pieces + [swap(piece, "blk", size, 1) for piece in pieces]
 
-    send, keep = gemm(core, panel, solved, steps_a, sent)
+    send, keep = gemm(core, panel, solved, steps_a, [])
+    sent = pack(units, core, inverses, window, send)
+    here = lax.ppermute(sent, "rows", pair)
     own_a, got_a, after = scatter(send, keep)
-    send, keep = gemm(core, panel, solved, steps_b, after)
+    send, keep = gemm(core, panel, solved, steps_b, [after, sent])
     send, got_a = together((send, got_a))
     own_b, got_b, after = scatter(send, keep)
     load_a, load_b = cut(mine.astype(jnp.int32)[None], loads, cols, (len(steps_a), len(steps_b)), after)
     part_a, half_a = collect(own_a, got_a)
-    half_a = anchor(half_a, [after])
+    here = anchor(here, [after])
+    half_a = anchor(half_a, [load_a])
     got_b[-1] = anchor(got_b[-1], [half_a])
     part_b, half_b = collect(own_b, got_b)
     left_a = remain(load_a, part_a, half_a)
     far_a = lax.ppermute(left_a.astype(BF), "rows", pair)
     there = swap(here, "blk", size, 1)
     far_w = unpack(core, here, there)
-    answer_a, known = chain(steps_a, side, inverses, window, far_w, left_a, far_a, None, [])
+    answer_a, known = chain(units, steps_a, side, inverses, window, far_w, left_a, far_a, [])
     got_a = spread(answer_a)
-    left_b = remain(load_b, part_b, anchor(half_b, [known]))
+    load_b = couple(load_b, window, known)
+    left_b = remain(load_b, part_b, anchor(half_b, [load_b]))
     far_b = lax.ppermute(left_b.astype(BF), "rows", pair)
-    answer_b, _ = chain(steps_b, side, inverses, window, far_w, left_b, far_b, known, [got_a[0]])
+    answer_b, _ = chain(units, steps_b, side, inverses, window, far_w, left_b, far_b, got_a)
     got_b = spread(answer_b)
     return put((steps_a[0], steps_b[0]), shape, put_at, forward(answer_a, got_a) + forward(answer_b, got_b))
 

time: 75.7 us -> 72.1 us (0.952)
  other arithmetic: 2.64 us -> 0.37 us
  Pallas kernels: 28.9 us -> 26.8 us
  waiting for transfers between devices: 16.9 us -> 18 us
    ppermute x25, starting transfers between devices: 18.7 us -> 21.1 us  [swap(): return lax.ppermute(value, axis, [(i, i ^ mask) for i in range(size)])]
    ppermute x25, waiting for transfers between devices: 15.7 us -> 18 us  [swap(): return lax.ppermute(value, axis, [(i, i ^ mask) for i in range(size)])]
    pallas_call x3 -> x4, Pallas kernels: 5.29 us -> 3.78 us  [the longest x2 2.14 us: chain(): pl.pallas_call(functools.partial(chain_kernel, units, steps, last), in_sp...]
    ppermute x1, starting transfers between devices: 3 us -> 1.93 us  [shards(): here = lax.ppermute(sent, 'rows', pair)]
    ppermute x1, starting transfers between devices: 1.54 us -> 0.56 us  [shards(): far_a = lax.ppermute(left_a.astype(BF), 'rows', pair)]
    ppermute x1, starting transfers between devices: 1.56 us -> 0.59 us  [shards(): far_b = lax.ppermute(left_b.astype(BF), 'rows', pair)]
    add x2, other arithmetic: 0.96 us -> 0.06 us  [remain(): return load - (part.astype(F32) + got.astype(F32)).reshape(load.shape)]
    unnamed x10 -> x6, local copies, waits for them, and re-layouts: 1.67 us -> 2.19 us
  transfers between devices with their start and end apart: 28 -> 28, of which waited for: 14 -> 12; matrix products, arithmetic and copies ran while one was open for 4% -> 1% of each run, Pallas kernels for 34% -> 21%
where the time goes in v3:
time: 72.1 us; the launch traced here: 71.9 us
  Pallas kernels  26.8 us (37%)
  starting transfers between devices  24.2 us (34%)
  waiting for transfers between devices  18 us (25%)
  local copies, waits for them, and re-layouts  2.27 us (3%)
    ppermute x25, starting transfers between devices, swap(): return lax.ppermute(value, axis, [(i, i ^ mask) for i in range(size)])  21.1 us
    pallas_call x2, Pallas kernels, gemm(): pl.pallas_call(functools.partial(gemm_kernel, steps[0], cuts), in_specs=[...  18.1 us
    ppermute x25, waiting for transfers between devices, swap(): return lax.ppermute(value, axis, [(i, i ^ mask) for i in range(size)])  18 us
    unnamed x6, local copies, waits for them, and re-layouts  2.19 us
    pallas_call x2, Pallas kernels, chain(): pl.pallas_call(functools.partial(chain_kernel, units, steps, last), in_sp...  2.14 us
    pallas_call x1, Pallas kernels, put(): pl.pallas_call(functools.partial(put_kernel, firsts), in_specs=[SMEM] + [...  1.98 us
    ppermute x1, starting transfers between devices, shards(): here = lax.ppermute(sent, 'rows', pair)  1.93 us
  transfers between devices with their start and end apart: 28, of which 12 were waited for; matrix products, arithmetic and copies ran while one was open for 1% of the time, Pallas kernels for 21%

profile of v3, /device:TPU:0, one launch (start us, length us, event | category | flops | bytes accessed | tf_op | source)
XLA Modules:
  0.0 71.9 jit_solution(12968084589352948282)
XLA Ops:
  0.0 9.0 %gemm.2 = (bf16[512,512]{1,0:T(8,128)(2,1)S(1)}, bf16[512,512]{1,0:T(8,128)(2,1)S(1)}) custom-call(s32[1]{0:T(128)} %bitcast.9.flag_ref, bf16[4,256,6144]{2,1,0:T(8,128)(2,1)} %panel.3, bf16[6144,1024]{1,0:T(8,128)(2,1)} %solved.3), custom_call_target="tpu_custom_call" | custom-call | flops 1 | bytes 1 | tf_op jit(solution)/shard_map/gemm/pallas_call | solution.py:83
  9.0 0.5 collective-permute-start.1
  9.6 0.1 pad_add_fusion.at_ref
  9.6 1.5 %collective-permute-done.1.got = bf16[512,512]{1,0:T(8,128)(2,1)S(1)} collective-permute-done((bf16[512,512]{1,0:T(8,128)(2,1)S(1)}, bf16[512,512]{1,0:T(8,128)(2,1)S(1)}, u32[]{:S(2)}, u32[]{:S(2)}) %collective-permute-start.1) | collective-permute-done | bytes 524320 | tf_op jit(solution)/shard_map/ppermute | solution.py:20
  11.1 0.7 split.2
  11.8 3.0 %collective-permute-start.3 = (bf16[512,128]{1,0:T(8,128)(2,1)S(1)}, bf16[512,128]{1,0:T(8,128)(2,1)S(1)}, u32[]{:S(2)}, u32[]{:S(2)}) collective-permute-start(bf16[512,128]{1,0:T(8,128)(2,1)S(1)} %get-tuple-element.31), channel_id=1, source_target_pairs={{0,8},{2,10},{4,12},{6,14},{8,0},{10,2},{12,4},{14,6},{16,24},{18,... | collective-permute-start | bytes 393224 | tf_op jit(solution)/shard_map/ppermute | solution.py:20
  14.8 1.4 %collective-permute-start.4 = (bf16[512,128]{1,0:T(8,128)(2,1)S(1)}, bf16[512,128]{1,0:T(8,128)(2,1)S(1)}, u32[]{:S(2)}, u32[]{:S(2)}) collective-permute-start(bf16[512,128]{1,0:T(8,128)(2,1)S(1)} %get-tuple-element.32), channel_id=1, source_target_pairs={{0,12},{2,14},{4,8},{6,10},{8,4},{10,6},{12,0},{14,2},{16,28},{18,... | collective-permute-start | bytes 393224 | tf_op jit(solution)/shard_map/ppermute | solution.py:20
  16.2 0.1 collective-permute-start.2
  16.3 1.2 %pack.1.refs_1_ = bf16[5,256,256]{2,1,0:T(8,128)(2,1)S(1)} custom-call(s32[1]{0:T(128)} %bitcast.9.flag_ref, bf16[4,256,512]{2,1,0:T(8,128)(2,1)} %inverses.5, bf16[4,256,2048]{2,1,0:T(8,128)(2,1)} %window.7, bf16[512,512]{1,0:T(8,128)(2,1)S(1)} %get-tuple-element.26.after), custom_call_target="tpu_custom_call" | custom-call | flops 1 | bytes 1310720 | tf_op jit(solution)/shard_map/pack/pallas_call | solution.py:155
  17.6 1.9 %collective-permute-start = (bf16[5,256,256]{2,1,0:T(8,128)(2,1)S(1)}, bf16[5,256,256]{2,1,0:T(8,128)(2,1)S(1)}, u32[]{:S(2)}, u32[]{:S(2)}) collective-permute-start(bf16[5,256,256]{2,1,0:T(8,128)(2,1)S(1)} %pack.1.refs_1_), channel_id=1, source_target_pairs={{0,1},{1,0},{2,3},{3,2},{4,5},{5,4},{6,7},{7,6},{8,9},{9,8},{10,11... | collective-permute-start | bytes 1966088 | tf_op jit(solution)/shard_map/ppermute | solution.py:388
  19.5 9.0 %gemm.3 = (bf16[512,512]{1,0:T(8,128)(2,1)S(1)}, bf16[512,512]{1,0:T(8,128)(2,1)S(1)}) custom-call(s32[1]{0:T(128)} %bitcast.9.flag_ref, bf16[4,256,6144]{2,1,0:T(8,128)(2,1)} %panel.3, bf16[6144,1024]{1,0:T(8,128)(2,1)} %solved.3, bf16[512,128]{1,0:T(8,128)(2,1)S(1)} %get-tuple-element.28.refs_0_, bf16[5,256,256]{2,1,0:T(8,128)(2,1)S(1)} %pack.1.refs_1_), custom_call_target="tpu_custom_call" | custom-call | flops 1 | bytes 1 | tf_op jit(solution)/shard_map/gemm/pallas_call | solution.py:83
  28.5 0.0 collective-permute-done.3
  28.5 0.0 collective-permute-done.4
  28.6 0.1 collective-permute-start.5
  28.6 0.1 add_convert_fusion.1
  28.7 2.7 %collective-permute-start.7 = (bf16[512,128]{1,0:T(8,128)(2,1)S(1)}, bf16[512,128]{1,0:T(8,128)(2,1)S(1)}, u32[]{:S(2)}, u32[]{:S(2)}) collective-permute-start(bf16[512,128]{1,0:T(8,128)(2,1)S(1)} %add_convert_fusion.1), channel_id=1, source_target_pairs={{0,16},{2,18},{4,20},{6,22},{8,24},{10,26},{12,28},{14,30},{16,0},... | collective-permute-start | bytes 393224 | tf_op jit(solution)/shard_map/ppermute | solution.py:20
  31.4 0.0 collective-permute-done.5.got
  31.4 0.7 split.3
  32.1 1.6 %collective-permute-start.17 = (bf16[512,128]{1,0:T(8,128)(2,1)S(1)}, bf16[512,128]{1,0:T(8,128)(2,1)S(1)}, u32[]{:S(2)}, u32[]{:S(2)}) collective-permute-start(bf16[512,128]{1,0:T(8,128)(2,1)S(1)} %get-tuple-element.44), channel_id=1, source_target_pairs={{0,8},{2,10},{4,12},{6,14},{8,0},{10,2},{12,4},{14,6},{16,24},{18,... | collective-permute-start | bytes 393224 | tf_op jit(solution)/shard_map/ppermute | solution.py:20
  33.7 1.4 %collective-permute-start.18 = (bf16[512,128]{1,0:T(8,128)(2,1)S(1)}, bf16[512,128]{1,0:T(8,128)(2,1)S(1)}, u32[]{:S(2)}, u32[]{:S(2)}) collective-permute-start(bf16[512,128]{1,0:T(8,128)(2,1)S(1)} %get-tuple-element.45), channel_id=1, source_target_pairs={{0,12},{2,14},{4,8},{6,10},{8,4},{10,6},{12,0},{14,2},{16,28},{18,... | collective-permute-start | bytes 393224 | tf_op jit(solution)/shard_map/ppermute | solution.py:20
  35.1 0.5 collective-permute-start.16
  35.6 0.0 collective-permute-start.6
  35.6 1.1 %cut.1 = (f32[2,256,128]{2,1,0:T(8,128)S(1)}, f32[2,256,128]{2,1,0:T(8,128)S(1)}) custom-call(s32[1]{0:T(128)} %bitcast.at_ref, f32[4,256,1024]{2,1,0:T(8,128)} %loads.1, bf16[512,128]{1,0:T(8,128)(2,1)S(1)} %get-tuple-element.34.refs_1_.after), custom_call_target="tpu_custom_call" | custom-call | flops 1 | bytes 8388608 | tf_op jit(solution)/shard_map/cut/pallas_call | solution.py:323
  36.8 1.7 %collective-permute-done.7.refs_0_ = bf16[512,128]{1,0:T(8,128)(2,1)S(1)} collective-permute-done((bf16[512,128]{1,0:T(8,128)(2,1)S(1)}, bf16[512,128]{1,0:T(8,128)(2,1)S(1)}, u32[]{:S(2)}, u32[]{:S(2)}) %collective-permute-start.7) | collective-permute-done | bytes 131104 | tf_op jit(solution)/shard_map/ppermute | solution.py:20
  38.6 0.6 collective-permute-start.8
  39.1 4.1 %collective-permute-done.18.refs_0_ = bf16[512,128]{1,0:T(8,128)(2,1)S(1)} collective-permute-done((bf16[512,128]{1,0:T(8,128)(2,1)S(1)}, bf16[512,128]{1,0:T(8,128)(2,1)S(1)}, u32[]{:S(2)}, u32[]{:S(2)}) %collective-permute-start.18) | collective-permute-done | bytes 131104 | tf_op jit(solution)/shard_map/ppermute | solution.py:20
  43.2 0.0 collective-permute-done.17
  43.2 0.0 collective-permute-done.16
  43.2 0.1 add_convert_fusion
  43.3 1.5 %collective-permute-start.19 = (bf16[512,128]{1,0:T(8,128)(2,1)S(1)}, bf16[512,128]{1,0:T(8,128)(2,1)S(1)}, u32[]{:S(2)}, u32[]{:S(2)}) collective-permute-start(bf16[512,128]{1,0:T(8,128)(2,1)S(1)} %add_convert_fusion), channel_id=1, source_target_pairs={{0,16},{2,18},{4,20},{6,22},{8,24},{10,26},{12,28},{14,30},{16,0},... | collective-permute-start | bytes 393224 | tf_op jit(solution)/shard_map/ppermute | solution.py:20
  44.8 0.0 collective-permute-done.6.there
  44.8 0.4 unpack.1.far_w
  45.2 0.0 copy-start
  45.3 2.2 %copy-done = bf16[4,256,2048]{2,1,0:T(8,128)(2,1)S(1)} copy-done((bf16[4,256,2048]{2,1,0:T(8,128)(2,1)S(1)}, bf16[4,256,2048]{2,1,0:T(8,128)(2,1)}, u32[]{:S(2)}) %copy-start) | copy-done | bytes 4194328
  47.4 0.9 %chain.2 = (bf16[2,256,128]{2,1,0:T(8,128)(2,1)S(1)}, bf16[1024,128]{1,0:T(8,128)(2,1)S(1)}) custom-call(s32[1]{0:T(128)} %bitcast.8.side_ref, bf16[4,256,512]{2,1,0:T(8,128)(2,1)S(1)} %copy-done.2, bf16[4,256,2048]{2,1,0:T(8,128)(2,1)S(1)} %copy-done, bf16[10,256,256]{2,1,0:T(8,128)(2,1)S(1)} %unpack.1.far_w, f32[2,256,128]{2,1,0:T(8,128)S(1)} %get-tuple-element.50.own_r, ...), custom_call_target="tpu_custom_call" | custom-call | tf_op jit(solution)/shard_map/chain/pallas_call | solution.py:229
  48.3 2.8 %collective-permute-start.11 = (bf16[2,256,128]{2,1,0:T(8,128)(2,1)S(1)}, bf16[2,256,128]{2,1,0:T(8,128)(2,1)S(1)}, u32[]{:S(2)}, u32[]{:S(2)}) collective-permute-start(bf16[2,256,128]{2,1,0:T(8,128)(2,1)S(1)} %get-tuple-element.40.refs_0_), channel_id=1, source_target_pairs={{0,12},{2,14},{4,8},{6,10},{8,4},{10,6},{12,0},{14,2},{16,28},{18,... | collective-permute-start | bytes 393224 | tf_op jit(solution)/shard_map/ppermute | solution.py:20
  51.2 0.1 collective-permute-start.10
  51.3 0.4 couple.1.refs_1_
  51.7 0.2 collective-permute-done.19.refs_0_
  52.0 0.1 fusion
  52.0 0.6 collective-permute-start.20
  52.6 1.2 %collective-permute-start.9 = (bf16[2,256,128]{2,1,0:T(8,128)(2,1)S(1)}, bf16[2,256,128]{2,1,0:T(8,128)(2,1)S(1)}, u32[]{:S(2)}, u32[]{:S(2)}) collective-permute-start(bf16[2,256,128]{2,1,0:T(8,128)(2,1)S(1)} %get-tuple-element.40.refs_0_), channel_id=1, source_target_pairs={{0,4},{2,6},{4,0},{6,2},{8,12},{10,14},{12,8},{14,10},{16,20},{18,... | collective-permute-start | bytes 393224 | tf_op jit(solution)/shard_map/ppermute | solution.py:20
  53.8 0.0 collective-permute-start.12
  53.8 1.9 %collective-permute-done.11.refs_2_.refs_3_ = bf16[2,256,128]{2,1,0:T(8,128)(2,1)S(1)} collective-permute-done((bf16[2,256,128]{2,1,0:T(8,128)(2,1)S(1)}, bf16[2,256,128]{2,1,0:T(8,128)(2,1)S(1)}, u32[]{:S(2)}, u32[]{:S(2)}) %collective-permute-start.11) | collective-permute-done | bytes 131104 | tf_op jit(solution)/shard_map/ppermute | solution.py:20
  55.7 0.0 collective-permute-start.15
  55.7 1.8 %collective-permute-done.10.refs_1_.refs_2_ = bf16[2,256,128]{2,1,0:T(8,128)(2,1)S(1)} collective-permute-done((bf16[2,256,128]{2,1,0:T(8,128)(2,1)S(1)}, bf16[2,256,128]{2,1,0:T(8,128)(2,1)S(1)}, u32[]{:S(2)}, u32[]{:S(2)}) %collective-permute-start.10) | collective-permute-done | bytes 131104 | tf_op jit(solution)/shard_map/ppermute | solution.py:20
  57.5 0.0 collective-permute-start.14
  57.5 0.0 collective-permute-done.20.far_r
  57.5 0.1 collective-permute-done.9.refs_0_.refs_1_
  57.6 1.3 %chain.3 = (bf16[2,256,128]{2,1,0:T(8,128)(2,1)S(1)}, bf16[512,128]{1,0:T(8,128)(2,1)}) custom-call(s32[1]{0:T(128)} %bitcast.8.side_ref, bf16[4,256,512]{2,1,0:T(8,128)(2,1)S(1)} %copy-done.2, bf16[4,256,2048]{2,1,0:T(8,128)(2,1)S(1)} %copy-done.1, bf16[10,256,256]{2,1,0:T(8,128)(2,1)S(1)} %unpack.1.far_w, f32[2,256,128]{2,1,0:T(8,128)S(1)} %get-tuple-element.48.own_r, ...), custom_call_target="tpu_custom_call" | custom-call | tf_op jit(solution)/shard_map/chain/pallas_call | solution.py:229
  58.9 2.7 %collective-permute-start.23 = (bf16[2,256,128]{2,1,0:T(8,128)(2,1)S(1)}, bf16[2,256,128]{2,1,0:T(8,128)(2,1)S(1)}, u32[]{:S(2)}, u32[]{:S(2)}) collective-permute-start(bf16[2,256,128]{2,1,0:T(8,128)(2,1)S(1)} %get-tuple-element.46.refs_8_), channel_id=1, source_target_pairs={{0,12},{2,14},{4,8},{6,10},{8,4},{10,6},{12,0},{14,2},{16,28},{18,... | collective-permute-start | bytes 393224 | tf_op jit(solution)/shard_map/ppermute | solution.py:20
  61.5 0.1 collective-permute-start.22
  61.7 0.0 collective-permute-done.12.refs_4_
  61.7 0.7 collective-permute-start.21
  62.4 0.0 collective-permute-start.24
  62.4 0.5 collective-permute-start.13
  62.9 3.2 %collective-permute-done.23.refs_11_ = bf16[2,256,128]{2,1,0:T(8,128)(2,1)S(1)} collective-permute-done((bf16[2,256,128]{2,1,0:T(8,128)(2,1)S(1)}, bf16[2,256,128]{2,1,0:T(8,128)(2,1)S(1)}, u32[]{:S(2)}, u32[]{:S(2)}) %collective-permute-start.23) | collective-permute-done | bytes 131104 | tf_op jit(solution)/shard_map/ppermute | solution.py:20
  66.1 1.3 %collective-permute-done.22.refs_10_ = bf16[2,256,128]{2,1,0:T(8,128)(2,1)S(1)} collective-permute-done((bf16[2,256,128]{2,1,0:T(8,128)(2,1)S(1)}, bf16[2,256,128]{2,1,0:T(8,128)(2,1)S(1)}, u32[]{:S(2)}, u32[]{:S(2)}) %collective-permute-start.22) | collective-permute-done | bytes 131104 | tf_op jit(solution)/shard_map/ppermute | solution.py:20
  67.4 1.0 %collective-permute-done.21.refs_9_ = bf16[2,256,128]{2,1,0:T(8,128)(2,1)S(1)} collective-permute-done((bf16[2,256,128]{2,1,0:T(8,128)(2,1)S(1)}, bf16[2,256,128]{2,1,0:T(8,128)(2,1)S(1)}, u32[]{:S(2)}, u32[]{:S(2)}) %collective-permute-start.21) | collective-permute-done | bytes 131104 | tf_op jit(solution)/shard_map/ppermute | solution.py:20
  68.4 0.0 collective-permute-start.25
  68.4 0.1 stack.50.at_ref
  68.5 0.2 collective-permute-done.26.refs_14_
  68.8 1.0 %collective-permute-done.25.refs_13_ = bf16[2,256,128]{2,1,0:T(8,128)(2,1)S(1)} collective-permute-done((bf16[2,256,128]{2,1,0:T(8,128)(2,1)S(1)}, bf16[2,256,128]{2,1,0:T(8,128)(2,1)S(1)}, u32[]{:S(2)}, u32[]{:S(2)}) %collective-permute-start.25) | collective-permute-done | bytes 131104 | tf_op jit(solution)/shard_map/ppermute | solution.py:20
  69.7 2.0 %put.1 = bf16[4,256,1024]{2,1,0:T(8,128)(2,1)} custom-call(s32[8]{0:T(128)S(1)} %stack.50.at_ref, bf16[2,256,128]{2,1,0:T(8,128)(2,1)S(1)} %get-tuple-element.40.refs_0_, bf16[2,256,128]{2,1,0:T(8,128)(2,1)S(1)} %collective-permute-done.9.refs_0_.refs_1_, bf16[2,256,128]{2,1,0:T(8,128)(2,1)S(1)} %collective-permute-done.10.refs_1_.refs_2_, ...), custom_call_target="tpu_custom_call" | custom-call | tf_op jit(solution)/shard_map/put/pallas_call | solution.py:294
  (21 shorter events, 0.1 us)
Async XLA Ops:
  9.0 2.1 %collective-permute-start.1 = (bf16[512,512]{1,0:T(8,128)(2,1)S(1)}, bf16[512,512]{1,0:T(8,128)(2,1)S(1)}, u32[]{:S(2)}, u32[]{:S(2)}) collective-permute-start(bf16[512,512]{1,0:T(8,128)(2,1)S(1)} %get-tuple-element.26.after), channel_id=1, source_target_pairs={{0,2},{2,0},{4,6},{6,4},{8,10},{10,8},{12,14},{14,12},{16,18},{18,... | collective-permute-start | bytes 1572872 | tf_op jit(solution)/shard_map/ppermute | solution.py:20
  11.8 16.7 %collective-permute-start.3 = (bf16[512,128]{1,0:T(8,128)(2,1)S(1)}, bf16[512,128]{1,0:T(8,128)(2,1)S(1)}, u32[]{:S(2)}, u32[]{:S(2)}) collective-permute-start(bf16[512,128]{1,0:T(8,128)(2,1)S(1)} %get-tuple-element.31), channel_id=1, source_target_pairs={{0,8},{2,10},{4,12},{6,14},{8,0},{10,2},{12,4},{14,6},{16,24},{18,... | collective-permute-start | bytes 393224 | tf_op jit(solution)/shard_map/ppermute | solution.py:20
  14.8 13.7 %collective-permute-start.4 = (bf16[512,128]{1,0:T(8,128)(2,1)S(1)}, bf16[512,128]{1,0:T(8,128)(2,1)S(1)}, u32[]{:S(2)}, u32[]{:S(2)}) collective-permute-start(bf16[512,128]{1,0:T(8,128)(2,1)S(1)} %get-tuple-element.32), channel_id=1, source_target_pairs={{0,12},{2,14},{4,8},{6,10},{8,4},{10,6},{12,0},{14,2},{16,28},{18,... | collective-permute-start | bytes 393224 | tf_op jit(solution)/shard_map/ppermute | solution.py:20
  16.2 12.3 %collective-permute-start.2 = (bf16[512,128]{1,0:T(8,128)(2,1)S(1)}, bf16[512,128]{1,0:T(8,128)(2,1)S(1)}, u32[]{:S(2)}, u32[]{:S(2)}) collective-permute-start(bf16[512,128]{1,0:T(8,128)(2,1)S(1)} %get-tuple-element.28.refs_0_), channel_id=1, source_target_pairs={{0,4},{2,6},{4,0},{6,2},{8,12},{10,14},{12,8},{14,10},{16,20},{18,... | collective-permute-start | bytes 393224 | tf_op jit(solution)/shard_map/ppermute | solution.py:20
  17.6 18.1 %collective-permute-start = (bf16[5,256,256]{2,1,0:T(8,128)(2,1)S(1)}, bf16[5,256,256]{2,1,0:T(8,128)(2,1)S(1)}, u32[]{:S(2)}, u32[]{:S(2)}) collective-permute-start(bf16[5,256,256]{2,1,0:T(8,128)(2,1)S(1)} %pack.1.refs_1_), channel_id=1, source_target_pairs={{0,1},{1,0},{2,3},{3,2},{4,5},{5,4},{6,7},{7,6},{8,9},{9,8},{10,11... | collective-permute-start | bytes 1966088 | tf_op jit(solution)/shard_map/ppermute | solution.py:388
  28.6 2.8 %collective-permute-start.5 = (bf16[512,512]{1,0:T(8,128)(2,1)S(1)}, bf16[512,512]{1,0:T(8,128)(2,1)S(1)}, u32[]{:S(2)}, u32[]{:S(2)}) collective-permute-start(bf16[512,512]{1,0:T(8,128)(2,1)S(1)} %get-tuple-element.33), channel_id=1, source_target_pairs={{0,2},{2,0},{4,6},{6,4},{8,10},{10,8},{12,14},{14,12},{16,18},{18,... | collective-permute-start | bytes 1572872 | tf_op jit(solution)/shard_map/ppermute | solution.py:20
  28.7 9.8 %collective-permute-start.7 = (bf16[512,128]{1,0:T(8,128)(2,1)S(1)}, bf16[512,128]{1,0:T(8,128)(2,1)S(1)}, u32[]{:S(2)}, u32[]{:S(2)}) collective-permute-start(bf16[512,128]{1,0:T(8,128)(2,1)S(1)} %add_convert_fusion.1), channel_id=1, source_target_pairs={{0,16},{2,18},{4,20},{6,22},{8,24},{10,26},{12,28},{14,30},{16,0},... | collective-permute-start | bytes 393224 | tf_op jit(solution)/shard_map/ppermute | solution.py:20
  32.1 11.1 %collective-permute-start.17 = (bf16[512,128]{1,0:T(8,128)(2,1)S(1)}, bf16[512,128]{1,0:T(8,128)(2,1)S(1)}, u32[]{:S(2)}, u32[]{:S(2)}) collective-permute-start(bf16[512,128]{1,0:T(8,128)(2,1)S(1)} %get-tuple-element.44), channel_id=1, source_target_pairs={{0,8},{2,10},{4,12},{6,14},{8,0},{10,2},{12,4},{14,6},{16,24},{18,... | collective-permute-start | bytes 393224 | tf_op jit(solution)/shard_map/ppermute | solution.py:20
  33.7 9.5 %collective-permute-start.18 = (bf16[512,128]{1,0:T(8,128)(2,1)S(1)}, bf16[512,128]{1,0:T(8,128)(2,1)S(1)}, u32[]{:S(2)}, u32[]{:S(2)}) collective-permute-start(bf16[512,128]{1,0:T(8,128)(2,1)S(1)} %get-tuple-element.45), channel_id=1, source_target_pairs={{0,12},{2,14},{4,8},{6,10},{8,4},{10,6},{12,0},{14,2},{16,28},{18,... | collective-permute-start | bytes 393224 | tf_op jit(solution)/shard_map/ppermute | solution.py:20
  35.1 8.1 %collective-permute-start.16 = (bf16[512,128]{1,0:T(8,128)(2,1)S(1)}, bf16[512,128]{1,0:T(8,128)(2,1)S(1)}, u32[]{:S(2)}, u32[]{:S(2)}) collective-permute-start(bf16[512,128]{1,0:T(8,128)(2,1)S(1)} %get-tuple-element.34.refs_1_.after), channel_id=1, source_target_pairs={{0,4},{2,6},{4,0},{6,2},{8,12},{10,14},{12,8},{14,10},{16,20},{18,... | collective-permute-start | bytes 393224 | tf_op jit(solution)/shard_map/ppermute | solution.py:20
  35.6 9.2 %collective-permute-start.6 = (bf16[5,256,256]{2,1,0:T(8,128)(2,1)S(1)}, bf16[5,256,256]{2,1,0:T(8,128)(2,1)S(1)}, u32[]{:S(2)}, u32[]{:S(2)}) collective-permute-start(bf16[5,256,256]{2,1,0:T(8,128)(2,1)S(1)} %anchor.4.here), channel_id=1, source_target_pairs={{0,2},{2,0},{4,6},{6,4},{8,10},{10,8},{12,14},{14,12},{16,18},{18,... | collective-permute-start | bytes 1966088 | tf_op jit(solution)/shard_map/ppermute | solution.py:20
  35.6 9.6 %copy-start.2 = (bf16[4,256,512]{2,1,0:T(8,128)(2,1)S(1)}, bf16[4,256,512]{2,1,0:T(8,128)(2,1)}, u32[]{:S(2)}) copy-start(bf16[4,256,512]{2,1,0:T(8,128)(2,1)} %inverses.5) | copy-start | bytes 3145732
  38.6 6.7 %collective-permute-start.8 = (bf16[2,256,128]{2,1,0:T(8,128)(2,1)S(1)}, bf16[2,256,128]{2,1,0:T(8,128)(2,1)S(1)}, u32[]{:S(2)}, u32[]{:S(2)}) collective-permute-start(bf16[2,256,128]{2,1,0:T(8,128)(2,1)S(1)} %get-tuple-element.49), channel_id=1, source_target_pairs={{0,1},{1,0},{2,3},{3,2},{4,5},{5,4},{6,7},{7,6},{8,9},{9,8},{10,11... | collective-permute-start | bytes 393224 | tf_op jit(solution)/shard_map/ppermute | solution.py:400
  43.3 8.7 %collective-permute-start.19 = (bf16[512,128]{1,0:T(8,128)(2,1)S(1)}, bf16[512,128]{1,0:T(8,128)(2,1)S(1)}, u32[]{:S(2)}, u32[]{:S(2)}) collective-permute-start(bf16[512,128]{1,0:T(8,128)(2,1)S(1)} %add_convert_fusion), channel_id=1, source_target_pairs={{0,16},{2,18},{4,20},{6,22},{8,24},{10,26},{12,28},{14,30},{16,0},... | collective-permute-start | bytes 393224 | tf_op jit(solution)/shard_map/ppermute | solution.py:20
  45.2 2.2 %copy-start = (bf16[4,256,2048]{2,1,0:T(8,128)(2,1)S(1)}, bf16[4,256,2048]{2,1,0:T(8,128)(2,1)}, u32[]{:S(2)}) copy-start(bf16[4,256,2048]{2,1,0:T(8,128)(2,1)} %window.7) | copy-start | bytes 12582916
  47.4 3.9 %copy-start.1 = (bf16[4,256,2048]{2,1,0:T(8,128)(2,1)S(1)}, bf16[4,256,2048]{2,1,0:T(8,128)(2,1)}, u32[]{:S(2)}) copy-start(bf16[4,256,2048]{2,1,0:T(8,128)(2,1)} %window.7) | copy-start | bytes 12582916
  48.3 7.4 %collective-permute-start.11 = (bf16[2,256,128]{2,1,0:T(8,128)(2,1)S(1)}, bf16[2,256,128]{2,1,0:T(8,128)(2,1)S(1)}, u32[]{:S(2)}, u32[]{:S(2)}) collective-permute-start(bf16[2,256,128]{2,1,0:T(8,128)(2,1)S(1)} %get-tuple-element.40.refs_0_), channel_id=1, source_target_pairs={{0,12},{2,14},{4,8},{6,10},{8,4},{10,6},{12,0},{14,2},{16,28},{18,... | collective-permute-start | bytes 393224 | tf_op jit(solution)/shard_map/ppermute | solution.py:20
  51.2 6.3 %collective-permute-start.10 = (bf16[2,256,128]{2,1,0:T(8,128)(2,1)S(1)}, bf16[2,256,128]{2,1,0:T(8,128)(2,1)S(1)}, u32[]{:S(2)}, u32[]{:S(2)}) collective-permute-start(bf16[2,256,128]{2,1,0:T(8,128)(2,1)S(1)} %get-tuple-element.40.refs_0_), channel_id=1, source_target_pairs={{0,8},{2,10},{4,12},{6,14},{8,0},{10,2},{12,4},{14,6},{16,24},{18,... | collective-permute-start | bytes 393224 | tf_op jit(solution)/shard_map/ppermute | solution.py:20
  52.0 5.4 %collective-permute-start.20 = (bf16[2,256,128]{2,1,0:T(8,128)(2,1)S(1)}, bf16[2,256,128]{2,1,0:T(8,128)(2,1)S(1)}, u32[]{:S(2)}, u32[]{:S(2)}) collective-permute-start(bf16[2,256,128]{2,1,0:T(8,128)(2,1)S(1)} %get-tuple-element.47), channel_id=1, source_target_pairs={{0,1},{1,0},{2,3},{3,2},{4,5},{5,4},{6,7},{7,6},{8,9},{9,8},{10,11... | collective-permute-start | bytes 393224 | tf_op jit(solution)/shard_map/ppermute | solution.py:407
  52.6 5.0 %collective-permute-start.9 = (bf16[2,256,128]{2,1,0:T(8,128)(2,1)S(1)}, bf16[2,256,128]{2,1,0:T(8,128)(2,1)S(1)}, u32[]{:S(2)}, u32[]{:S(2)}) collective-permute-start(bf16[2,256,128]{2,1,0:T(8,128)(2,1)S(1)} %get-tuple-element.40.refs_0_), channel_id=1, source_target_pairs={{0,4},{2,6},{4,0},{6,2},{8,12},{10,14},{12,8},{14,10},{16,20},{18,... | collective-permute-start | bytes 393224 | tf_op jit(solution)/shard_map/ppermute | solution.py:20
  53.8 7.8 %collective-permute-start.12 = (bf16[2,256,128]{2,1,0:T(8,128)(2,1)S(1)}, bf16[2,256,128]{2,1,0:T(8,128)(2,1)S(1)}, u32[]{:S(2)}, u32[]{:S(2)}) collective-permute-start(bf16[2,256,128]{2,1,0:T(8,128)(2,1)S(1)} %get-tuple-element.40.refs_0_), channel_id=1, source_target_pairs={{0,2},{2,0},{4,6},{6,4},{8,10},{10,8},{12,14},{14,12},{16,18},{18,... | collective-permute-start | bytes 393224 | tf_op jit(solution)/shard_map/ppermute | solution.py:20
  55.7 6.6 %collective-permute-start.15 = (bf16[2,256,128]{2,1,0:T(8,128)(2,1)S(1)}, bf16[2,256,128]{2,1,0:T(8,128)(2,1)S(1)}, u32[]{:S(2)}, u32[]{:S(2)}) collective-permute-start(bf16[2,256,128]{2,1,0:T(8,128)(2,1)S(1)} %collective-permute-done.11.refs_2_.refs_3_), channel_id=1, source_target_pairs={{0,2},{2,0},{4,6},{6,4},{8,10},{10,8},{12,14},{14,12},{16,18},{18,... | collective-permute-start | bytes 393224 | tf_op jit(solution)/shard_map/ppermute | solution.py:20
  57.5 4.9 %collective-permute-start.14 = (bf16[2,256,128]{2,1,0:T(8,128)(2,1)S(1)}, bf16[2,256,128]{2,1,0:T(8,128)(2,1)S(1)}, u32[]{:S(2)}, u32[]{:S(2)}) collective-permute-start(bf16[2,256,128]{2,1,0:T(8,128)(2,1)S(1)} %collective-permute-done.10.refs_1_.refs_2_), channel_id=1, source_target_pairs={{0,2},{2,0},{4,6},{6,4},{8,10},{10,8},{12,14},{14,12},{16,18},{18,... | collective-permute-start | bytes 393224 | tf_op jit(solution)/shard_map/ppermute | solution.py:20
  58.9 7.2 %collective-permute-start.23 = (bf16[2,256,128]{2,1,0:T(8,128)(2,1)S(1)}, bf16[2,256,128]{2,1,0:T(8,128)(2,1)S(1)}, u32[]{:S(2)}, u32[]{:S(2)}) collective-permute-start(bf16[2,256,128]{2,1,0:T(8,128)(2,1)S(1)} %get-tuple-element.46.refs_8_), channel_id=1, source_target_pairs={{0,12},{2,14},{4,8},{6,10},{8,4},{10,6},{12,0},{14,2},{16,28},{18,... | collective-permute-start | bytes 393224 | tf_op jit(solution)/shard_map/ppermute | solution.py:20
  61.5 5.9 %collective-permute-start.22 = (bf16[2,256,128]{2,1,0:T(8,128)(2,1)S(1)}, bf16[2,256,128]{2,1,0:T(8,128)(2,1)S(1)}, u32[]{:S(2)}, u32[]{:S(2)}) collective-permute-start(bf16[2,256,128]{2,1,0:T(8,128)(2,1)S(1)} %get-tuple-element.46.refs_8_), channel_id=1, source_target_pairs={{0,8},{2,10},{4,12},{6,14},{8,0},{10,2},{12,4},{14,6},{16,24},{18,... | collective-permute-start | bytes 393224 | tf_op jit(solution)/shard_map/ppermute | solution.py:20
  61.7 6.7 %collective-permute-start.21 = (bf16[2,256,128]{2,1,0:T(8,128)(2,1)S(1)}, bf16[2,256,128]{2,1,0:T(8,128)(2,1)S(1)}, u32[]{:S(2)}, u32[]{:S(2)}) collective-permute-start(bf16[2,256,128]{2,1,0:T(8,128)(2,1)S(1)} %get-tuple-element.46.refs_8_), channel_id=1, source_target_pairs={{0,4},{2,6},{4,0},{6,2},{8,12},{10,14},{12,8},{14,10},{16,20},{18,... | collective-permute-start | bytes 393224 | tf_op jit(solution)/shard_map/ppermute | solution.py:20
  62.4 6.1 %collective-permute-start.24 = (bf16[2,256,128]{2,1,0:T(8,128)(2,1)S(1)}, bf16[2,256,128]{2,1,0:T(8,128)(2,1)S(1)}, u32[]{:S(2)}, u32[]{:S(2)}) collective-permute-start(bf16[2,256,128]{2,1,0:T(8,128)(2,1)S(1)} %get-tuple-element.46.refs_8_), channel_id=1, source_target_pairs={{0,2},{2,0},{4,6},{6,4},{8,10},{10,8},{12,14},{14,12},{16,18},{18,... | collective-permute-start | bytes 393224 | tf_op jit(solution)/shard_map/ppermute | solution.py:20
  62.4 6.1 %collective-permute-start.13 = (bf16[2,256,128]{2,1,0:T(8,128)(2,1)S(1)}, bf16[2,256,128]{2,1,0:T(8,128)(2,1)S(1)}, u32[]{:S(2)}, u32[]{:S(2)}) collective-permute-start(bf16[2,256,128]{2,1,0:T(8,128)(2,1)S(1)} %collective-permute-done.9.refs_0_.refs_1_), channel_id=1, source_target_pairs={{0,2},{2,0},{4,6},{6,4},{8,10},{10,8},{12,14},{14,12},{16,18},{18,... | collective-permute-start | bytes 393224 | tf_op jit(solution)/shard_map/ppermute | solution.py:20
  66.1 2.4 %collective-permute-start.27 = (bf16[2,256,128]{2,1,0:T(8,128)(2,1)S(1)}, bf16[2,256,128]{2,1,0:T(8,128)(2,1)S(1)}, u32[]{:S(2)}, u32[]{:S(2)}) collective-permute-start(bf16[2,256,128]{2,1,0:T(8,128)(2,1)S(1)} %collective-permute-done.23.refs_11_), channel_id=1, source_target_pairs={{0,2},{2,0},{4,6},{6,4},{8,10},{10,8},{12,14},{14,12},{16,18},{18,... | collective-permute-start | bytes 393224 | tf_op jit(solution)/shard_map/ppermute | solution.py:20
  67.4 1.3 %collective-permute-start.26 = (bf16[2,256,128]{2,1,0:T(8,128)(2,1)S(1)}, bf16[2,256,128]{2,1,0:T(8,128)(2,1)S(1)}, u32[]{:S(2)}, u32[]{:S(2)}) collective-permute-start(bf16[2,256,128]{2,1,0:T(8,128)(2,1)S(1)} %collective-permute-done.22.refs_10_), channel_id=1, source_target_pairs={{0,2},{2,0},{4,6},{6,4},{8,10},{10,8},{12,14},{14,12},{16,18},{18,... | collective-permute-start | bytes 393224 | tf_op jit(solution)/shard_map/ppermute | solution.py:20
  68.4 1.3 %collective-permute-start.25 = (bf16[2,256,128]{2,1,0:T(8,128)(2,1)S(1)}, bf16[2,256,128]{2,1,0:T(8,128)(2,1)S(1)}, u32[]{:S(2)}, u32[]{:S(2)}) collective-permute-start(bf16[2,256,128]{2,1,0:T(8,128)(2,1)S(1)} %collective-permute-done.21.refs_9_), channel_id=1, source_target_pairs={{0,2},{2,0},{4,6},{6,4},{8,10},{10,8},{12,14},{14,12},{16,18},{18,... | collective-permute-start | bytes 393224 | tf_op jit(solution)/shard_map/ppermute | solution.py:20

commit v4 on v3

--- a/solution.py
+++ b/solution.py
@@ -77,8 +77,8 @@
     count = len(steps)
     pieces = next(p for p in (6, 8, 4, 3, 2, 1) if depth % (p * LANES) == 0)
     cuts = (depth // pieces,) * pieces
-    if cuts[-1] % (2 * LANES) == 0:
-        cuts = cuts[:-1] + (cuts[-1] // 2,) * 2
+    if cuts[0] % (2 * LANES) == 0:
+        cuts = (cuts[0] // 2,) * 2 + cuts[1:]
     rows = count * half
     return pl.pallas_call(
         functools.partial(gemm_kernel, steps[0], cuts),
@@ -101,23 +101,24 @@
     )(flag, in_hbm(panel), in_hbm(solved), *after)
 
 
-def split_kernel(at_ref, keep, got, *pieces):
+def split_kernel(count, at_ref, keep, got, *refs):
+    pieces = refs[-count:]
     width = pieces[0].shape[1]
     for index, piece in enumerate(pieces):
         span = pl.ds(pl.multiple_of(at_ref[index] * width, width), width)
         piece[...] = (keep[:, span].astype(F32) + got[:, span].astype(F32)).astype(piece.dtype)
 
 
-def split(at, keep, got, count):
+def split(at, keep, got, count, after):
     rows, cols = keep.shape
     return pl.pallas_call(
-        split_kernel,
-        in_specs=[SMEM, VMEM, VMEM],
+        functools.partial(split_kernel, count),
+        in_specs=[SMEM, VMEM, VMEM] + [ANY] * len(after),
         out_specs=[VMEM] * count,
         out_shape=[jax.ShapeDtypeStruct((rows, cols // count), BF if i else F32) for i in range(count)],
         compiler_params=params(16),
         name="split",
-    )(at, keep, got)
+    )(at, keep, got, *after)
 
 
 def far_units(groups):
@@ -191,19 +192,32 @@
     )(flag, here, there)
 
 
-def chain_kernel(units, steps, last, side_ref, inverses, window, far_w, own_r, far_r, *refs):
-    own_out, solved, right = refs[-3:]
+def chain_kernel(units, steps, last, waits, side_ref, inverses, far_w, own_r, far_r, *refs):
     _, half, block = inverses.shape
-    start = steps[0]
+    start, count = steps[0], len(steps)
+    if waits:
+        inner = refs[0]
+        own_out, right, solved = refs[-3:]
+    else:
+        window, later = refs[:2]
+        own_out, later_out, right, solved, inner, outer, sems = refs[-7:]
+        tiles = window.at[start + 1 : start + count, :, start * block : (start + count - 1) * block]
+        fetch_inner = pltpu.make_async_copy(tiles, inner, sems.at[0])
+        tiles = window.at[start + count :, :, start * block : (start + count) * block]
+        fetch_outer = pltpu.make_async_copy(tiles, outer, sems.at[1])
+        fetch_inner.start()
+        fetch_outer.start()
     side = side_ref[0]
     near_at = pl.multiple_of(side * half, half)
     far_at = pl.multiple_of((1 - side) * half, half)
     for place, step in enumerate(steps):
         near = own_r[place].astype(F32)
         far = far_r[place].astype(F32)
+        if place == 1 and not waits:
+            fetch_inner.wait()
         if place:
             known = solved[: place * block, :]
-            near = near - jnp.dot(window[step, :, start * block : step * block], known, preferred_element_type=F32)
+            near = near - jnp.dot(inner[place - 1, :, : place * block], known, preferred_element_type=F32)
             for piece in range(2 * place):
                 known = solved[piece * half : (piece + 1) * half, :]
                 tile = far_w[units.index(("window", step, 2 * start + piece))]
@@ -219,42 +233,63 @@
                 far = far + jnp.dot(tile, right[piece * half : (piece + 1) * half, :], preferred_element_type=F32)
             solved[pl.ds(pl.multiple_of(place * block + near_at, half), half), :] = near
             solved[pl.ds(pl.multiple_of(place * block + far_at, half), half), :] = far.astype(BF)
-
-
-def chain(units, steps, side, inverses, window, far_w, own_r, far_r, after):
+    if not waits:
+        fetch_outer.wait()
+        flat = outer[...].reshape(outer.shape[0] * half, count * block)
+        taken = jnp.dot(flat, solved[...], preferred_element_type=F32)
+        later_out[...] = later[...] - taken.reshape(later.shape)
+
+
+def chain(units, steps, side, inverses, far_w, own_r, far_r, tiles, after):
     count, half, cols = own_r.shape
     block = 2 * half
-    last = inverses.shape[0] - 1
-    args = [side, inverses, window, far_w, own_r, far_r]
-    return pl.pallas_call(
-        functools.partial(chain_kernel, units, steps, last),
-        in_specs=[SMEM] + [VMEM] * (len(args) - 1) + [ANY] * len(after),
-        out_specs=[VMEM, VMEM],
-        out_shape=[
-            jax.ShapeDtypeStruct((count, half, cols), BF),
-            jax.ShapeDtypeStruct((min(count, last - steps[0]) * block, cols), BF),
-        ],
-        scratch_shapes=[pltpu.VMEM((block, cols), BF)],
-        compiler_params=params(8),
+    waits = len(tiles) == 1
+    args = [side, inverses, far_w, own_r, far_r]
+    outs = [jax.ShapeDtypeStruct((count, half, cols), BF)]
+    scratch = [pltpu.VMEM((block, cols), BF), pltpu.VMEM((count * block, cols), BF)]
+    if waits:
+        specs = [VMEM]
+    else:
+        window, later = tiles
+        tiles = [in_hbm(window), later]
+        specs = [ANY, VMEM]
+        outs.append(jax.ShapeDtypeStruct(later.shape, F32))
+        scratch += [
+            pltpu.VMEM((count - 1, half, (count - 1) * block), BF),
+            pltpu.VMEM((later.shape[0], half, count * block), BF),
+            pltpu.SemaphoreType.DMA((2,)),
+        ]
+    return pl.pallas_call(
+        functools.partial(chain_kernel, units, steps, inverses.shape[0] - 1, waits),
+        in_specs=[SMEM] + [VMEM] * (len(args) - 1) + specs + [ANY] * len(after),
+        out_specs=[VMEM] * len(outs),
+        out_shape=outs,
+        scratch_shapes=scratch,
+        compiler_params=params(12),
         name="chain",
-    )(*args, *after)
-
-
-def couple_kernel(load, window, known, out):
-    count, half, _ = load.shape
-    flat = window[-count:, :, : known.shape[0]].reshape(count * half, known.shape[0])
-    out[...] = load[...] - jnp.dot(flat, known[...], preferred_element_type=F32).reshape(load.shape)
-
-
-def couple(load, window, known):
-    return pl.pallas_call(
-        couple_kernel,
-        in_specs=[VMEM] * 3,
+    )(*args, *tiles, *after)
+
+
+def fetch_kernel(first, column, window, after, out, sems):
+    del after
+    count, _, cols = out.shape
+    copy = pltpu.make_async_copy(window.at[first : first + count, :, column : column + cols], out, sems.at[0])
+    copy.start()
+    copy.wait()
+
+
+def fetch(window, steps, block, after):
+    count, half = len(steps) - 1, window.shape[1]
+    return pl.pallas_call(
+        functools.partial(fetch_kernel, steps[1], steps[0] * block),
+        in_specs=[ANY, ANY],
         out_specs=VMEM,
-        out_shape=jax.ShapeDtypeStruct(load.shape, F32),
-        compiler_params=params(8),
-        name="couple",
-    )(load, window, known)
+        out_shape=jax.ShapeDtypeStruct((count, half, count * block), BF),
+        scratch_shapes=[pltpu.SemaphoreType.DMA((1,))],
+        compiler_params=params(4),
+        cost_estimate=cost(1, 1 << 22),
+        name="fetch",
+    )(in_hbm(window), after)
 
 
 def anchor_kernel(*refs):
@@ -276,21 +311,20 @@
 
 def put_kernel(firsts, at_ref, *refs):
     out, sems = refs[-2:]
-    pieces = refs[:-2]
-    per = len(pieces) // len(firsts)
     copies = []
-    for index, piece in enumerate(pieces):
+    for index, (first, piece) in enumerate(zip(firsts, refs)):
         count, _, cols = piece.shape
-        first = firsts[index // per]
-        span = pl.ds(pl.multiple_of(at_ref[index % per] * cols, cols), cols)
-        copy = pltpu.make_async_copy(piece, out.at[first : first + count, :, span], sems.at[index])
-        copy.start()
-        copies.append(copy)
+        span = pl.ds(pl.multiple_of(at_ref[index] * cols, cols), cols)
+        copies.append(pltpu.make_async_copy(piece, out.at[first : first + count, :, span], sems.at[index]))
+        copies[-1].start()
     for copy in copies:
         copy.wait()
 
 
-def put(firsts, shape, at, pieces):
+def put(shape, placed):
+    firsts = [first for first, _, _ in placed]
+    at = jnp.stack([column for _, column, _ in placed]).astype(jnp.int32)
+    pieces = [piece for _, _, piece in placed]
     return pl.pallas_call(
         functools.partial(put_kernel, firsts),
         in_specs=[SMEM] + [VMEM] * len(pieces),
@@ -361,8 +395,8 @@
     units = far_units((steps_a, steps_b))
     together = lax.optimization_barrier
 
-    def scatter(send, keep):
-        pieces = split(split_at, keep, swap(send, "blk", size, 1), len(cross))
+    def scatter(send, keep, after):
+        pieces = split(split_at, keep, swap(send, "blk", size, 1), len(cross), after)
         return pieces[0], [swap(piece, "blk", size, mask) for mask, piece in zip(cross[1:], pieces[1:])], pieces[1]
 
     def collect(own, got):
@@ -386,28 +420,31 @@
     send, keep = gemm(core, panel, solved, steps_a, [])
     sent = pack(units, core, inverses, window, send)
     here = lax.ppermute(sent, "rows", pair)
-    own_a, got_a, after = scatter(send, keep)
-    send, keep = gemm(core, panel, solved, steps_b, [after, sent])
+    own_a, got_a, after = scatter(send, keep, [sent])
+    send, keep = gemm(core, panel, solved, steps_b, [after])
     send, got_a = together((send, got_a))
-    own_b, got_b, after = scatter(send, keep)
+    own_b, got_b, after = scatter(send, keep, [])
     load_a, load_b = cut(mine.astype(jnp.int32)[None], loads, cols, (len(steps_a), len(steps_b)), after)
     part_a, half_a = collect(own_a, got_a)
     here = anchor(here, [after])
     half_a = anchor(half_a, [load_a])
-    got_b[-1] = anchor(got_b[-1], [half_a])
+    tiles_b = fetch(window, steps_b, block, load_a)
+    got_b[-1] = anchor(got_b[-1], [half_a, tiles_b])
     part_b, half_b = collect(own_b, got_b)
     left_a = remain(load_a, part_a, half_a)
     far_a = lax.ppermute(left_a.astype(BF), "rows", pair)
     there = swap(here, "blk", size, 1)
     far_w = unpack(core, here, there)
-    answer_a, known = chain(units, steps_a, side, inverses, window, far_w, left_a, far_a, [])
+    answer_a, load_b = chain(units, steps_a, side, inverses, far_w, left_a, far_a, [window, load_b], [])
     got_a = spread(answer_a)
-    load_b = couple(load_b, window, known)
     left_b = remain(load_b, part_b, anchor(half_b, [load_b]))
-    far_b = lax.ppermute(left_b.astype(BF), "rows", pair)
-    answer_b, _ = chain(units, steps_b, side, inverses, window, far_w, left_b, far_b, got_a)
+    rounded = left_b.astype(BF)
+    far_b = lax.ppermute(rounded, "rows", pair)
+    (answer_b,) = chain(units, steps_b, side, inverses, far_w, left_b, far_b, [tiles_b], got_a)
     got_b = spread(answer_b)
-    return put((steps_a[0], steps_b[0]), shape, put_at, forward(answer_a, got_a) + forward(answer_b, got_b))
+    pieces = [(steps_a[0], put_at[i], piece) for i, piece in enumerate(forward(answer_a, got_a))]
+    pieces += [(steps_b[0], put_at[i], piece) for i, piece in enumerate(forward(answer_b, got_b))]
+    return put(shape, pieces)
 
 
 def solution(mesh):

time: 72.1 us -> 69.9 us (0.969)
  local copies, waits for them, and re-layouts: 2.27 us -> 0.1 us
  starting transfers between devices: 24.2 us -> 23.4 us
    unnamed x6 -> x2, local copies, waits for them, and re-layouts: 2.19 us -> 0.01 us
    pallas_call x5, Pallas kernels: 3.95 us -> 5.15 us  [the longest x2 2.82 us: chain(): pl.pallas_call(functools.partial(chain_kernel, units, steps, inverses.sha...]
  transfers between devices with their start and end apart: 28 -> 28, of which waited for: 12 -> 12; matrix products, arithmetic and copies ran while one was open for 1% -> 2% of each run, Pallas kernels for 21% -> 23%
where the time goes in v4:
time: 69.9 us; the launch traced here: 69.7 us
  Pallas kernels  27.4 us (39%)
  starting transfers between devices  23.4 us (33%)
  waiting for transfers between devices  17.3 us (25%)
  other arithmetic  1 us (1%)
    ppermute x25, starting transfers between devices, swap(): return lax.ppermute(value, axis, [(i, i ^ mask) for i in range(size)])  20.4 us
    pallas_call x2, Pallas kernels, gemm(): pl.pallas_call(functools.partial(gemm_kernel, steps[0], cuts), in_specs=[...  17.6 us
    ppermute x25, waiting for transfers between devices, swap(): return lax.ppermute(value, axis, [(i, i ^ mask) for i in range(size)])  17.3 us
    pallas_call x2, Pallas kernels, chain(): pl.pallas_call(functools.partial(chain_kernel, units, steps, inverses.sha...  2.82 us
    pallas_call x1, Pallas kernels, put(): pl.pallas_call(functools.partial(put_kernel, firsts), in_specs=[SMEM] + [...  1.98 us
    ppermute x1, starting transfers between devices, shards(): here = lax.ppermute(sent, 'rows', pair)  1.86 us
  transfers between devices with their start and end apart: 28, of which 12 were waited for; matrix products, arithmetic and copies ran while one was open for 2% of the time, Pallas kernels for 23%

profile of v4, /device:TPU:0, one launch (start us, length us, event | category | flops | bytes accessed | tf_op | source)
XLA Modules:
  0.0 69.7 jit_solution(11968895684313117636)
XLA Ops:
  0.0 8.8 %gemm.2 = (bf16[512,512]{1,0:T(8,128)(2,1)S(1)}, bf16[512,512]{1,0:T(8,128)(2,1)S(1)}) custom-call(s32[1]{0:T(128)} %bitcast.9.flag_ref, bf16[4,256,6144]{2,1,0:T(8,128)(2,1)} %panel.3, bf16[6144,1024]{1,0:T(8,128)(2,1)} %solved.3), custom_call_target="tpu_custom_call" | custom-call | flops 1 | bytes 1 | tf_op jit(solution)/shard_map/gemm/pallas_call | solution.py:83
  8.8 0.5 collective-permute-start.1
  9.3 1.2 %pack.1.refs_0_ = bf16[5,256,256]{2,1,0:T(8,128)(2,1)S(1)} custom-call(s32[1]{0:T(128)} %bitcast.9.flag_ref, bf16[4,256,512]{2,1,0:T(8,128)(2,1)} %inverses.5, bf16[4,256,2048]{2,1,0:T(8,128)(2,1)} %window.3, bf16[512,512]{1,0:T(8,128)(2,1)S(1)} %get-tuple-element.25.after), custom_call_target="tpu_custom_call" | custom-call | flops 1 | bytes 1310720 | tf_op jit(solution)/shard_map/pack/pallas_call | solution.py:156
  10.6 0.1 pad_add_fusion.at_ref
  10.6 0.2 collective-permute-done.1.got
  10.9 0.7 split.2
  11.6 3.0 %collective-permute-start.3 = (bf16[512,128]{1,0:T(8,128)(2,1)S(1)}, bf16[512,128]{1,0:T(8,128)(2,1)S(1)}, u32[]{:S(2)}, u32[]{:S(2)}) collective-permute-start(bf16[512,128]{1,0:T(8,128)(2,1)S(1)} %get-tuple-element.30), channel_id=1, source_target_pairs={{0,8},{2,10},{4,12},{6,14},{8,0},{10,2},{12,4},{14,6},{16,24},{18,... | collective-permute-start | bytes 393224 | tf_op jit(solution)/shard_map/ppermute | solution.py:20
  14.6 1.4 %collective-permute-start.4 = (bf16[512,128]{1,0:T(8,128)(2,1)S(1)}, bf16[512,128]{1,0:T(8,128)(2,1)S(1)}, u32[]{:S(2)}, u32[]{:S(2)}) collective-permute-start(bf16[512,128]{1,0:T(8,128)(2,1)S(1)} %get-tuple-element.31), channel_id=1, source_target_pairs={{0,12},{2,14},{4,8},{6,10},{8,4},{10,6},{12,0},{14,2},{16,28},{18,... | collective-permute-start | bytes 393224 | tf_op jit(solution)/shard_map/ppermute | solution.py:20
  16.0 0.1 collective-permute-start.2
  16.1 1.9 %collective-permute-start = (bf16[5,256,256]{2,1,0:T(8,128)(2,1)S(1)}, bf16[5,256,256]{2,1,0:T(8,128)(2,1)S(1)}, u32[]{:S(2)}, u32[]{:S(2)}) collective-permute-start(bf16[5,256,256]{2,1,0:T(8,128)(2,1)S(1)} %pack.1.refs_0_), channel_id=1, source_target_pairs={{0,1},{1,0},{2,3},{3,2},{4,5},{5,4},{6,7},{7,6},{8,9},{9,8},{10,11... | collective-permute-start | bytes 1966088 | tf_op jit(solution)/shard_map/ppermute | solution.py:422
  18.0 8.8 %gemm.3 = (bf16[512,512]{1,0:T(8,128)(2,1)S(1)}, bf16[512,512]{1,0:T(8,128)(2,1)S(1)}) custom-call(s32[1]{0:T(128)} %bitcast.9.flag_ref, bf16[4,256,6144]{2,1,0:T(8,128)(2,1)} %panel.3, bf16[6144,1024]{1,0:T(8,128)(2,1)} %solved.3, bf16[512,128]{1,0:T(8,128)(2,1)S(1)} %get-tuple-element.27.refs_0_), custom_call_target="tpu_custom_call" | custom-call | flops 1 | bytes 1 | tf_op jit(solution)/shard_map/gemm/pallas_call | solution.py:83
  26.8 0.0 collective-permute-done.3
  26.8 0.0 collective-permute-done.4
  26.8 0.0 collective-permute-done.2
  26.8 0.1 collective-permute-start.5
  26.9 0.1 add_convert_fusion.1
  27.0 2.7 %collective-permute-start.7 = (bf16[512,128]{1,0:T(8,128)(2,1)S(1)}, bf16[512,128]{1,0:T(8,128)(2,1)S(1)}, u32[]{:S(2)}, u32[]{:S(2)}) collective-permute-start(bf16[512,128]{1,0:T(8,128)(2,1)S(1)} %add_convert_fusion.1), channel_id=1, source_target_pairs={{0,16},{2,18},{4,20},{6,22},{8,24},{10,26},{12,28},{14,30},{16,0},... | collective-permute-start | bytes 393224 | tf_op jit(solution)/shard_map/ppermute | solution.py:20
  29.6 0.0 collective-permute-done.5.got
  29.6 0.7 split.3
  30.3 1.6 %collective-permute-start.17 = (bf16[512,128]{1,0:T(8,128)(2,1)S(1)}, bf16[512,128]{1,0:T(8,128)(2,1)S(1)}, u32[]{:S(2)}, u32[]{:S(2)}) collective-permute-start(bf16[512,128]{1,0:T(8,128)(2,1)S(1)} %get-tuple-element.43), channel_id=1, source_target_pairs={{0,8},{2,10},{4,12},{6,14},{8,0},{10,2},{12,4},{14,6},{16,24},{18,... | collective-permute-start | bytes 393224 | tf_op jit(solution)/shard_map/ppermute | solution.py:20
  32.0 1.4 %collective-permute-start.18 = (bf16[512,128]{1,0:T(8,128)(2,1)S(1)}, bf16[512,128]{1,0:T(8,128)(2,1)S(1)}, u32[]{:S(2)}, u32[]{:S(2)}) collective-permute-start(bf16[512,128]{1,0:T(8,128)(2,1)S(1)} %get-tuple-element.44), channel_id=1, source_target_pairs={{0,12},{2,14},{4,8},{6,10},{8,4},{10,6},{12,0},{14,2},{16,28},{18,... | collective-permute-start | bytes 393224 | tf_op jit(solution)/shard_map/ppermute | solution.py:20
  33.4 0.5 collective-permute-start.16
  33.9 1.0 %cut.1 = (f32[2,256,128]{2,1,0:T(8,128)S(1)}, f32[2,256,128]{2,1,0:T(8,128)S(1)}) custom-call(s32[1]{0:T(128)} %bitcast.at_ref, f32[4,256,1024]{2,1,0:T(8,128)} %loads.1, bf16[512,128]{1,0:T(8,128)(2,1)S(1)} %get-tuple-element.33.refs_1_.after), custom_call_target="tpu_custom_call" | custom-call | flops 1 | bytes 8388608 | tf_op jit(solution)/shard_map/cut/pallas_call | solution.py:357
  34.9 1.0 %fetch.1.refs_2_.refs_0_ = bf16[1,256,512]{2,1,0:T(8,128)(2,1)S(1)} custom-call(bf16[4,256,2048]{2,1,0:T(8,128)(2,1)} %window.3, f32[2,256,128]{2,1,0:T(8,128)S(1)} %get-tuple-element.34.refs_1_.after), custom_call_target="tpu_custom_call" | custom-call | flops 1 | bytes 4194304 | tf_op jit(solution)/shard_map/fetch/pallas_call | solution.py:283
  35.9 0.0 copy-start
  35.9 0.1 collective-permute-start.6
  36.0 0.7 %collective-permute-done.7.refs_0_ = bf16[512,128]{1,0:T(8,128)(2,1)S(1)} collective-permute-done((bf16[512,128]{1,0:T(8,128)(2,1)S(1)}, bf16[512,128]{1,0:T(8,128)(2,1)S(1)}, u32[]{:S(2)}, u32[]{:S(2)}) %collective-permute-start.7) | collective-permute-done | bytes 131104 | tf_op jit(solution)/shard_map/ppermute | solution.py:20
  36.8 0.7 %fusion.1 = (bf16[2,256,128]{2,1,0:T(8,128)(2,1)}, f32[2,256,128]{2,1,0:T(8,128)S(1)}) fusion(f32[2,256,128]{2,1,0:T(8,128)S(1)} %get-tuple-element.34.refs_1_.after, f32[2,256,128]{2,1,0:T(8,128)S(1)} %bitcast.17), kind=kLoop, calls=%fused_computation.6 | loop fusion | flops 131072 | bytes 917504 | tf_op jit(solution)/shard_map/convert_element_type | solution.py:435
  37.5 0.5 collective-permute-start.8
  38.0 3.5 %collective-permute-done.18.refs_0_ = bf16[512,128]{1,0:T(8,128)(2,1)S(1)} collective-permute-done((bf16[512,128]{1,0:T(8,128)(2,1)S(1)}, bf16[512,128]{1,0:T(8,128)(2,1)S(1)}, u32[]{:S(2)}, u32[]{:S(2)}) %collective-permute-start.18) | collective-permute-done | bytes 131104 | tf_op jit(solution)/shard_map/ppermute | solution.py:20
  41.5 0.0 collective-permute-done.17
  41.5 0.0 collective-permute-done.16
  41.5 0.1 add_convert_fusion
  41.5 1.5 %collective-permute-start.19 = (bf16[512,128]{1,0:T(8,128)(2,1)S(1)}, bf16[512,128]{1,0:T(8,128)(2,1)S(1)}, u32[]{:S(2)}, u32[]{:S(2)}) collective-permute-start(bf16[512,128]{1,0:T(8,128)(2,1)S(1)} %add_convert_fusion), channel_id=1, source_target_pairs={{0,16},{2,18},{4,20},{6,22},{8,24},{10,26},{12,28},{14,30},{16,0},... | collective-permute-start | bytes 393224 | tf_op jit(solution)/shard_map/ppermute | solution.py:20
  43.1 0.4 unpack.1.far_w
  43.5 0.0 collective-permute-done.8.far_r
  43.5 2.0 %chain.2 = (bf16[2,256,128]{2,1,0:T(8,128)(2,1)S(1)}, f32[2,256,128]{2,1,0:T(8,128)S(1)}) custom-call(s32[1]{0:T(128)} %bitcast.8.side_ref, bf16[4,256,512]{2,1,0:T(8,128)(2,1)S(1)} %copy-done, bf16[10,256,256]{2,1,0:T(8,128)(2,1)S(1)} %unpack.1.far_w, f32[2,256,128]{2,1,0:T(8,128)S(1)} %get-tuple-element.48.own_r, ...), custom_call_target="tpu_custom_call" | custom-call | tf_op jit(solution)/shard_map/chain/pallas_call | solution.py:262
  45.5 2.8 %collective-permute-start.11 = (bf16[2,256,128]{2,1,0:T(8,128)(2,1)S(1)}, bf16[2,256,128]{2,1,0:T(8,128)(2,1)S(1)}, u32[]{:S(2)}, u32[]{:S(2)}) collective-permute-start(bf16[2,256,128]{2,1,0:T(8,128)(2,1)S(1)} %get-tuple-element.40.refs_0_), channel_id=1, source_target_pairs={{0,12},{2,14},{4,8},{6,10},{8,4},{10,6},{12,0},{14,2},{16,28},{18,... | collective-permute-start | bytes 393224 | tf_op jit(solution)/shard_map/ppermute | solution.py:20
  48.4 0.1 collective-permute-start.10
  48.5 1.7 %collective-permute-done.19.refs_0_ = bf16[512,128]{1,0:T(8,128)(2,1)S(1)} collective-permute-done((bf16[512,128]{1,0:T(8,128)(2,1)S(1)}, bf16[512,128]{1,0:T(8,128)(2,1)S(1)}, u32[]{:S(2)}, u32[]{:S(2)}) %collective-permute-start.19) | collective-permute-done | bytes 131104 | tf_op jit(solution)/shard_map/ppermute | solution.py:20
  50.3 0.6 collective-permute-start.20
  50.9 0.5 collective-permute-start.9
  51.4 0.0 collective-permute-start.12
  51.4 1.6 %collective-permute-done.11.refs_3_ = bf16[2,256,128]{2,1,0:T(8,128)(2,1)S(1)} collective-permute-done((bf16[2,256,128]{2,1,0:T(8,128)(2,1)S(1)}, bf16[2,256,128]{2,1,0:T(8,128)(2,1)S(1)}, u32[]{:S(2)}, u32[]{:S(2)}) %collective-permute-start.11) | collective-permute-done | bytes 131104 | tf_op jit(solution)/shard_map/ppermute | solution.py:20
  53.0 2.7 %collective-permute-done.10.refs_2_ = bf16[2,256,128]{2,1,0:T(8,128)(2,1)S(1)} collective-permute-done((bf16[2,256,128]{2,1,0:T(8,128)(2,1)S(1)}, bf16[2,256,128]{2,1,0:T(8,128)(2,1)S(1)}, u32[]{:S(2)}, u32[]{:S(2)}) %collective-permute-start.10) | collective-permute-done | bytes 131104 | tf_op jit(solution)/shard_map/ppermute | solution.py:20
  55.7 0.0 collective-permute-done.20.far_r
  55.7 0.2 collective-permute-done.9.refs_1_
  55.9 0.8 %chain.3.refs_8_ = bf16[2,256,128]{2,1,0:T(8,128)(2,1)S(1)} custom-call(s32[1]{0:T(128)} %bitcast.8.side_ref, bf16[4,256,512]{2,1,0:T(8,128)(2,1)S(1)} %copy-done, bf16[10,256,256]{2,1,0:T(8,128)(2,1)S(1)} %unpack.1.far_w, f32[2,256,128]{2,1,0:T(8,128)S(1)} %get-tuple-element.46.own_r, bf16[2,256,128]{2,1,0:T(8,128)(2,1)S(1)} %collective-permute-done.20.far_r, ...), custom_call_target="tpu_custom_call" | custom-call | tf_op jit(solution)/shard_map/chain/pallas_call | solution.py:262
  56.7 1.2 %collective-permute-start.23 = (bf16[2,256,128]{2,1,0:T(8,128)(2,1)S(1)}, bf16[2,256,128]{2,1,0:T(8,128)(2,1)S(1)}, u32[]{:S(2)}, u32[]{:S(2)}) collective-permute-start(bf16[2,256,128]{2,1,0:T(8,128)(2,1)S(1)} %chain.3.refs_8_), channel_id=1, source_target_pairs={{0,12},{2,14},{4,8},{6,10},{8,4},{10,6},{12,0},{14,2},{16,28},{18,... | collective-permute-start | bytes 393224 | tf_op jit(solution)/shard_map/ppermute | solution.py:20
  57.9 1.5 %collective-permute-start.22 = (bf16[2,256,128]{2,1,0:T(8,128)(2,1)S(1)}, bf16[2,256,128]{2,1,0:T(8,128)(2,1)S(1)}, u32[]{:S(2)}, u32[]{:S(2)}) collective-permute-start(bf16[2,256,128]{2,1,0:T(8,128)(2,1)S(1)} %chain.3.refs_8_), channel_id=1, source_target_pairs={{0,8},{2,10},{4,12},{6,14},{8,0},{10,2},{12,4},{14,6},{16,24},{18,... | collective-permute-start | bytes 393224 | tf_op jit(solution)/shard_map/ppermute | solution.py:20
  59.4 0.8 %collective-permute-start.21 = (bf16[2,256,128]{2,1,0:T(8,128)(2,1)S(1)}, bf16[2,256,128]{2,1,0:T(8,128)(2,1)S(1)}, u32[]{:S(2)}, u32[]{:S(2)}) collective-permute-start(bf16[2,256,128]{2,1,0:T(8,128)(2,1)S(1)} %chain.3.refs_8_), channel_id=1, source_target_pairs={{0,4},{2,6},{4,0},{6,2},{8,12},{10,14},{12,8},{14,10},{16,20},{18,... | collective-permute-start | bytes 393224 | tf_op jit(solution)/shard_map/ppermute | solution.py:20
  60.2 0.5 collective-permute-start.13
  60.7 3.2 %collective-permute-done.23.refs_11_ = bf16[2,256,128]{2,1,0:T(8,128)(2,1)S(1)} collective-permute-done((bf16[2,256,128]{2,1,0:T(8,128)(2,1)S(1)}, bf16[2,256,128]{2,1,0:T(8,128)(2,1)S(1)}, u32[]{:S(2)}, u32[]{:S(2)}) %collective-permute-start.23) | collective-permute-done | bytes 131104 | tf_op jit(solution)/shard_map/ppermute | solution.py:20
  64.0 0.0 collective-permute-start.27
  64.0 1.2 %collective-permute-done.22.refs_10_ = bf16[2,256,128]{2,1,0:T(8,128)(2,1)S(1)} collective-permute-done((bf16[2,256,128]{2,1,0:T(8,128)(2,1)S(1)}, bf16[2,256,128]{2,1,0:T(8,128)(2,1)S(1)}, u32[]{:S(2)}, u32[]{:S(2)}) %collective-permute-start.22) | collective-permute-done | bytes 131104 | tf_op jit(solution)/shard_map/ppermute | solution.py:20
  65.2 0.0 collective-permute-start.26
  65.2 1.0 %collective-permute-done.21.refs_9_ = bf16[2,256,128]{2,1,0:T(8,128)(2,1)S(1)} collective-permute-done((bf16[2,256,128]{2,1,0:T(8,128)(2,1)S(1)}, bf16[2,256,128]{2,1,0:T(8,128)(2,1)S(1)}, u32[]{:S(2)}, u32[]{:S(2)}) %collective-permute-start.21) | collective-permute-done | bytes 131104 | tf_op jit(solution)/shard_map/ppermute | solution.py:20
  66.2 0.0 collective-permute-start.25
  66.2 0.1 stack.50.at_ref
  66.3 0.0 collective-permute-done.13.refs_5_
  66.3 0.0 collective-permute-done.27.refs_15_
  66.3 0.2 collective-permute-done.26.refs_14_
  66.5 1.0 %collective-permute-done.25.refs_13_ = bf16[2,256,128]{2,1,0:T(8,128)(2,1)S(1)} collective-permute-done((bf16[2,256,128]{2,1,0:T(8,128)(2,1)S(1)}, bf16[2,256,128]{2,1,0:T(8,128)(2,1)S(1)}, u32[]{:S(2)}, u32[]{:S(2)}) %collective-permute-start.25) | collective-permute-done | bytes 131104 | tf_op jit(solution)/shard_map/ppermute | solution.py:20
  67.5 2.0 %put.1 = bf16[4,256,1024]{2,1,0:T(8,128)(2,1)} custom-call(s32[16]{0:T(128)S(1)} %stack.50.at_ref, bf16[2,256,128]{2,1,0:T(8,128)(2,1)S(1)} %get-tuple-element.40.refs_0_, bf16[2,256,128]{2,1,0:T(8,128)(2,1)S(1)} %collective-permute-done.9.refs_1_, bf16[2,256,128]{2,1,0:T(8,128)(2,1)S(1)} %collective-permute-done.10.refs_2_, ...), custom_call_target="tpu_custom_call" | custom-call | tf_op jit(solution)/shard_map/put/pallas_call | solution.py:328
  (17 shorter events, 0.1 us)
Async XLA Ops:
  8.8 2.1 %collective-permute-start.1 = (bf16[512,512]{1,0:T(8,128)(2,1)S(1)}, bf16[512,512]{1,0:T(8,128)(2,1)S(1)}, u32[]{:S(2)}, u32[]{:S(2)}) collective-permute-start(bf16[512,512]{1,0:T(8,128)(2,1)S(1)} %get-tuple-element.25.after), channel_id=1, source_target_pairs={{0,2},{2,0},{4,6},{6,4},{8,10},{10,8},{12,14},{14,12},{16,18},{18,... | collective-permute-start | bytes 1572872 | tf_op jit(solution)/shard_map/ppermute | solution.py:20
  11.6 15.2 %collective-permute-start.3 = (bf16[512,128]{1,0:T(8,128)(2,1)S(1)}, bf16[512,128]{1,0:T(8,128)(2,1)S(1)}, u32[]{:S(2)}, u32[]{:S(2)}) collective-permute-start(bf16[512,128]{1,0:T(8,128)(2,1)S(1)} %get-tuple-element.30), channel_id=1, source_target_pairs={{0,8},{2,10},{4,12},{6,14},{8,0},{10,2},{12,4},{14,6},{16,24},{18,... | collective-permute-start | bytes 393224 | tf_op jit(solution)/shard_map/ppermute | solution.py:20
  14.6 12.2 %collective-permute-start.4 = (bf16[512,128]{1,0:T(8,128)(2,1)S(1)}, bf16[512,128]{1,0:T(8,128)(2,1)S(1)}, u32[]{:S(2)}, u32[]{:S(2)}) collective-permute-start(bf16[512,128]{1,0:T(8,128)(2,1)S(1)} %get-tuple-element.31), channel_id=1, source_target_pairs={{0,12},{2,14},{4,8},{6,10},{8,4},{10,6},{12,0},{14,2},{16,28},{18,... | collective-permute-start | bytes 393224 | tf_op jit(solution)/shard_map/ppermute | solution.py:20
  16.0 10.8 %collective-permute-start.2 = (bf16[512,128]{1,0:T(8,128)(2,1)S(1)}, bf16[512,128]{1,0:T(8,128)(2,1)S(1)}, u32[]{:S(2)}, u32[]{:S(2)}) collective-permute-start(bf16[512,128]{1,0:T(8,128)(2,1)S(1)} %get-tuple-element.27.refs_0_), channel_id=1, source_target_pairs={{0,4},{2,6},{4,0},{6,2},{8,12},{10,14},{12,8},{14,10},{16,20},{18,... | collective-permute-start | bytes 393224 | tf_op jit(solution)/shard_map/ppermute | solution.py:20
  16.1 19.8 %collective-permute-start = (bf16[5,256,256]{2,1,0:T(8,128)(2,1)S(1)}, bf16[5,256,256]{2,1,0:T(8,128)(2,1)S(1)}, u32[]{:S(2)}, u32[]{:S(2)}) collective-permute-start(bf16[5,256,256]{2,1,0:T(8,128)(2,1)S(1)} %pack.1.refs_0_), channel_id=1, source_target_pairs={{0,1},{1,0},{2,3},{3,2},{4,5},{5,4},{6,7},{7,6},{8,9},{9,8},{10,11... | collective-permute-start | bytes 1966088 | tf_op jit(solution)/shard_map/ppermute | solution.py:422
  26.8 2.8 %collective-permute-start.5 = (bf16[512,512]{1,0:T(8,128)(2,1)S(1)}, bf16[512,512]{1,0:T(8,128)(2,1)S(1)}, u32[]{:S(2)}, u32[]{:S(2)}) collective-permute-start(bf16[512,512]{1,0:T(8,128)(2,1)S(1)} %get-tuple-element.32), channel_id=1, source_target_pairs={{0,2},{2,0},{4,6},{6,4},{8,10},{10,8},{12,14},{14,12},{16,18},{18,... | collective-permute-start | bytes 1572872 | tf_op jit(solution)/shard_map/ppermute | solution.py:20
  27.0 9.8 %collective-permute-start.7 = (bf16[512,128]{1,0:T(8,128)(2,1)S(1)}, bf16[512,128]{1,0:T(8,128)(2,1)S(1)}, u32[]{:S(2)}, u32[]{:S(2)}) collective-permute-start(bf16[512,128]{1,0:T(8,128)(2,1)S(1)} %add_convert_fusion.1), channel_id=1, source_target_pairs={{0,16},{2,18},{4,20},{6,22},{8,24},{10,26},{12,28},{14,30},{16,0},... | collective-permute-start | bytes 393224 | tf_op jit(solution)/shard_map/ppermute | solution.py:20
  30.3 11.1 %collective-permute-start.17 = (bf16[512,128]{1,0:T(8,128)(2,1)S(1)}, bf16[512,128]{1,0:T(8,128)(2,1)S(1)}, u32[]{:S(2)}, u32[]{:S(2)}) collective-permute-start(bf16[512,128]{1,0:T(8,128)(2,1)S(1)} %get-tuple-element.43), channel_id=1, source_target_pairs={{0,8},{2,10},{4,12},{6,14},{8,0},{10,2},{12,4},{14,6},{16,24},{18,... | collective-permute-start | bytes 393224 | tf_op jit(solution)/shard_map/ppermute | solution.py:20
  32.0 9.5 %collective-permute-start.18 = (bf16[512,128]{1,0:T(8,128)(2,1)S(1)}, bf16[512,128]{1,0:T(8,128)(2,1)S(1)}, u32[]{:S(2)}, u32[]{:S(2)}) collective-permute-start(bf16[512,128]{1,0:T(8,128)(2,1)S(1)} %get-tuple-element.44), channel_id=1, source_target_pairs={{0,12},{2,14},{4,8},{6,10},{8,4},{10,6},{12,0},{14,2},{16,28},{18,... | collective-permute-start | bytes 393224 | tf_op jit(solution)/shard_map/ppermute | solution.py:20
  33.4 8.1 %collective-permute-start.16 = (bf16[512,128]{1,0:T(8,128)(2,1)S(1)}, bf16[512,128]{1,0:T(8,128)(2,1)S(1)}, u32[]{:S(2)}, u32[]{:S(2)}) collective-permute-start(bf16[512,128]{1,0:T(8,128)(2,1)S(1)} %get-tuple-element.33.refs_1_.after), channel_id=1, source_target_pairs={{0,4},{2,6},{4,0},{6,2},{8,12},{10,14},{12,8},{14,10},{16,20},{18,... | collective-permute-start | bytes 393224 | tf_op jit(solution)/shard_map/ppermute | solution.py:20
  35.9 7.6 %copy-start = (bf16[4,256,512]{2,1,0:T(8,128)(2,1)S(1)}, bf16[4,256,512]{2,1,0:T(8,128)(2,1)}, u32[]{:S(2)}) copy-start(bf16[4,256,512]{2,1,0:T(8,128)(2,1)} %inverses.5) | copy-start | bytes 3145732
  35.9 7.1 %collective-permute-start.6 = (bf16[5,256,256]{2,1,0:T(8,128)(2,1)S(1)}, bf16[5,256,256]{2,1,0:T(8,128)(2,1)S(1)}, u32[]{:S(2)}, u32[]{:S(2)}) collective-permute-start(bf16[5,256,256]{2,1,0:T(8,128)(2,1)S(1)} %anchor.4.here), channel_id=1, source_target_pairs={{0,2},{2,0},{4,6},{6,4},{8,10},{10,8},{12,14},{14,12},{16,18},{18,... | collective-permute-start | bytes 1966088 | tf_op jit(solution)/shard_map/ppermute | solution.py:20
  37.5 6.0 %collective-permute-start.8 = (bf16[2,256,128]{2,1,0:T(8,128)(2,1)}, bf16[2,256,128]{2,1,0:T(8,128)(2,1)S(1)}, u32[]{:S(2)}, u32[]{:S(2)}) collective-permute-start(bf16[2,256,128]{2,1,0:T(8,128)(2,1)} %get-tuple-element.47), channel_id=1, source_target_pairs={{0,1},{1,0},{2,3},{3,2},{4,5},{5,4},{6,7},{7,6},{8,9},{9,8},{10,11... | collective-permute-start | bytes 393224 | tf_op jit(solution)/shard_map/ppermute | solution.py:435
  41.5 8.7 %collective-permute-start.19 = (bf16[512,128]{1,0:T(8,128)(2,1)S(1)}, bf16[512,128]{1,0:T(8,128)(2,1)S(1)}, u32[]{:S(2)}, u32[]{:S(2)}) collective-permute-start(bf16[512,128]{1,0:T(8,128)(2,1)S(1)} %add_convert_fusion), channel_id=1, source_target_pairs={{0,16},{2,18},{4,20},{6,22},{8,24},{10,26},{12,28},{14,30},{16,0},... | collective-permute-start | bytes 393224 | tf_op jit(solution)/shard_map/ppermute | solution.py:20
  45.5 7.4 %collective-permute-start.11 = (bf16[2,256,128]{2,1,0:T(8,128)(2,1)S(1)}, bf16[2,256,128]{2,1,0:T(8,128)(2,1)S(1)}, u32[]{:S(2)}, u32[]{:S(2)}) collective-permute-start(bf16[2,256,128]{2,1,0:T(8,128)(2,1)S(1)} %get-tuple-element.40.refs_0_), channel_id=1, source_target_pairs={{0,12},{2,14},{4,8},{6,10},{8,4},{10,6},{12,0},{14,2},{16,28},{18,... | collective-permute-start | bytes 393224 | tf_op jit(solution)/shard_map/ppermute | solution.py:20
  48.4 7.3 %collective-permute-start.10 = (bf16[2,256,128]{2,1,0:T(8,128)(2,1)S(1)}, bf16[2,256,128]{2,1,0:T(8,128)(2,1)S(1)}, u32[]{:S(2)}, u32[]{:S(2)}) collective-permute-start(bf16[2,256,128]{2,1,0:T(8,128)(2,1)S(1)} %get-tuple-element.40.refs_0_), channel_id=1, source_target_pairs={{0,8},{2,10},{4,12},{6,14},{8,0},{10,2},{12,4},{14,6},{16,24},{18,... | collective-permute-start | bytes 393224 | tf_op jit(solution)/shard_map/ppermute | solution.py:20
  50.3 5.4 %collective-permute-start.20 = (bf16[2,256,128]{2,1,0:T(8,128)(2,1)S(1)}, bf16[2,256,128]{2,1,0:T(8,128)(2,1)S(1)}, u32[]{:S(2)}, u32[]{:S(2)}) collective-permute-start(bf16[2,256,128]{2,1,0:T(8,128)(2,1)S(1)} %get-tuple-element.45), channel_id=1, source_target_pairs={{0,1},{1,0},{2,3},{3,2},{4,5},{5,4},{6,7},{7,6},{8,9},{9,8},{10,11... | collective-permute-start | bytes 393224 | tf_op jit(solution)/shard_map/ppermute | solution.py:442
  50.9 5.0 %collective-permute-start.9 = (bf16[2,256,128]{2,1,0:T(8,128)(2,1)S(1)}, bf16[2,256,128]{2,1,0:T(8,128)(2,1)S(1)}, u32[]{:S(2)}, u32[]{:S(2)}) collective-permute-start(bf16[2,256,128]{2,1,0:T(8,128)(2,1)S(1)} %get-tuple-element.40.refs_0_), channel_id=1, source_target_pairs={{0,4},{2,6},{4,0},{6,2},{8,12},{10,14},{12,8},{14,10},{16,20},{18,... | collective-permute-start | bytes 393224 | tf_op jit(solution)/shard_map/ppermute | solution.py:20
  51.4 8.1 %collective-permute-start.12 = (bf16[2,256,128]{2,1,0:T(8,128)(2,1)S(1)}, bf16[2,256,128]{2,1,0:T(8,128)(2,1)S(1)}, u32[]{:S(2)}, u32[]{:S(2)}) collective-permute-start(bf16[2,256,128]{2,1,0:T(8,128)(2,1)S(1)} %get-tuple-element.40.refs_0_), channel_id=1, source_target_pairs={{0,2},{2,0},{4,6},{6,4},{8,10},{10,8},{12,14},{14,12},{16,18},{18,... | collective-permute-start | bytes 393224 | tf_op jit(solution)/shard_map/ppermute | solution.py:20
  53.0 7.3 %collective-permute-start.15 = (bf16[2,256,128]{2,1,0:T(8,128)(2,1)S(1)}, bf16[2,256,128]{2,1,0:T(8,128)(2,1)S(1)}, u32[]{:S(2)}, u32[]{:S(2)}) collective-permute-start(bf16[2,256,128]{2,1,0:T(8,128)(2,1)S(1)} %collective-permute-done.11.refs_3_), channel_id=1, source_target_pairs={{0,2},{2,0},{4,6},{6,4},{8,10},{10,8},{12,14},{14,12},{16,18},{18,... | collective-permute-start | bytes 393224 | tf_op jit(solution)/shard_map/ppermute | solution.py:20
  55.7 4.6 %collective-permute-start.14 = (bf16[2,256,128]{2,1,0:T(8,128)(2,1)S(1)}, bf16[2,256,128]{2,1,0:T(8,128)(2,1)S(1)}, u32[]{:S(2)}, u32[]{:S(2)}) collective-permute-start(bf16[2,256,128]{2,1,0:T(8,128)(2,1)S(1)} %collective-permute-done.10.refs_2_), channel_id=1, source_target_pairs={{0,2},{2,0},{4,6},{6,4},{8,10},{10,8},{12,14},{14,12},{16,18},{18,... | collective-permute-start | bytes 393224 | tf_op jit(solution)/shard_map/ppermute | solution.py:20
  56.7 7.3 %collective-permute-start.23 = (bf16[2,256,128]{2,1,0:T(8,128)(2,1)S(1)}, bf16[2,256,128]{2,1,0:T(8,128)(2,1)S(1)}, u32[]{:S(2)}, u32[]{:S(2)}) collective-permute-start(bf16[2,256,128]{2,1,0:T(8,128)(2,1)S(1)} %chain.3.refs_8_), channel_id=1, source_target_pairs={{0,12},{2,14},{4,8},{6,10},{8,4},{10,6},{12,0},{14,2},{16,28},{18,... | collective-permute-start | bytes 393224 | tf_op jit(solution)/shard_map/ppermute | solution.py:20
  57.9 7.3 %collective-permute-start.22 = (bf16[2,256,128]{2,1,0:T(8,128)(2,1)S(1)}, bf16[2,256,128]{2,1,0:T(8,128)(2,1)S(1)}, u32[]{:S(2)}, u32[]{:S(2)}) collective-permute-start(bf16[2,256,128]{2,1,0:T(8,128)(2,1)S(1)} %chain.3.refs_8_), channel_id=1, source_target_pairs={{0,8},{2,10},{4,12},{6,14},{8,0},{10,2},{12,4},{14,6},{16,24},{18,... | collective-permute-start | bytes 393224 | tf_op jit(solution)/shard_map/ppermute | solution.py:20
  59.4 6.7 %collective-permute-start.21 = (bf16[2,256,128]{2,1,0:T(8,128)(2,1)S(1)}, bf16[2,256,128]{2,1,0:T(8,128)(2,1)S(1)}, u32[]{:S(2)}, u32[]{:S(2)}) collective-permute-start(bf16[2,256,128]{2,1,0:T(8,128)(2,1)S(1)} %chain.3.refs_8_), channel_id=1, source_target_pairs={{0,4},{2,6},{4,0},{6,2},{8,12},{10,14},{12,8},{14,10},{16,20},{18,... | collective-permute-start | bytes 393224 | tf_op jit(solution)/shard_map/ppermute | solution.py:20
  60.2 6.0 %collective-permute-start.24 = (bf16[2,256,128]{2,1,0:T(8,128)(2,1)S(1)}, bf16[2,256,128]{2,1,0:T(8,128)(2,1)S(1)}, u32[]{:S(2)}, u32[]{:S(2)}) collective-permute-start(bf16[2,256,128]{2,1,0:T(8,128)(2,1)S(1)} %chain.3.refs_8_), channel_id=1, source_target_pairs={{0,2},{2,0},{4,6},{6,4},{8,10},{10,8},{12,14},{14,12},{16,18},{18,... | collective-permute-start | bytes 393224 | tf_op jit(solution)/shard_map/ppermute | solution.py:20
  60.2 6.0 %collective-permute-start.13 = (bf16[2,256,128]{2,1,0:T(8,128)(2,1)S(1)}, bf16[2,256,128]{2,1,0:T(8,128)(2,1)S(1)}, u32[]{:S(2)}, u32[]{:S(2)}) collective-permute-start(bf16[2,256,128]{2,1,0:T(8,128)(2,1)S(1)} %collective-permute-done.9.refs_1_), channel_id=1, source_target_pairs={{0,2},{2,0},{4,6},{6,4},{8,10},{10,8},{12,14},{14,12},{16,18},{18,... | collective-permute-start | bytes 393224 | tf_op jit(solution)/shard_map/ppermute | solution.py:20
  64.0 2.3 %collective-permute-start.27 = (bf16[2,256,128]{2,1,0:T(8,128)(2,1)S(1)}, bf16[2,256,128]{2,1,0:T(8,128)(2,1)S(1)}, u32[]{:S(2)}, u32[]{:S(2)}) collective-permute-start(bf16[2,256,128]{2,1,0:T(8,128)(2,1)S(1)} %collective-permute-done.23.refs_11_), channel_id=1, source_target_pairs={{0,2},{2,0},{4,6},{6,4},{8,10},{10,8},{12,14},{14,12},{16,18},{18,... | collective-permute-start | bytes 393224 | tf_op jit(solution)/shard_map/ppermute | solution.py:20
  65.2 1.3 %collective-permute-start.26 = (bf16[2,256,128]{2,1,0:T(8,128)(2,1)S(1)}, bf16[2,256,128]{2,1,0:T(8,128)(2,1)S(1)}, u32[]{:S(2)}, u32[]{:S(2)}) collective-permute-start(bf16[2,256,128]{2,1,0:T(8,128)(2,1)S(1)} %collective-permute-done.22.refs_10_), channel_id=1, source_target_pairs={{0,2},{2,0},{4,6},{6,4},{8,10},{10,8},{12,14},{14,12},{16,18},{18,... | collective-permute-start | bytes 393224 | tf_op jit(solution)/shard_map/ppermute | solution.py:20
  66.2 1.3 %collective-permute-start.25 = (bf16[2,256,128]{2,1,0:T(8,128)(2,1)S(1)}, bf16[2,256,128]{2,1,0:T(8,128)(2,1)S(1)}, u32[]{:S(2)}, u32[]{:S(2)}) collective-permute-start(bf16[2,256,128]{2,1,0:T(8,128)(2,1)S(1)} %collective-permute-done.21.refs_9_), channel_id=1, source_target_pairs={{0,2},{2,0},{4,6},{6,4},{8,10},{10,8},{12,14},{14,12},{16,18},{18,... | collective-permute-start | bytes 393224 | tf_op jit(solution)/shard_map/ppermute | solution.py:20

commit v5 on v4

--- a/solution.py
+++ b/solution.py
@@ -18,10 +18,6 @@
 
 def swap(value, axis, size, mask):
     return lax.ppermute(value, axis, [(i, i ^ mask) for i in range(size)])
-
-
-def pick(flag, when_set, when_clear):
-    return jnp.where(flag, when_set, when_clear)
 
 
 def cost(flops, moved):
@@ -383,7 +379,8 @@
     blocks = 1 << halvings
     mine = sum(flags[bit] << (inner - bit) for bit in range(halvings))
     reverse = [sum(((mask >> bit) & 1) << (inner - bit) for bit in range(halvings)) for mask in range(blocks)]
-    cross = [2 * mask for mask in range(1 << inner)]
+    gray = [2 * (i ^ (i >> 1)) for i in range(1 << inner)]
+    cross = gray[:1] + gray[:0:-1]
     split_at = jnp.stack([(mine ^ reverse[mask]) & ((1 << inner) - 1) for mask in cross]).astype(jnp.int32)
     put_at = jnp.stack([mine ^ reverse[mask] for mask in cross + [mask + 1 for mask in cross]]).astype(jnp.int32)
     core = flags[0].astype(jnp.int32)[None]

time: 69.9 us -> 68.7 us (0.983)
  waiting for transfers between devices: 17.3 us -> 15.1 us
  starting transfers between devices: 23.4 us -> 24.4 us
    ppermute x25, waiting for transfers between devices: 17.3 us -> 13.8 us  [swap(): return lax.ppermute(value, axis, [(i, i ^ mask) for i in range(size)])]
    ppermute x1, waiting for transfers between devices: 0.01 us -> 1.28 us  [shards(): far_b = lax.ppermute(rounded, 'rows', pair)]
    ppermute x25, starting transfers between devices: 20.4 us -> 21.6 us  [swap(): return lax.ppermute(value, axis, [(i, i ^ mask) for i in range(size)])]
  transfers between devices with their start and end apart: 28 -> 28, of which waited for: 12 -> 15; matrix products, arithmetic and copies ran while one was open for 2% -> 2% of each run, Pallas kernels for 23% -> 23%
where the time goes in v5:
time: 68.7 us; the launch traced here: 68.5 us
  Pallas kernels  27.4 us (40%)
  starting transfers between devices  24.4 us (36%)
  waiting for transfers between devices  15.1 us (22%)
  other arithmetic  1 us (1%)
    ppermute x25, starting transfers between devices, swap(): return lax.ppermute(value, axis, [(i, i ^ mask) for i in range(size)])  21.6 us
    pallas_call x2, Pallas kernels, gemm(): pl.pallas_call(functools.partial(gemm_kernel, steps[0], cuts), in_specs=[...  17.6 us
    ppermute x25, waiting for transfers between devices, swap(): return lax.ppermute(value, axis, [(i, i ^ mask) for i in range(size)])  13.8 us
    pallas_call x2, Pallas kernels, chain(): pl.pallas_call(functools.partial(chain_kernel, units, steps, inverses.sha...  2.81 us
    pallas_call x1, Pallas kernels, put(): pl.pallas_call(functools.partial(put_kernel, firsts), in_specs=[SMEM] + [...  1.98 us
    ppermute x1, starting transfers between devices, shards(): here = lax.ppermute(sent, 'rows', pair)  1.8 us
  transfers between devices with their start and end apart: 28, of which 15 were waited for; matrix products, arithmetic and copies ran while one was open for 2% of the time, Pallas kernels for 23%

profile of v5, /device:TPU:0, one launch (start us, length us, event | category | flops | bytes accessed | tf_op | source)
XLA Modules:
  0.0 68.5 jit_solution(13150697592174364204)
XLA Ops:
  0.0 8.8 %gemm.2 = (bf16[512,512]{1,0:T(8,128)(2,1)S(1)}, bf16[512,512]{1,0:T(8,128)(2,1)S(1)}) custom-call(s32[1]{0:T(128)} %bitcast.9.flag_ref, bf16[4,256,6144]{2,1,0:T(8,128)(2,1)} %panel.3, bf16[6144,1024]{1,0:T(8,128)(2,1)} %solved.3), custom_call_target="tpu_custom_call" | custom-call | flops 1 | bytes 1 | tf_op jit(solution)/shard_map/gemm/pallas_call | solution.py:79
  8.8 0.5 collective-permute-start.1
  9.3 1.2 %pack.1.refs_0_ = bf16[5,256,256]{2,1,0:T(8,128)(2,1)S(1)} custom-call(s32[1]{0:T(128)} %bitcast.9.flag_ref, bf16[4,256,512]{2,1,0:T(8,128)(2,1)} %inverses.5, bf16[4,256,2048]{2,1,0:T(8,128)(2,1)} %window.3, bf16[512,512]{1,0:T(8,128)(2,1)S(1)} %get-tuple-element.25.after), custom_call_target="tpu_custom_call" | custom-call | flops 1 | bytes 1310720 | tf_op jit(solution)/shard_map/pack/pallas_call | solution.py:152
  10.6 0.1 pad_add_fusion.at_ref
  10.6 0.2 collective-permute-done.1.got
  10.9 0.7 split.2
  11.6 4.0 %collective-permute-start.3 = (bf16[512,128]{1,0:T(8,128)(2,1)S(1)}, bf16[512,128]{1,0:T(8,128)(2,1)S(1)}, u32[]{:S(2)}, u32[]{:S(2)}) collective-permute-start(bf16[512,128]{1,0:T(8,128)(2,1)S(1)} %get-tuple-element.30), channel_id=1, source_target_pairs={{0,12},{2,14},{4,8},{6,10},{8,4},{10,6},{12,0},{14,2},{16,28},{18,... | collective-permute-start | bytes 393224 | tf_op jit(solution)/shard_map/ppermute | solution.py:20
  15.5 0.5 collective-permute-start.4
  16.0 0.1 collective-permute-start.2
  16.2 1.8 %collective-permute-start = (bf16[5,256,256]{2,1,0:T(8,128)(2,1)S(1)}, bf16[5,256,256]{2,1,0:T(8,128)(2,1)S(1)}, u32[]{:S(2)}, u32[]{:S(2)}) collective-permute-start(bf16[5,256,256]{2,1,0:T(8,128)(2,1)S(1)} %pack.1.refs_0_), channel_id=1, source_target_pairs={{0,1},{1,0},{2,3},{3,2},{4,5},{5,4},{6,7},{7,6},{8,9},{9,8},{10,11... | collective-permute-start | bytes 1966088 | tf_op jit(solution)/shard_map/ppermute | solution.py:419
  18.0 8.8 %gemm.3 = (bf16[512,512]{1,0:T(8,128)(2,1)S(1)}, bf16[512,512]{1,0:T(8,128)(2,1)S(1)}) custom-call(s32[1]{0:T(128)} %bitcast.9.flag_ref, bf16[4,256,6144]{2,1,0:T(8,128)(2,1)} %panel.3, bf16[6144,1024]{1,0:T(8,128)(2,1)} %solved.3, bf16[512,128]{1,0:T(8,128)(2,1)S(1)} %get-tuple-element.27.refs_0_), custom_call_target="tpu_custom_call" | custom-call | flops 1 | bytes 1 | tf_op jit(solution)/shard_map/gemm/pallas_call | solution.py:79
  26.8 0.0 collective-permute-done.3
  26.8 0.0 collective-permute-done.4
  26.8 0.0 collective-permute-done.2
  26.8 0.1 collective-permute-start.5
  26.9 0.1 add_convert_fusion.1
  27.0 2.7 %collective-permute-start.7 = (bf16[512,128]{1,0:T(8,128)(2,1)S(1)}, bf16[512,128]{1,0:T(8,128)(2,1)S(1)}, u32[]{:S(2)}, u32[]{:S(2)}) collective-permute-start(bf16[512,128]{1,0:T(8,128)(2,1)S(1)} %add_convert_fusion.1), channel_id=1, source_target_pairs={{0,16},{2,18},{4,20},{6,22},{8,24},{10,26},{12,28},{14,30},{16,0},... | collective-permute-start | bytes 393224 | tf_op jit(solution)/shard_map/ppermute | solution.py:20
  29.6 0.0 collective-permute-done.5.got
  29.6 0.7 %split.3 = (f32[512,128]{1,0:T(8,128)S(1)}, bf16[512,128]{1,0:T(8,128)(2,1)S(1)}, bf16[512,128]{1,0:T(8,128)(2,1)S(1)}, bf16[512,128]{1,0:T(8,128)(2,1)S(1)}) custom-call(s32[4]{0:T(128)S(1)} %pad_add_fusion.at_ref, bf16[512,512]{1,0:T(8,128)(2,1)S(1)} %get-tuple-element.28.keep, bf16[512,512]{1,0:T(8,128)(2,1)S(1)} %collective-permute-done.5.got), custom_call_target="tpu_custom_call" | custom-call | tf_op jit(solution)/shard_map/split/pallas_call | solution.py:110
  30.3 2.6 %collective-permute-start.17 = (bf16[512,128]{1,0:T(8,128)(2,1)S(1)}, bf16[512,128]{1,0:T(8,128)(2,1)S(1)}, u32[]{:S(2)}, u32[]{:S(2)}) collective-permute-start(bf16[512,128]{1,0:T(8,128)(2,1)S(1)} %get-tuple-element.43), channel_id=1, source_target_pairs={{0,12},{2,14},{4,8},{6,10},{8,4},{10,6},{12,0},{14,2},{16,28},{18,... | collective-permute-start | bytes 393224 | tf_op jit(solution)/shard_map/ppermute | solution.py:20
  32.9 0.5 collective-permute-start.18
  33.4 0.5 collective-permute-start.16
  33.9 1.0 %cut.1 = (f32[2,256,128]{2,1,0:T(8,128)S(1)}, f32[2,256,128]{2,1,0:T(8,128)S(1)}) custom-call(s32[1]{0:T(128)} %bitcast.at_ref, f32[4,256,1024]{2,1,0:T(8,128)} %loads.1, bf16[512,128]{1,0:T(8,128)(2,1)S(1)} %get-tuple-element.33.refs_1_.after), custom_call_target="tpu_custom_call" | custom-call | flops 1 | bytes 8388608 | tf_op jit(solution)/shard_map/cut/pallas_call | solution.py:353
  34.9 1.0 %fetch.1.refs_2_.refs_0_ = bf16[1,256,512]{2,1,0:T(8,128)(2,1)S(1)} custom-call(bf16[4,256,2048]{2,1,0:T(8,128)(2,1)} %window.3, f32[2,256,128]{2,1,0:T(8,128)S(1)} %get-tuple-element.34.refs_1_.after), custom_call_target="tpu_custom_call" | custom-call | flops 1 | bytes 4194304 | tf_op jit(solution)/shard_map/fetch/pallas_call | solution.py:279
  35.9 0.0 copy-start
  35.9 0.0 collective-permute-done.refs_0_
  35.9 0.1 collective-permute-start.6
  36.0 0.7 %collective-permute-done.7.refs_0_ = bf16[512,128]{1,0:T(8,128)(2,1)S(1)} collective-permute-done((bf16[512,128]{1,0:T(8,128)(2,1)S(1)}, bf16[512,128]{1,0:T(8,128)(2,1)S(1)}, u32[]{:S(2)}, u32[]{:S(2)}) %collective-permute-start.7) | collective-permute-done | bytes 131104 | tf_op jit(solution)/shard_map/ppermute | solution.py:20
  36.8 0.7 %fusion.1 = (bf16[2,256,128]{2,1,0:T(8,128)(2,1)}, f32[2,256,128]{2,1,0:T(8,128)S(1)}) fusion(f32[2,256,128]{2,1,0:T(8,128)S(1)} %get-tuple-element.34.refs_1_.after, f32[2,256,128]{2,1,0:T(8,128)S(1)} %bitcast.17), kind=kLoop, calls=%fused_computation.6 | loop fusion | flops 131072 | bytes 917504 | tf_op jit(solution)/shard_map/convert_element_type | solution.py:432
  37.5 0.5 collective-permute-start.8
  38.0 1.7 %collective-permute-done.18.refs_0_ = bf16[512,128]{1,0:T(8,128)(2,1)S(1)} collective-permute-done((bf16[512,128]{1,0:T(8,128)(2,1)S(1)}, bf16[512,128]{1,0:T(8,128)(2,1)S(1)}, u32[]{:S(2)}, u32[]{:S(2)}) %collective-permute-start.18) | collective-permute-done | bytes 131104 | tf_op jit(solution)/shard_map/ppermute | solution.py:20
  39.7 0.0 collective-permute-done.17
  39.7 1.8 %collective-permute-done.16 = bf16[512,128]{1,0:T(8,128)(2,1)S(1)} collective-permute-done((bf16[512,128]{1,0:T(8,128)(2,1)S(1)}, bf16[512,128]{1,0:T(8,128)(2,1)S(1)}, u32[]{:S(2)}, u32[]{:S(2)}) %collective-permute-start.16) | collective-permute-done | bytes 131104 | tf_op jit(solution)/shard_map/ppermute | solution.py:20
  41.5 0.1 add_convert_fusion
  41.6 1.8 %collective-permute-start.19 = (bf16[512,128]{1,0:T(8,128)(2,1)S(1)}, bf16[512,128]{1,0:T(8,128)(2,1)S(1)}, u32[]{:S(2)}, u32[]{:S(2)}) collective-permute-start(bf16[512,128]{1,0:T(8,128)(2,1)S(1)} %add_convert_fusion), channel_id=1, source_target_pairs={{0,16},{2,18},{4,20},{6,22},{8,24},{10,26},{12,28},{14,30},{16,0},... | collective-permute-start | bytes 393224 | tf_op jit(solution)/shard_map/ppermute | solution.py:20
  43.4 0.4 unpack.1.far_w
  43.8 0.0 collective-permute-done.8.far_r
  43.8 2.0 %chain.2 = (bf16[2,256,128]{2,1,0:T(8,128)(2,1)S(1)}, f32[2,256,128]{2,1,0:T(8,128)S(1)}) custom-call(s32[1]{0:T(128)} %bitcast.8.side_ref, bf16[4,256,512]{2,1,0:T(8,128)(2,1)S(1)} %copy-done, bf16[10,256,256]{2,1,0:T(8,128)(2,1)S(1)} %unpack.1.far_w, f32[2,256,128]{2,1,0:T(8,128)S(1)} %get-tuple-element.48.own_r, ...), custom_call_target="tpu_custom_call" | custom-call | tf_op jit(solution)/shard_map/chain/pallas_call | solution.py:258
  45.9 0.6 collective-permute-start.11
  46.5 3.4 %collective-permute-start.10 = (bf16[2,256,128]{2,1,0:T(8,128)(2,1)S(1)}, bf16[2,256,128]{2,1,0:T(8,128)(2,1)S(1)}, u32[]{:S(2)}, u32[]{:S(2)}) collective-permute-start(bf16[2,256,128]{2,1,0:T(8,128)(2,1)S(1)} %get-tuple-element.40.refs_0_), channel_id=1, source_target_pairs={{0,12},{2,14},{4,8},{6,10},{8,4},{10,6},{12,0},{14,2},{16,28},{18,... | collective-permute-start | bytes 393224 | tf_op jit(solution)/shard_map/ppermute | solution.py:20
  49.9 0.4 collective-permute-done.19.refs_0_
  50.3 0.5 collective-permute-start.20
  50.9 2.7 %collective-permute-done.11.refs_3_ = bf16[2,256,128]{2,1,0:T(8,128)(2,1)S(1)} collective-permute-done((bf16[2,256,128]{2,1,0:T(8,128)(2,1)S(1)}, bf16[2,256,128]{2,1,0:T(8,128)(2,1)S(1)}, u32[]{:S(2)}, u32[]{:S(2)}) %collective-permute-start.11) | collective-permute-done | bytes 131104 | tf_op jit(solution)/shard_map/ppermute | solution.py:20
  53.6 0.3 collective-permute-done.10.refs_2_
  53.9 0.2 collective-permute-start.14
  54.1 1.3 %collective-permute-done.20.far_r = bf16[2,256,128]{2,1,0:T(8,128)(2,1)S(1)} collective-permute-done((bf16[2,256,128]{2,1,0:T(8,128)(2,1)S(1)}, bf16[2,256,128]{2,1,0:T(8,128)(2,1)S(1)}, u32[]{:S(2)}, u32[]{:S(2)}) %collective-permute-start.20) | collective-permute-done | bytes 131104 | tf_op jit(solution)/shard_map/ppermute | solution.py:439
  55.4 0.5 collective-permute-done.9.refs_1_
  55.8 0.8 %chain.3.refs_8_ = bf16[2,256,128]{2,1,0:T(8,128)(2,1)S(1)} custom-call(s32[1]{0:T(128)} %bitcast.8.side_ref, bf16[4,256,512]{2,1,0:T(8,128)(2,1)S(1)} %copy-done, bf16[10,256,256]{2,1,0:T(8,128)(2,1)S(1)} %unpack.1.far_w, f32[2,256,128]{2,1,0:T(8,128)S(1)} %get-tuple-element.46.own_r, bf16[2,256,128]{2,1,0:T(8,128)(2,1)S(1)} %collective-permute-done.20.far_r, ...), custom_call_target="tpu_custom_call" | custom-call | tf_op jit(solution)/shard_map/chain/pallas_call | solution.py:258
  56.7 0.5 collective-permute-start.23
  57.2 2.4 %collective-permute-start.22 = (bf16[2,256,128]{2,1,0:T(8,128)(2,1)S(1)}, bf16[2,256,128]{2,1,0:T(8,128)(2,1)S(1)}, u32[]{:S(2)}, u32[]{:S(2)}) collective-permute-start(bf16[2,256,128]{2,1,0:T(8,128)(2,1)S(1)} %chain.3.refs_8_), channel_id=1, source_target_pairs={{0,12},{2,14},{4,8},{6,10},{8,4},{10,6},{12,0},{14,2},{16,28},{18,... | collective-permute-start | bytes 393224 | tf_op jit(solution)/shard_map/ppermute | solution.py:20
  59.6 0.6 collective-permute-start.21
  60.2 0.0 collective-permute-done.15.refs_7_
  60.2 0.5 collective-permute-start.13
  60.7 3.1 %collective-permute-done.23.refs_11_ = bf16[2,256,128]{2,1,0:T(8,128)(2,1)S(1)} collective-permute-done((bf16[2,256,128]{2,1,0:T(8,128)(2,1)S(1)}, bf16[2,256,128]{2,1,0:T(8,128)(2,1)S(1)}, u32[]{:S(2)}, u32[]{:S(2)}) %collective-permute-start.23) | collective-permute-done | bytes 131104 | tf_op jit(solution)/shard_map/ppermute | solution.py:20
  63.8 0.0 collective-permute-start.27
  63.8 0.6 collective-permute-done.22.refs_10_
  64.4 0.6 collective-permute-done.21.refs_9_
  65.0 0.0 collective-permute-start.25
  65.0 0.1 stack.50.at_ref
  65.1 0.0 collective-permute-done.24.refs_12_
  65.1 0.1 collective-permute-done.27.refs_15_
  65.2 0.6 collective-permute-done.26.refs_14_
  65.8 0.6 collective-permute-done.25.refs_13_
  66.3 2.0 %put.1 = bf16[4,256,1024]{2,1,0:T(8,128)(2,1)} custom-call(s32[16]{0:T(128)S(1)} %stack.50.at_ref, bf16[2,256,128]{2,1,0:T(8,128)(2,1)S(1)} %get-tuple-element.40.refs_0_, bf16[2,256,128]{2,1,0:T(8,128)(2,1)S(1)} %collective-permute-done.9.refs_1_, bf16[2,256,128]{2,1,0:T(8,128)(2,1)S(1)} %collective-permute-done.10.refs_2_, ...), custom_call_target="tpu_custom_call" | custom-call | tf_op jit(solution)/shard_map/put/pallas_call | solution.py:324
  (17 shorter events, 0.1 us)
Async XLA Ops:
  8.8 2.1 %collective-permute-start.1 = (bf16[512,512]{1,0:T(8,128)(2,1)S(1)}, bf16[512,512]{1,0:T(8,128)(2,1)S(1)}, u32[]{:S(2)}, u32[]{:S(2)}) collective-permute-start(bf16[512,512]{1,0:T(8,128)(2,1)S(1)} %get-tuple-element.25.after), channel_id=1, source_target_pairs={{0,2},{2,0},{4,6},{6,4},{8,10},{10,8},{12,14},{14,12},{16,18},{18,... | collective-permute-start | bytes 1572872 | tf_op jit(solution)/shard_map/ppermute | solution.py:20
  11.6 15.2 %collective-permute-start.3 = (bf16[512,128]{1,0:T(8,128)(2,1)S(1)}, bf16[512,128]{1,0:T(8,128)(2,1)S(1)}, u32[]{:S(2)}, u32[]{:S(2)}) collective-permute-start(bf16[512,128]{1,0:T(8,128)(2,1)S(1)} %get-tuple-element.30), channel_id=1, source_target_pairs={{0,12},{2,14},{4,8},{6,10},{8,4},{10,6},{12,0},{14,2},{16,28},{18,... | collective-permute-start | bytes 393224 | tf_op jit(solution)/shard_map/ppermute | solution.py:20
  15.5 11.3 %collective-permute-start.4 = (bf16[512,128]{1,0:T(8,128)(2,1)S(1)}, bf16[512,128]{1,0:T(8,128)(2,1)S(1)}, u32[]{:S(2)}, u32[]{:S(2)}) collective-permute-start(bf16[512,128]{1,0:T(8,128)(2,1)S(1)} %get-tuple-element.31), channel_id=1, source_target_pairs={{0,4},{2,6},{4,0},{6,2},{8,12},{10,14},{12,8},{14,10},{16,20},{18,... | collective-permute-start | bytes 393224 | tf_op jit(solution)/shard_map/ppermute | solution.py:20
  16.0 10.8 %collective-permute-start.2 = (bf16[512,128]{1,0:T(8,128)(2,1)S(1)}, bf16[512,128]{1,0:T(8,128)(2,1)S(1)}, u32[]{:S(2)}, u32[]{:S(2)}) collective-permute-start(bf16[512,128]{1,0:T(8,128)(2,1)S(1)} %get-tuple-element.27.refs_0_), channel_id=1, source_target_pairs={{0,8},{2,10},{4,12},{6,14},{8,0},{10,2},{12,4},{14,6},{16,24},{18,... | collective-permute-start | bytes 393224 | tf_op jit(solution)/shard_map/ppermute | solution.py:20
  16.2 19.8 %collective-permute-start = (bf16[5,256,256]{2,1,0:T(8,128)(2,1)S(1)}, bf16[5,256,256]{2,1,0:T(8,128)(2,1)S(1)}, u32[]{:S(2)}, u32[]{:S(2)}) collective-permute-start(bf16[5,256,256]{2,1,0:T(8,128)(2,1)S(1)} %pack.1.refs_0_), channel_id=1, source_target_pairs={{0,1},{1,0},{2,3},{3,2},{4,5},{5,4},{6,7},{7,6},{8,9},{9,8},{10,11... | collective-permute-start | bytes 1966088 | tf_op jit(solution)/shard_map/ppermute | solution.py:419
  26.8 2.8 %collective-permute-start.5 = (bf16[512,512]{1,0:T(8,128)(2,1)S(1)}, bf16[512,512]{1,0:T(8,128)(2,1)S(1)}, u32[]{:S(2)}, u32[]{:S(2)}) collective-permute-start(bf16[512,512]{1,0:T(8,128)(2,1)S(1)} %get-tuple-element.32), channel_id=1, source_target_pairs={{0,2},{2,0},{4,6},{6,4},{8,10},{10,8},{12,14},{14,12},{16,18},{18,... | collective-permute-start | bytes 1572872 | tf_op jit(solution)/shard_map/ppermute | solution.py:20
  27.0 9.8 %collective-permute-start.7 = (bf16[512,128]{1,0:T(8,128)(2,1)S(1)}, bf16[512,128]{1,0:T(8,128)(2,1)S(1)}, u32[]{:S(2)}, u32[]{:S(2)}) collective-permute-start(bf16[512,128]{1,0:T(8,128)(2,1)S(1)} %add_convert_fusion.1), channel_id=1, source_target_pairs={{0,16},{2,18},{4,20},{6,22},{8,24},{10,26},{12,28},{14,30},{16,0},... | collective-permute-start | bytes 393224 | tf_op jit(solution)/shard_map/ppermute | solution.py:20
  30.3 9.4 %collective-permute-start.17 = (bf16[512,128]{1,0:T(8,128)(2,1)S(1)}, bf16[512,128]{1,0:T(8,128)(2,1)S(1)}, u32[]{:S(2)}, u32[]{:S(2)}) collective-permute-start(bf16[512,128]{1,0:T(8,128)(2,1)S(1)} %get-tuple-element.43), channel_id=1, source_target_pairs={{0,12},{2,14},{4,8},{6,10},{8,4},{10,6},{12,0},{14,2},{16,28},{18,... | collective-permute-start | bytes 393224 | tf_op jit(solution)/shard_map/ppermute | solution.py:20
  32.9 6.8 %collective-permute-start.18 = (bf16[512,128]{1,0:T(8,128)(2,1)S(1)}, bf16[512,128]{1,0:T(8,128)(2,1)S(1)}, u32[]{:S(2)}, u32[]{:S(2)}) collective-permute-start(bf16[512,128]{1,0:T(8,128)(2,1)S(1)} %get-tuple-element.44), channel_id=1, source_target_pairs={{0,4},{2,6},{4,0},{6,2},{8,12},{10,14},{12,8},{14,10},{16,20},{18,... | collective-permute-start | bytes 393224 | tf_op jit(solution)/shard_map/ppermute | solution.py:20
  33.4 8.1 %collective-permute-start.16 = (bf16[512,128]{1,0:T(8,128)(2,1)S(1)}, bf16[512,128]{1,0:T(8,128)(2,1)S(1)}, u32[]{:S(2)}, u32[]{:S(2)}) collective-permute-start(bf16[512,128]{1,0:T(8,128)(2,1)S(1)} %get-tuple-element.33.refs_1_.after), channel_id=1, source_target_pairs={{0,8},{2,10},{4,12},{6,14},{8,0},{10,2},{12,4},{14,6},{16,24},{18,... | collective-permute-start | bytes 393224 | tf_op jit(solution)/shard_map/ppermute | solution.py:20
  35.9 7.9 %copy-start = (bf16[4,256,512]{2,1,0:T(8,128)(2,1)S(1)}, bf16[4,256,512]{2,1,0:T(8,128)(2,1)}, u32[]{:S(2)}) copy-start(bf16[4,256,512]{2,1,0:T(8,128)(2,1)} %inverses.5) | copy-start | bytes 3145732
  35.9 7.4 %collective-permute-start.6 = (bf16[5,256,256]{2,1,0:T(8,128)(2,1)S(1)}, bf16[5,256,256]{2,1,0:T(8,128)(2,1)S(1)}, u32[]{:S(2)}, u32[]{:S(2)}) collective-permute-start(bf16[5,256,256]{2,1,0:T(8,128)(2,1)S(1)} %anchor.4.here), channel_id=1, source_target_pairs={{0,2},{2,0},{4,6},{6,4},{8,10},{10,8},{12,14},{14,12},{16,18},{18,... | collective-permute-start | bytes 1966088 | tf_op jit(solution)/shard_map/ppermute | solution.py:20
  37.5 6.4 %collective-permute-start.8 = (bf16[2,256,128]{2,1,0:T(8,128)(2,1)}, bf16[2,256,128]{2,1,0:T(8,128)(2,1)S(1)}, u32[]{:S(2)}, u32[]{:S(2)}) collective-permute-start(bf16[2,256,128]{2,1,0:T(8,128)(2,1)} %get-tuple-element.47), channel_id=1, source_target_pairs={{0,1},{1,0},{2,3},{3,2},{4,5},{5,4},{6,7},{7,6},{8,9},{9,8},{10,11... | collective-permute-start | bytes 393224 | tf_op jit(solution)/shard_map/ppermute | solution.py:432
  41.6 8.7 %collective-permute-start.19 = (bf16[512,128]{1,0:T(8,128)(2,1)S(1)}, bf16[512,128]{1,0:T(8,128)(2,1)S(1)}, u32[]{:S(2)}, u32[]{:S(2)}) collective-permute-start(bf16[512,128]{1,0:T(8,128)(2,1)S(1)} %add_convert_fusion), channel_id=1, source_target_pairs={{0,16},{2,18},{4,20},{6,22},{8,24},{10,26},{12,28},{14,30},{16,0},... | collective-permute-start | bytes 393224 | tf_op jit(solution)/shard_map/ppermute | solution.py:20
  45.9 7.7 %collective-permute-start.11 = (bf16[2,256,128]{2,1,0:T(8,128)(2,1)S(1)}, bf16[2,256,128]{2,1,0:T(8,128)(2,1)S(1)}, u32[]{:S(2)}, u32[]{:S(2)}) collective-permute-start(bf16[2,256,128]{2,1,0:T(8,128)(2,1)S(1)} %get-tuple-element.40.refs_0_), channel_id=1, source_target_pairs={{0,4},{2,6},{4,0},{6,2},{8,12},{10,14},{12,8},{14,10},{16,20},{18,... | collective-permute-start | bytes 393224 | tf_op jit(solution)/shard_map/ppermute | solution.py:20
  46.5 7.4 %collective-permute-start.10 = (bf16[2,256,128]{2,1,0:T(8,128)(2,1)S(1)}, bf16[2,256,128]{2,1,0:T(8,128)(2,1)S(1)}, u32[]{:S(2)}, u32[]{:S(2)}) collective-permute-start(bf16[2,256,128]{2,1,0:T(8,128)(2,1)S(1)} %get-tuple-element.40.refs_0_), channel_id=1, source_target_pairs={{0,12},{2,14},{4,8},{6,10},{8,4},{10,6},{12,0},{14,2},{16,28},{18,... | collective-permute-start | bytes 393224 | tf_op jit(solution)/shard_map/ppermute | solution.py:20
  50.3 5.0 %collective-permute-start.20 = (bf16[2,256,128]{2,1,0:T(8,128)(2,1)S(1)}, bf16[2,256,128]{2,1,0:T(8,128)(2,1)S(1)}, u32[]{:S(2)}, u32[]{:S(2)}) collective-permute-start(bf16[2,256,128]{2,1,0:T(8,128)(2,1)S(1)} %get-tuple-element.45), channel_id=1, source_target_pairs={{0,1},{1,0},{2,3},{3,2},{4,5},{5,4},{6,7},{7,6},{8,9},{9,8},{10,11... | collective-permute-start | bytes 393224 | tf_op jit(solution)/shard_map/ppermute | solution.py:439
  50.9 5.0 %collective-permute-start.9 = (bf16[2,256,128]{2,1,0:T(8,128)(2,1)S(1)}, bf16[2,256,128]{2,1,0:T(8,128)(2,1)S(1)}, u32[]{:S(2)}, u32[]{:S(2)}) collective-permute-start(bf16[2,256,128]{2,1,0:T(8,128)(2,1)S(1)} %get-tuple-element.40.refs_0_), channel_id=1, source_target_pairs={{0,8},{2,10},{4,12},{6,14},{8,0},{10,2},{12,4},{14,6},{16,24},{18,... | collective-permute-start | bytes 393224 | tf_op jit(solution)/shard_map/ppermute | solution.py:20
  50.9 8.7 %collective-permute-start.12 = (bf16[2,256,128]{2,1,0:T(8,128)(2,1)S(1)}, bf16[2,256,128]{2,1,0:T(8,128)(2,1)S(1)}, u32[]{:S(2)}, u32[]{:S(2)}) collective-permute-start(bf16[2,256,128]{2,1,0:T(8,128)(2,1)S(1)} %get-tuple-element.40.refs_0_), channel_id=1, source_target_pairs={{0,2},{2,0},{4,6},{6,4},{8,10},{10,8},{12,14},{14,12},{16,18},{18,... | collective-permute-start | bytes 393224 | tf_op jit(solution)/shard_map/ppermute | solution.py:20
  53.6 6.7 %collective-permute-start.15 = (bf16[2,256,128]{2,1,0:T(8,128)(2,1)S(1)}, bf16[2,256,128]{2,1,0:T(8,128)(2,1)S(1)}, u32[]{:S(2)}, u32[]{:S(2)}) collective-permute-start(bf16[2,256,128]{2,1,0:T(8,128)(2,1)S(1)} %collective-permute-done.11.refs_3_), channel_id=1, source_target_pairs={{0,2},{2,0},{4,6},{6,4},{8,10},{10,8},{12,14},{14,12},{16,18},{18,... | collective-permute-start | bytes 393224 | tf_op jit(solution)/shard_map/ppermute | solution.py:20
  53.9 6.4 %collective-permute-start.14 = (bf16[2,256,128]{2,1,0:T(8,128)(2,1)S(1)}, bf16[2,256,128]{2,1,0:T(8,128)(2,1)S(1)}, u32[]{:S(2)}, u32[]{:S(2)}) collective-permute-start(bf16[2,256,128]{2,1,0:T(8,128)(2,1)S(1)} %collective-permute-done.10.refs_2_), channel_id=1, source_target_pairs={{0,2},{2,0},{4,6},{6,4},{8,10},{10,8},{12,14},{14,12},{16,18},{18,... | collective-permute-start | bytes 393224 | tf_op jit(solution)/shard_map/ppermute | solution.py:20
  56.7 7.2 %collective-permute-start.23 = (bf16[2,256,128]{2,1,0:T(8,128)(2,1)S(1)}, bf16[2,256,128]{2,1,0:T(8,128)(2,1)S(1)}, u32[]{:S(2)}, u32[]{:S(2)}) collective-permute-start(bf16[2,256,128]{2,1,0:T(8,128)(2,1)S(1)} %chain.3.refs_8_), channel_id=1, source_target_pairs={{0,4},{2,6},{4,0},{6,2},{8,12},{10,14},{12,8},{14,10},{16,20},{18,... | collective-permute-start | bytes 393224 | tf_op jit(solution)/shard_map/ppermute | solution.py:20
  57.2 7.2 %collective-permute-start.22 = (bf16[2,256,128]{2,1,0:T(8,128)(2,1)S(1)}, bf16[2,256,128]{2,1,0:T(8,128)(2,1)S(1)}, u32[]{:S(2)}, u32[]{:S(2)}) collective-permute-start(bf16[2,256,128]{2,1,0:T(8,128)(2,1)S(1)} %chain.3.refs_8_), channel_id=1, source_target_pairs={{0,12},{2,14},{4,8},{6,10},{8,4},{10,6},{12,0},{14,2},{16,28},{18,... | collective-permute-start | bytes 393224 | tf_op jit(solution)/shard_map/ppermute | solution.py:20
  59.6 5.4 %collective-permute-start.21 = (bf16[2,256,128]{2,1,0:T(8,128)(2,1)S(1)}, bf16[2,256,128]{2,1,0:T(8,128)(2,1)S(1)}, u32[]{:S(2)}, u32[]{:S(2)}) collective-permute-start(bf16[2,256,128]{2,1,0:T(8,128)(2,1)S(1)} %chain.3.refs_8_), channel_id=1, source_target_pairs={{0,8},{2,10},{4,12},{6,14},{8,0},{10,2},{12,4},{14,6},{16,24},{18,... | collective-permute-start | bytes 393224 | tf_op jit(solution)/shard_map/ppermute | solution.py:20
  60.2 4.9 %collective-permute-start.24 = (bf16[2,256,128]{2,1,0:T(8,128)(2,1)S(1)}, bf16[2,256,128]{2,1,0:T(8,128)(2,1)S(1)}, u32[]{:S(2)}, u32[]{:S(2)}) collective-permute-start(bf16[2,256,128]{2,1,0:T(8,128)(2,1)S(1)} %chain.3.refs_8_), channel_id=1, source_target_pairs={{0,2},{2,0},{4,6},{6,4},{8,10},{10,8},{12,14},{14,12},{16,18},{18,... | collective-permute-start | bytes 393224 | tf_op jit(solution)/shard_map/ppermute | solution.py:20
  60.2 4.9 %collective-permute-start.13 = (bf16[2,256,128]{2,1,0:T(8,128)(2,1)S(1)}, bf16[2,256,128]{2,1,0:T(8,128)(2,1)S(1)}, u32[]{:S(2)}, u32[]{:S(2)}) collective-permute-start(bf16[2,256,128]{2,1,0:T(8,128)(2,1)S(1)} %collective-permute-done.9.refs_1_), channel_id=1, source_target_pairs={{0,2},{2,0},{4,6},{6,4},{8,10},{10,8},{12,14},{14,12},{16,18},{18,... | collective-permute-start | bytes 393224 | tf_op jit(solution)/shard_map/ppermute | solution.py:20
  63.8 1.3 %collective-permute-start.27 = (bf16[2,256,128]{2,1,0:T(8,128)(2,1)S(1)}, bf16[2,256,128]{2,1,0:T(8,128)(2,1)S(1)}, u32[]{:S(2)}, u32[]{:S(2)}) collective-permute-start(bf16[2,256,128]{2,1,0:T(8,128)(2,1)S(1)} %collective-permute-done.23.refs_11_), channel_id=1, source_target_pairs={{0,2},{2,0},{4,6},{6,4},{8,10},{10,8},{12,14},{14,12},{16,18},{18,... | collective-permute-start | bytes 393224 | tf_op jit(solution)/shard_map/ppermute | solution.py:20
  64.4 1.3 %collective-permute-start.26 = (bf16[2,256,128]{2,1,0:T(8,128)(2,1)S(1)}, bf16[2,256,128]{2,1,0:T(8,128)(2,1)S(1)}, u32[]{:S(2)}, u32[]{:S(2)}) collective-permute-start(bf16[2,256,128]{2,1,0:T(8,128)(2,1)S(1)} %collective-permute-done.22.refs_10_), channel_id=1, source_target_pairs={{0,2},{2,0},{4,6},{6,4},{8,10},{10,8},{12,14},{14,12},{16,18},{18,... | collective-permute-start | bytes 393224 | tf_op jit(solution)/shard_map/ppermute | solution.py:20
  65.0 1.3 %collective-permute-start.25 = (bf16[2,256,128]{2,1,0:T(8,128)(2,1)S(1)}, bf16[2,256,128]{2,1,0:T(8,128)(2,1)S(1)}, u32[]{:S(2)}, u32[]{:S(2)}) collective-permute-start(bf16[2,256,128]{2,1,0:T(8,128)(2,1)S(1)} %collective-permute-done.21.refs_9_), channel_id=1, source_target_pairs={{0,2},{2,0},{4,6},{6,4},{8,10},{10,8},{12,14},{14,12},{16,18},{18,... | collective-permute-start | bytes 393224 | tf_op jit(solution)/shard_map/ppermute | solution.py:20

commit v6 on v5

--- a/solution.py
+++ b/solution.py
@@ -381,7 +381,8 @@
     reverse = [sum(((mask >> bit) & 1) << (inner - bit) for bit in range(halvings)) for mask in range(blocks)]
     gray = [2 * (i ^ (i >> 1)) for i in range(1 << inner)]
     cross = gray[:1] + gray[:0:-1]
-    split_at = jnp.stack([(mine ^ reverse[mask]) & ((1 << inner) - 1) for mask in cross]).astype(jnp.int32)
+    outward = cross[:1] + sorted(cross[1:], reverse=True)
+    split_at = jnp.stack([(mine ^ reverse[mask]) & ((1 << inner) - 1) for mask in outward]).astype(jnp.int32)
     put_at = jnp.stack([mine ^ reverse[mask] for mask in cross + [mask + 1 for mask in cross]]).astype(jnp.int32)
     core = flags[0].astype(jnp.int32)[None]
 
@@ -393,8 +394,8 @@
     together = lax.optimization_barrier
 
     def scatter(send, keep, after):
-        pieces = split(split_at, keep, swap(send, "blk", size, 1), len(cross), after)
-        return pieces[0], [swap(piece, "blk", size, mask) for mask, piece in zip(cross[1:], pieces[1:])], pieces[1]
+        pieces = split(split_at, keep, swap(send, "blk", size, 1), len(outward), after)
+        return pieces[0], [swap(piece, "blk", size, mask) for mask, piece in zip(outward[1:], pieces[1:])], pieces[1]
 
     def collect(own, got):
         for piece in got:

time: 68.7 us -> 68.5 us (level)
    ppermute x25, waiting for transfers between devices: 13.8 us -> 13.1 us  [swap(): return lax.ppermute(value, axis, [(i, i ^ mask) for i in range(size)])]
  transfers between devices with their start and end apart: 28 -> 28, of which waited for: 15 -> 13; matrix products, arithmetic and copies ran while one was open for 2% -> 2% of each run, Pallas kernels for 23% -> 23%
where the time goes in v6:
time: 68.5 us; the launch traced here: 68.3 us
  Pallas kernels  27.4 us (40%)
  starting transfers between devices  24.8 us (36%)
  waiting for transfers between devices  14.5 us (21%)
  other arithmetic  1 us (1%)
    ppermute x25, starting transfers between devices, swap(): return lax.ppermute(value, axis, [(i, i ^ mask) for i in range(size)])  21.9 us
    pallas_call x2, Pallas kernels, gemm(): pl.pallas_call(functools.partial(gemm_kernel, steps[0], cuts), in_specs=[...  17.6 us
    ppermute x25, waiting for transfers between devices, swap(): return lax.ppermute(value, axis, [(i, i ^ mask) for i in range(size)])  13.1 us
    pallas_call x2, Pallas kernels, chain(): pl.pallas_call(functools.partial(chain_kernel, units, steps, inverses.sha...  2.82 us
    pallas_call x1, Pallas kernels, put(): pl.pallas_call(functools.partial(put_kernel, firsts), in_specs=[SMEM] + [...  1.98 us
    ppermute x1, starting transfers between devices, shards(): here = lax.ppermute(sent, 'rows', pair)  1.86 us
    ppermute x1, waiting for transfers between devices, shards(): far_b = lax.ppermute(rounded, 'rows', pair)  1.43 us
  transfers between devices with their start and end apart: 28, of which 13 were waited for; matrix products, arithmetic and copies ran while one was open for 2% of the time, Pallas kernels for 23%

profile of v6, /device:TPU:0, one launch (start us, length us, event | category | flops | bytes accessed | tf_op | source)
XLA Modules:
  0.0 68.3 jit_solution(16288486086369236968)
XLA Ops:
  0.0 8.8 %gemm.2 = (bf16[512,512]{1,0:T(8,128)(2,1)S(1)}, bf16[512,512]{1,0:T(8,128)(2,1)S(1)}) custom-call(s32[1]{0:T(128)} %bitcast.9.flag_ref, bf16[4,256,6144]{2,1,0:T(8,128)(2,1)} %panel.3, bf16[6144,1024]{1,0:T(8,128)(2,1)} %solved.3), custom_call_target="tpu_custom_call" | custom-call | flops 1 | bytes 1 | tf_op jit(solution)/shard_map/gemm/pallas_call | solution.py:79
  8.8 0.5 collective-permute-start.1
  9.3 1.2 %pack.1.refs_0_ = bf16[5,256,256]{2,1,0:T(8,128)(2,1)S(1)} custom-call(s32[1]{0:T(128)} %bitcast.9.flag_ref, bf16[4,256,512]{2,1,0:T(8,128)(2,1)} %inverses.5, bf16[4,256,2048]{2,1,0:T(8,128)(2,1)} %window.3, bf16[512,512]{1,0:T(8,128)(2,1)S(1)} %get-tuple-element.25.after), custom_call_target="tpu_custom_call" | custom-call | flops 1 | bytes 1310720 | tf_op jit(solution)/shard_map/pack/pallas_call | solution.py:152
  10.6 0.1 pad_add_fusion.at_ref
  10.6 0.2 collective-permute-done.1.got
  10.9 0.7 %split.2 = (f32[512,128]{1,0:T(8,128)S(1)}, bf16[512,128]{1,0:T(8,128)(2,1)S(1)}, bf16[512,128]{1,0:T(8,128)(2,1)S(1)}, bf16[512,128]{1,0:T(8,128)(2,1)S(1)}) custom-call(s32[4]{0:T(128)S(1)} %pad_add_fusion.at_ref, bf16[512,512]{1,0:T(8,128)(2,1)S(1)} %get-tuple-element.26.keep, bf16[512,512]{1,0:T(8,128)(2,1)S(1)} %collective-permute-done.1.got, ...), custom_call_target="tpu_custom_call" | custom-call | tf_op jit(solution)/shard_map/split/pallas_call | solution.py:110
  11.6 3.0 %collective-permute-start.3 = (bf16[512,128]{1,0:T(8,128)(2,1)S(1)}, bf16[512,128]{1,0:T(8,128)(2,1)S(1)}, u32[]{:S(2)}, u32[]{:S(2)}) collective-permute-start(bf16[512,128]{1,0:T(8,128)(2,1)S(1)} %get-tuple-element.30), channel_id=1, source_target_pairs={{0,8},{2,10},{4,12},{6,14},{8,0},{10,2},{12,4},{14,6},{16,24},{18,... | collective-permute-start | bytes 393224 | tf_op jit(solution)/shard_map/ppermute | solution.py:20
  14.6 1.5 %collective-permute-start.4 = (bf16[512,128]{1,0:T(8,128)(2,1)S(1)}, bf16[512,128]{1,0:T(8,128)(2,1)S(1)}, u32[]{:S(2)}, u32[]{:S(2)}) collective-permute-start(bf16[512,128]{1,0:T(8,128)(2,1)S(1)} %get-tuple-element.31), channel_id=1, source_target_pairs={{0,4},{2,6},{4,0},{6,2},{8,12},{10,14},{12,8},{14,10},{16,20},{18,... | collective-permute-start | bytes 393224 | tf_op jit(solution)/shard_map/ppermute | solution.py:20
  16.1 0.0 collective-permute-start.2
  16.1 1.9 %collective-permute-start = (bf16[5,256,256]{2,1,0:T(8,128)(2,1)S(1)}, bf16[5,256,256]{2,1,0:T(8,128)(2,1)S(1)}, u32[]{:S(2)}, u32[]{:S(2)}) collective-permute-start(bf16[5,256,256]{2,1,0:T(8,128)(2,1)S(1)} %pack.1.refs_0_), channel_id=1, source_target_pairs={{0,1},{1,0},{2,3},{3,2},{4,5},{5,4},{6,7},{7,6},{8,9},{9,8},{10,11... | collective-permute-start | bytes 1966088 | tf_op jit(solution)/shard_map/ppermute | solution.py:420
  18.0 8.8 %gemm.3 = (bf16[512,512]{1,0:T(8,128)(2,1)S(1)}, bf16[512,512]{1,0:T(8,128)(2,1)S(1)}) custom-call(s32[1]{0:T(128)} %bitcast.9.flag_ref, bf16[4,256,6144]{2,1,0:T(8,128)(2,1)} %panel.3, bf16[6144,1024]{1,0:T(8,128)(2,1)} %solved.3, bf16[512,128]{1,0:T(8,128)(2,1)S(1)} %get-tuple-element.27.refs_0_), custom_call_target="tpu_custom_call" | custom-call | flops 1 | bytes 1 | tf_op jit(solution)/shard_map/gemm/pallas_call | solution.py:79
  26.8 0.0 collective-permute-done.4
  26.8 0.0 collective-permute-done.2
  26.8 0.1 collective-permute-start.5
  26.9 0.1 add_convert_fusion.1
  27.0 2.7 %collective-permute-start.7 = (bf16[512,128]{1,0:T(8,128)(2,1)S(1)}, bf16[512,128]{1,0:T(8,128)(2,1)S(1)}, u32[]{:S(2)}, u32[]{:S(2)}) collective-permute-start(bf16[512,128]{1,0:T(8,128)(2,1)S(1)} %add_convert_fusion.1), channel_id=1, source_target_pairs={{0,16},{2,18},{4,20},{6,22},{8,24},{10,26},{12,28},{14,30},{16,0},... | collective-permute-start | bytes 393224 | tf_op jit(solution)/shard_map/ppermute | solution.py:20
  29.6 0.0 collective-permute-done.5.got
  29.6 0.7 %split.3 = (f32[512,128]{1,0:T(8,128)S(1)}, bf16[512,128]{1,0:T(8,128)(2,1)S(1)}, bf16[512,128]{1,0:T(8,128)(2,1)S(1)}, bf16[512,128]{1,0:T(8,128)(2,1)S(1)}) custom-call(s32[4]{0:T(128)S(1)} %pad_add_fusion.at_ref, bf16[512,512]{1,0:T(8,128)(2,1)S(1)} %get-tuple-element.28.keep, bf16[512,512]{1,0:T(8,128)(2,1)S(1)} %collective-permute-done.5.got), custom_call_target="tpu_custom_call" | custom-call | tf_op jit(solution)/shard_map/split/pallas_call | solution.py:110
  30.3 1.6 %collective-permute-start.17 = (bf16[512,128]{1,0:T(8,128)(2,1)S(1)}, bf16[512,128]{1,0:T(8,128)(2,1)S(1)}, u32[]{:S(2)}, u32[]{:S(2)}) collective-permute-start(bf16[512,128]{1,0:T(8,128)(2,1)S(1)} %get-tuple-element.43), channel_id=1, source_target_pairs={{0,8},{2,10},{4,12},{6,14},{8,0},{10,2},{12,4},{14,6},{16,24},{18,... | collective-permute-start | bytes 393224 | tf_op jit(solution)/shard_map/ppermute | solution.py:20
  32.0 1.5 %collective-permute-start.18 = (bf16[512,128]{1,0:T(8,128)(2,1)S(1)}, bf16[512,128]{1,0:T(8,128)(2,1)S(1)}, u32[]{:S(2)}, u32[]{:S(2)}) collective-permute-start(bf16[512,128]{1,0:T(8,128)(2,1)S(1)} %get-tuple-element.44), channel_id=1, source_target_pairs={{0,4},{2,6},{4,0},{6,2},{8,12},{10,14},{12,8},{14,10},{16,20},{18,... | collective-permute-start | bytes 393224 | tf_op jit(solution)/shard_map/ppermute | solution.py:20
  33.5 0.4 collective-permute-start.16
  33.9 1.0 %cut.1 = (f32[2,256,128]{2,1,0:T(8,128)S(1)}, f32[2,256,128]{2,1,0:T(8,128)S(1)}) custom-call(s32[1]{0:T(128)} %bitcast.at_ref, f32[4,256,1024]{2,1,0:T(8,128)} %loads.1, bf16[512,128]{1,0:T(8,128)(2,1)S(1)} %get-tuple-element.33.refs_1_.after), custom_call_target="tpu_custom_call" | custom-call | flops 1 | bytes 8388608 | tf_op jit(solution)/shard_map/cut/pallas_call | solution.py:353
  34.9 1.0 %fetch.1.refs_2_.refs_0_ = bf16[1,256,512]{2,1,0:T(8,128)(2,1)S(1)} custom-call(bf16[4,256,2048]{2,1,0:T(8,128)(2,1)} %window.3, f32[2,256,128]{2,1,0:T(8,128)S(1)} %get-tuple-element.34.refs_1_.after), custom_call_target="tpu_custom_call" | custom-call | flops 1 | bytes 4194304 | tf_op jit(solution)/shard_map/fetch/pallas_call | solution.py:279
  35.9 0.0 copy-start
  35.9 0.1 collective-permute-start.6
  36.0 0.7 %collective-permute-done.7.refs_0_ = bf16[512,128]{1,0:T(8,128)(2,1)S(1)} collective-permute-done((bf16[512,128]{1,0:T(8,128)(2,1)S(1)}, bf16[512,128]{1,0:T(8,128)(2,1)S(1)}, u32[]{:S(2)}, u32[]{:S(2)}) %collective-permute-start.7) | collective-permute-done | bytes 131104 | tf_op jit(solution)/shard_map/ppermute | solution.py:20
  36.8 0.7 %fusion.1 = (bf16[2,256,128]{2,1,0:T(8,128)(2,1)}, f32[2,256,128]{2,1,0:T(8,128)S(1)}) fusion(f32[2,256,128]{2,1,0:T(8,128)S(1)} %get-tuple-element.34.refs_1_.after, f32[2,256,128]{2,1,0:T(8,128)S(1)} %bitcast.17), kind=kLoop, calls=%fused_computation.6 | loop fusion | flops 131072 | bytes 917504 | tf_op jit(solution)/shard_map/convert_element_type | solution.py:433
  37.5 0.5 collective-permute-start.8
  38.0 0.4 collective-permute-done.17
  38.4 3.0 %collective-permute-done.16 = bf16[512,128]{1,0:T(8,128)(2,1)S(1)} collective-permute-done((bf16[512,128]{1,0:T(8,128)(2,1)S(1)}, bf16[512,128]{1,0:T(8,128)(2,1)S(1)}, u32[]{:S(2)}, u32[]{:S(2)}) %collective-permute-start.16) | collective-permute-done | bytes 131104 | tf_op jit(solution)/shard_map/ppermute | solution.py:20
  41.5 0.1 add_convert_fusion
  41.5 0.9 %collective-permute-start.19 = (bf16[512,128]{1,0:T(8,128)(2,1)S(1)}, bf16[512,128]{1,0:T(8,128)(2,1)S(1)}, u32[]{:S(2)}, u32[]{:S(2)}) collective-permute-start(bf16[512,128]{1,0:T(8,128)(2,1)S(1)} %add_convert_fusion), channel_id=1, source_target_pairs={{0,16},{2,18},{4,20},{6,22},{8,24},{10,26},{12,28},{14,30},{16,0},... | collective-permute-start | bytes 393224 | tf_op jit(solution)/shard_map/ppermute | solution.py:20
  42.4 0.0 collective-permute-done.6.there
  42.4 0.4 unpack.1.far_w
  42.9 2.0 %chain.2 = (bf16[2,256,128]{2,1,0:T(8,128)(2,1)S(1)}, f32[2,256,128]{2,1,0:T(8,128)S(1)}) custom-call(s32[1]{0:T(128)} %bitcast.8.side_ref, bf16[4,256,512]{2,1,0:T(8,128)(2,1)S(1)} %copy-done, bf16[10,256,256]{2,1,0:T(8,128)(2,1)S(1)} %unpack.1.far_w, f32[2,256,128]{2,1,0:T(8,128)S(1)} %get-tuple-element.48.own_r, ...), custom_call_target="tpu_custom_call" | custom-call | tf_op jit(solution)/shard_map/chain/pallas_call | solution.py:258
  44.9 1.6 %collective-permute-start.11 = (bf16[2,256,128]{2,1,0:T(8,128)(2,1)S(1)}, bf16[2,256,128]{2,1,0:T(8,128)(2,1)S(1)}, u32[]{:S(2)}, u32[]{:S(2)}) collective-permute-start(bf16[2,256,128]{2,1,0:T(8,128)(2,1)S(1)} %get-tuple-element.40.refs_0_), channel_id=1, source_target_pairs={{0,4},{2,6},{4,0},{6,2},{8,12},{10,14},{12,8},{14,10},{16,20},{18,... | collective-permute-start | bytes 393224 | tf_op jit(solution)/shard_map/ppermute | solution.py:20
  46.5 3.4 %collective-permute-start.10 = (bf16[2,256,128]{2,1,0:T(8,128)(2,1)S(1)}, bf16[2,256,128]{2,1,0:T(8,128)(2,1)S(1)}, u32[]{:S(2)}, u32[]{:S(2)}) collective-permute-start(bf16[2,256,128]{2,1,0:T(8,128)(2,1)S(1)} %get-tuple-element.40.refs_0_), channel_id=1, source_target_pairs={{0,12},{2,14},{4,8},{6,10},{8,4},{10,6},{12,0},{14,2},{16,28},{18,... | collective-permute-start | bytes 393224 | tf_op jit(solution)/shard_map/ppermute | solution.py:20
  49.9 0.3 collective-permute-done.19.refs_0_
  50.3 0.6 collective-permute-start.20
  50.9 0.0 collective-permute-start.9
  50.9 0.0 collective-permute-start.12
  50.9 0.0 collective-permute-done.11.refs_3_
  50.9 0.5 collective-permute-start.15
  51.4 2.5 %collective-permute-done.10.refs_2_ = bf16[2,256,128]{2,1,0:T(8,128)(2,1)S(1)} collective-permute-done((bf16[2,256,128]{2,1,0:T(8,128)(2,1)S(1)}, bf16[2,256,128]{2,1,0:T(8,128)(2,1)S(1)}, u32[]{:S(2)}, u32[]{:S(2)}) %collective-permute-start.10) | collective-permute-done | bytes 131104 | tf_op jit(solution)/shard_map/ppermute | solution.py:20
  53.9 0.0 collective-permute-start.14
  53.9 1.4 %collective-permute-done.20.far_r = bf16[2,256,128]{2,1,0:T(8,128)(2,1)S(1)} collective-permute-done((bf16[2,256,128]{2,1,0:T(8,128)(2,1)S(1)}, bf16[2,256,128]{2,1,0:T(8,128)(2,1)S(1)}, u32[]{:S(2)}, u32[]{:S(2)}) %collective-permute-start.20) | collective-permute-done | bytes 131104 | tf_op jit(solution)/shard_map/ppermute | solution.py:440
  55.3 0.5 collective-permute-done.9.refs_1_
  55.8 0.8 %chain.3.refs_8_ = bf16[2,256,128]{2,1,0:T(8,128)(2,1)S(1)} custom-call(s32[1]{0:T(128)} %bitcast.8.side_ref, bf16[4,256,512]{2,1,0:T(8,128)(2,1)S(1)} %copy-done, bf16[10,256,256]{2,1,0:T(8,128)(2,1)S(1)} %unpack.1.far_w, f32[2,256,128]{2,1,0:T(8,128)S(1)} %get-tuple-element.46.own_r, bf16[2,256,128]{2,1,0:T(8,128)(2,1)S(1)} %collective-permute-done.20.far_r, ...), custom_call_target="tpu_custom_call" | custom-call | tf_op jit(solution)/shard_map/chain/pallas_call | solution.py:258
  56.7 0.5 collective-permute-start.23
  57.1 2.1 %collective-permute-start.22 = (bf16[2,256,128]{2,1,0:T(8,128)(2,1)S(1)}, bf16[2,256,128]{2,1,0:T(8,128)(2,1)S(1)}, u32[]{:S(2)}, u32[]{:S(2)}) collective-permute-start(bf16[2,256,128]{2,1,0:T(8,128)(2,1)S(1)} %chain.3.refs_8_), channel_id=1, source_target_pairs={{0,12},{2,14},{4,8},{6,10},{8,4},{10,6},{12,0},{14,2},{16,28},{18,... | collective-permute-start | bytes 393224 | tf_op jit(solution)/shard_map/ppermute | solution.py:20
  59.2 0.0 collective-permute-done.12.refs_4_
  59.2 1.0 %collective-permute-start.21 = (bf16[2,256,128]{2,1,0:T(8,128)(2,1)S(1)}, bf16[2,256,128]{2,1,0:T(8,128)(2,1)S(1)}, u32[]{:S(2)}, u32[]{:S(2)}) collective-permute-start(bf16[2,256,128]{2,1,0:T(8,128)(2,1)S(1)} %chain.3.refs_8_), channel_id=1, source_target_pairs={{0,8},{2,10},{4,12},{6,14},{8,0},{10,2},{12,4},{14,6},{16,24},{18,... | collective-permute-start | bytes 393224 | tf_op jit(solution)/shard_map/ppermute | solution.py:20
  60.2 0.0 collective-permute-done.15.refs_7_
  60.2 0.5 collective-permute-start.13
  60.7 2.1 %collective-permute-done.23.refs_11_ = bf16[2,256,128]{2,1,0:T(8,128)(2,1)S(1)} collective-permute-done((bf16[2,256,128]{2,1,0:T(8,128)(2,1)S(1)}, bf16[2,256,128]{2,1,0:T(8,128)(2,1)S(1)}, u32[]{:S(2)}, u32[]{:S(2)}) %collective-permute-start.23) | collective-permute-done | bytes 131104 | tf_op jit(solution)/shard_map/ppermute | solution.py:20
  62.8 1.3 %collective-permute-done.22.refs_10_ = bf16[2,256,128]{2,1,0:T(8,128)(2,1)S(1)} collective-permute-done((bf16[2,256,128]{2,1,0:T(8,128)(2,1)S(1)}, bf16[2,256,128]{2,1,0:T(8,128)(2,1)S(1)}, u32[]{:S(2)}, u32[]{:S(2)}) %collective-permute-start.22) | collective-permute-done | bytes 131104 | tf_op jit(solution)/shard_map/ppermute | solution.py:20
  64.1 0.0 collective-permute-start.26
  64.1 0.7 %collective-permute-done.21.refs_9_ = bf16[2,256,128]{2,1,0:T(8,128)(2,1)S(1)} collective-permute-done((bf16[2,256,128]{2,1,0:T(8,128)(2,1)S(1)}, bf16[2,256,128]{2,1,0:T(8,128)(2,1)S(1)}, u32[]{:S(2)}, u32[]{:S(2)}) %collective-permute-start.21) | collective-permute-done | bytes 131104 | tf_op jit(solution)/shard_map/ppermute | solution.py:20
  64.8 0.0 collective-permute-start.25
  64.8 0.1 stack.50.at_ref
  64.9 0.0 collective-permute-done.27.refs_15_
  64.9 0.5 collective-permute-done.26.refs_14_
  65.4 0.7 %collective-permute-done.25.refs_13_ = bf16[2,256,128]{2,1,0:T(8,128)(2,1)S(1)} collective-permute-done((bf16[2,256,128]{2,1,0:T(8,128)(2,1)S(1)}, bf16[2,256,128]{2,1,0:T(8,128)(2,1)S(1)}, u32[]{:S(2)}, u32[]{:S(2)}) %collective-permute-start.25) | collective-permute-done | bytes 131104 | tf_op jit(solution)/shard_map/ppermute | solution.py:20
  66.1 2.0 %put.1 = bf16[4,256,1024]{2,1,0:T(8,128)(2,1)} custom-call(s32[16]{0:T(128)S(1)} %stack.50.at_ref, bf16[2,256,128]{2,1,0:T(8,128)(2,1)S(1)} %get-tuple-element.40.refs_0_, bf16[2,256,128]{2,1,0:T(8,128)(2,1)S(1)} %collective-permute-done.9.refs_1_, bf16[2,256,128]{2,1,0:T(8,128)(2,1)S(1)} %collective-permute-done.10.refs_2_, ...), custom_call_target="tpu_custom_call" | custom-call | tf_op jit(solution)/shard_map/put/pallas_call | solution.py:324
  (17 shorter events, 0.1 us)
Async XLA Ops:
  8.8 2.1 %collective-permute-start.1 = (bf16[512,512]{1,0:T(8,128)(2,1)S(1)}, bf16[512,512]{1,0:T(8,128)(2,1)S(1)}, u32[]{:S(2)}, u32[]{:S(2)}) collective-permute-start(bf16[512,512]{1,0:T(8,128)(2,1)S(1)} %get-tuple-element.25.after), channel_id=1, source_target_pairs={{0,2},{2,0},{4,6},{6,4},{8,10},{10,8},{12,14},{14,12},{16,18},{18,... | collective-permute-start | bytes 1572872 | tf_op jit(solution)/shard_map/ppermute | solution.py:20
  11.6 15.2 %collective-permute-start.3 = (bf16[512,128]{1,0:T(8,128)(2,1)S(1)}, bf16[512,128]{1,0:T(8,128)(2,1)S(1)}, u32[]{:S(2)}, u32[]{:S(2)}) collective-permute-start(bf16[512,128]{1,0:T(8,128)(2,1)S(1)} %get-tuple-element.30), channel_id=1, source_target_pairs={{0,8},{2,10},{4,12},{6,14},{8,0},{10,2},{12,4},{14,6},{16,24},{18,... | collective-permute-start | bytes 393224 | tf_op jit(solution)/shard_map/ppermute | solution.py:20
  14.6 12.2 %collective-permute-start.4 = (bf16[512,128]{1,0:T(8,128)(2,1)S(1)}, bf16[512,128]{1,0:T(8,128)(2,1)S(1)}, u32[]{:S(2)}, u32[]{:S(2)}) collective-permute-start(bf16[512,128]{1,0:T(8,128)(2,1)S(1)} %get-tuple-element.31), channel_id=1, source_target_pairs={{0,4},{2,6},{4,0},{6,2},{8,12},{10,14},{12,8},{14,10},{16,20},{18,... | collective-permute-start | bytes 393224 | tf_op jit(solution)/shard_map/ppermute | solution.py:20
  16.1 10.7 %collective-permute-start.2 = (bf16[512,128]{1,0:T(8,128)(2,1)S(1)}, bf16[512,128]{1,0:T(8,128)(2,1)S(1)}, u32[]{:S(2)}, u32[]{:S(2)}) collective-permute-start(bf16[512,128]{1,0:T(8,128)(2,1)S(1)} %get-tuple-element.27.refs_0_), channel_id=1, source_target_pairs={{0,12},{2,14},{4,8},{6,10},{8,4},{10,6},{12,0},{14,2},{16,28},{18,... | collective-permute-start | bytes 393224 | tf_op jit(solution)/shard_map/ppermute | solution.py:20
  16.1 19.8 %collective-permute-start = (bf16[5,256,256]{2,1,0:T(8,128)(2,1)S(1)}, bf16[5,256,256]{2,1,0:T(8,128)(2,1)S(1)}, u32[]{:S(2)}, u32[]{:S(2)}) collective-permute-start(bf16[5,256,256]{2,1,0:T(8,128)(2,1)S(1)} %pack.1.refs_0_), channel_id=1, source_target_pairs={{0,1},{1,0},{2,3},{3,2},{4,5},{5,4},{6,7},{7,6},{8,9},{9,8},{10,11... | collective-permute-start | bytes 1966088 | tf_op jit(solution)/shard_map/ppermute | solution.py:420
  26.8 2.8 %collective-permute-start.5 = (bf16[512,512]{1,0:T(8,128)(2,1)S(1)}, bf16[512,512]{1,0:T(8,128)(2,1)S(1)}, u32[]{:S(2)}, u32[]{:S(2)}) collective-permute-start(bf16[512,512]{1,0:T(8,128)(2,1)S(1)} %get-tuple-element.32), channel_id=1, source_target_pairs={{0,2},{2,0},{4,6},{6,4},{8,10},{10,8},{12,14},{14,12},{16,18},{18,... | collective-permute-start | bytes 1572872 | tf_op jit(solution)/shard_map/ppermute | solution.py:20
  27.0 9.8 %collective-permute-start.7 = (bf16[512,128]{1,0:T(8,128)(2,1)S(1)}, bf16[512,128]{1,0:T(8,128)(2,1)S(1)}, u32[]{:S(2)}, u32[]{:S(2)}) collective-permute-start(bf16[512,128]{1,0:T(8,128)(2,1)S(1)} %add_convert_fusion.1), channel_id=1, source_target_pairs={{0,16},{2,18},{4,20},{6,22},{8,24},{10,26},{12,28},{14,30},{16,0},... | collective-permute-start | bytes 393224 | tf_op jit(solution)/shard_map/ppermute | solution.py:20
  30.3 8.1 %collective-permute-start.17 = (bf16[512,128]{1,0:T(8,128)(2,1)S(1)}, bf16[512,128]{1,0:T(8,128)(2,1)S(1)}, u32[]{:S(2)}, u32[]{:S(2)}) collective-permute-start(bf16[512,128]{1,0:T(8,128)(2,1)S(1)} %get-tuple-element.43), channel_id=1, source_target_pairs={{0,8},{2,10},{4,12},{6,14},{8,0},{10,2},{12,4},{14,6},{16,24},{18,... | collective-permute-start | bytes 393224 | tf_op jit(solution)/shard_map/ppermute | solution.py:20
  32.0 6.0 %collective-permute-start.18 = (bf16[512,128]{1,0:T(8,128)(2,1)S(1)}, bf16[512,128]{1,0:T(8,128)(2,1)S(1)}, u32[]{:S(2)}, u32[]{:S(2)}) collective-permute-start(bf16[512,128]{1,0:T(8,128)(2,1)S(1)} %get-tuple-element.44), channel_id=1, source_target_pairs={{0,4},{2,6},{4,0},{6,2},{8,12},{10,14},{12,8},{14,10},{16,20},{18,... | collective-permute-start | bytes 393224 | tf_op jit(solution)/shard_map/ppermute | solution.py:20
  33.5 8.0 %collective-permute-start.16 = (bf16[512,128]{1,0:T(8,128)(2,1)S(1)}, bf16[512,128]{1,0:T(8,128)(2,1)S(1)}, u32[]{:S(2)}, u32[]{:S(2)}) collective-permute-start(bf16[512,128]{1,0:T(8,128)(2,1)S(1)} %get-tuple-element.33.refs_1_.after), channel_id=1, source_target_pairs={{0,12},{2,14},{4,8},{6,10},{8,4},{10,6},{12,0},{14,2},{16,28},{18,... | collective-permute-start | bytes 393224 | tf_op jit(solution)/shard_map/ppermute | solution.py:20
  35.9 7.0 %copy-start = (bf16[4,256,512]{2,1,0:T(8,128)(2,1)S(1)}, bf16[4,256,512]{2,1,0:T(8,128)(2,1)}, u32[]{:S(2)}) copy-start(bf16[4,256,512]{2,1,0:T(8,128)(2,1)} %inverses.5) | copy-start | bytes 3145732
  35.9 6.5 %collective-permute-start.6 = (bf16[5,256,256]{2,1,0:T(8,128)(2,1)S(1)}, bf16[5,256,256]{2,1,0:T(8,128)(2,1)S(1)}, u32[]{:S(2)}, u32[]{:S(2)}) collective-permute-start(bf16[5,256,256]{2,1,0:T(8,128)(2,1)S(1)} %anchor.4.here), channel_id=1, source_target_pairs={{0,2},{2,0},{4,6},{6,4},{8,10},{10,8},{12,14},{14,12},{16,18},{18,... | collective-permute-start | bytes 1966088 | tf_op jit(solution)/shard_map/ppermute | solution.py:20
  37.5 5.4 %collective-permute-start.8 = (bf16[2,256,128]{2,1,0:T(8,128)(2,1)}, bf16[2,256,128]{2,1,0:T(8,128)(2,1)S(1)}, u32[]{:S(2)}, u32[]{:S(2)}) collective-permute-start(bf16[2,256,128]{2,1,0:T(8,128)(2,1)} %get-tuple-element.47), channel_id=1, source_target_pairs={{0,1},{1,0},{2,3},{3,2},{4,5},{5,4},{6,7},{7,6},{8,9},{9,8},{10,11... | collective-permute-start | bytes 393224 | tf_op jit(solution)/shard_map/ppermute | solution.py:433
  41.5 8.7 %collective-permute-start.19 = (bf16[512,128]{1,0:T(8,128)(2,1)S(1)}, bf16[512,128]{1,0:T(8,128)(2,1)S(1)}, u32[]{:S(2)}, u32[]{:S(2)}) collective-permute-start(bf16[512,128]{1,0:T(8,128)(2,1)S(1)} %add_convert_fusion), channel_id=1, source_target_pairs={{0,16},{2,18},{4,20},{6,22},{8,24},{10,26},{12,28},{14,30},{16,0},... | collective-permute-start | bytes 393224 | tf_op jit(solution)/shard_map/ppermute | solution.py:20
  44.9 6.0 %collective-permute-start.11 = (bf16[2,256,128]{2,1,0:T(8,128)(2,1)S(1)}, bf16[2,256,128]{2,1,0:T(8,128)(2,1)S(1)}, u32[]{:S(2)}, u32[]{:S(2)}) collective-permute-start(bf16[2,256,128]{2,1,0:T(8,128)(2,1)S(1)} %get-tuple-element.40.refs_0_), channel_id=1, source_target_pairs={{0,4},{2,6},{4,0},{6,2},{8,12},{10,14},{12,8},{14,10},{16,20},{18,... | collective-permute-start | bytes 393224 | tf_op jit(solution)/shard_map/ppermute | solution.py:20
  46.5 7.4 %collective-permute-start.10 = (bf16[2,256,128]{2,1,0:T(8,128)(2,1)S(1)}, bf16[2,256,128]{2,1,0:T(8,128)(2,1)S(1)}, u32[]{:S(2)}, u32[]{:S(2)}) collective-permute-start(bf16[2,256,128]{2,1,0:T(8,128)(2,1)S(1)} %get-tuple-element.40.refs_0_), channel_id=1, source_target_pairs={{0,12},{2,14},{4,8},{6,10},{8,4},{10,6},{12,0},{14,2},{16,28},{18,... | collective-permute-start | bytes 393224 | tf_op jit(solution)/shard_map/ppermute | solution.py:20
  50.3 5.0 %collective-permute-start.20 = (bf16[2,256,128]{2,1,0:T(8,128)(2,1)S(1)}, bf16[2,256,128]{2,1,0:T(8,128)(2,1)S(1)}, u32[]{:S(2)}, u32[]{:S(2)}) collective-permute-start(bf16[2,256,128]{2,1,0:T(8,128)(2,1)S(1)} %get-tuple-element.45), channel_id=1, source_target_pairs={{0,1},{1,0},{2,3},{3,2},{4,5},{5,4},{6,7},{7,6},{8,9},{9,8},{10,11... | collective-permute-start | bytes 393224 | tf_op jit(solution)/shard_map/ppermute | solution.py:440
  50.9 5.0 %collective-permute-start.9 = (bf16[2,256,128]{2,1,0:T(8,128)(2,1)S(1)}, bf16[2,256,128]{2,1,0:T(8,128)(2,1)S(1)}, u32[]{:S(2)}, u32[]{:S(2)}) collective-permute-start(bf16[2,256,128]{2,1,0:T(8,128)(2,1)S(1)} %get-tuple-element.40.refs_0_), channel_id=1, source_target_pairs={{0,8},{2,10},{4,12},{6,14},{8,0},{10,2},{12,4},{14,6},{16,24},{18,... | collective-permute-start | bytes 393224 | tf_op jit(solution)/shard_map/ppermute | solution.py:20
  50.9 8.3 %collective-permute-start.12 = (bf16[2,256,128]{2,1,0:T(8,128)(2,1)S(1)}, bf16[2,256,128]{2,1,0:T(8,128)(2,1)S(1)}, u32[]{:S(2)}, u32[]{:S(2)}) collective-permute-start(bf16[2,256,128]{2,1,0:T(8,128)(2,1)S(1)} %get-tuple-element.40.refs_0_), channel_id=1, source_target_pairs={{0,2},{2,0},{4,6},{6,4},{8,10},{10,8},{12,14},{14,12},{16,18},{18,... | collective-permute-start | bytes 393224 | tf_op jit(solution)/shard_map/ppermute | solution.py:20
  50.9 9.3 %collective-permute-start.15 = (bf16[2,256,128]{2,1,0:T(8,128)(2,1)S(1)}, bf16[2,256,128]{2,1,0:T(8,128)(2,1)S(1)}, u32[]{:S(2)}, u32[]{:S(2)}) collective-permute-start(bf16[2,256,128]{2,1,0:T(8,128)(2,1)S(1)} %collective-permute-done.11.refs_3_), channel_id=1, source_target_pairs={{0,2},{2,0},{4,6},{6,4},{8,10},{10,8},{12,14},{14,12},{16,18},{18,... | collective-permute-start | bytes 393224 | tf_op jit(solution)/shard_map/ppermute | solution.py:20
  53.9 6.3 %collective-permute-start.14 = (bf16[2,256,128]{2,1,0:T(8,128)(2,1)S(1)}, bf16[2,256,128]{2,1,0:T(8,128)(2,1)S(1)}, u32[]{:S(2)}, u32[]{:S(2)}) collective-permute-start(bf16[2,256,128]{2,1,0:T(8,128)(2,1)S(1)} %collective-permute-done.10.refs_2_), channel_id=1, source_target_pairs={{0,2},{2,0},{4,6},{6,4},{8,10},{10,8},{12,14},{14,12},{16,18},{18,... | collective-permute-start | bytes 393224 | tf_op jit(solution)/shard_map/ppermute | solution.py:20
  56.7 6.2 %collective-permute-start.23 = (bf16[2,256,128]{2,1,0:T(8,128)(2,1)S(1)}, bf16[2,256,128]{2,1,0:T(8,128)(2,1)S(1)}, u32[]{:S(2)}, u32[]{:S(2)}) collective-permute-start(bf16[2,256,128]{2,1,0:T(8,128)(2,1)S(1)} %chain.3.refs_8_), channel_id=1, source_target_pairs={{0,4},{2,6},{4,0},{6,2},{8,12},{10,14},{12,8},{14,10},{16,20},{18,... | collective-permute-start | bytes 393224 | tf_op jit(solution)/shard_map/ppermute | solution.py:20
  57.1 6.9 %collective-permute-start.22 = (bf16[2,256,128]{2,1,0:T(8,128)(2,1)S(1)}, bf16[2,256,128]{2,1,0:T(8,128)(2,1)S(1)}, u32[]{:S(2)}, u32[]{:S(2)}) collective-permute-start(bf16[2,256,128]{2,1,0:T(8,128)(2,1)S(1)} %chain.3.refs_8_), channel_id=1, source_target_pairs={{0,12},{2,14},{4,8},{6,10},{8,4},{10,6},{12,0},{14,2},{16,28},{18,... | collective-permute-start | bytes 393224 | tf_op jit(solution)/shard_map/ppermute | solution.py:20
  59.2 5.6 %collective-permute-start.21 = (bf16[2,256,128]{2,1,0:T(8,128)(2,1)S(1)}, bf16[2,256,128]{2,1,0:T(8,128)(2,1)S(1)}, u32[]{:S(2)}, u32[]{:S(2)}) collective-permute-start(bf16[2,256,128]{2,1,0:T(8,128)(2,1)S(1)} %chain.3.refs_8_), channel_id=1, source_target_pairs={{0,8},{2,10},{4,12},{6,14},{8,0},{10,2},{12,4},{14,6},{16,24},{18,... | collective-permute-start | bytes 393224 | tf_op jit(solution)/shard_map/ppermute | solution.py:20
  60.2 4.7 %collective-permute-start.24 = (bf16[2,256,128]{2,1,0:T(8,128)(2,1)S(1)}, bf16[2,256,128]{2,1,0:T(8,128)(2,1)S(1)}, u32[]{:S(2)}, u32[]{:S(2)}) collective-permute-start(bf16[2,256,128]{2,1,0:T(8,128)(2,1)S(1)} %chain.3.refs_8_), channel_id=1, source_target_pairs={{0,2},{2,0},{4,6},{6,4},{8,10},{10,8},{12,14},{14,12},{16,18},{18,... | collective-permute-start | bytes 393224 | tf_op jit(solution)/shard_map/ppermute | solution.py:20
  60.2 4.7 %collective-permute-start.13 = (bf16[2,256,128]{2,1,0:T(8,128)(2,1)S(1)}, bf16[2,256,128]{2,1,0:T(8,128)(2,1)S(1)}, u32[]{:S(2)}, u32[]{:S(2)}) collective-permute-start(bf16[2,256,128]{2,1,0:T(8,128)(2,1)S(1)} %collective-permute-done.9.refs_1_), channel_id=1, source_target_pairs={{0,2},{2,0},{4,6},{6,4},{8,10},{10,8},{12,14},{14,12},{16,18},{18,... | collective-permute-start | bytes 393224 | tf_op jit(solution)/shard_map/ppermute | solution.py:20
  62.8 2.1 %collective-permute-start.27 = (bf16[2,256,128]{2,1,0:T(8,128)(2,1)S(1)}, bf16[2,256,128]{2,1,0:T(8,128)(2,1)S(1)}, u32[]{:S(2)}, u32[]{:S(2)}) collective-permute-start(bf16[2,256,128]{2,1,0:T(8,128)(2,1)S(1)} %collective-permute-done.23.refs_11_), channel_id=1, source_target_pairs={{0,2},{2,0},{4,6},{6,4},{8,10},{10,8},{12,14},{14,12},{16,18},{18,... | collective-permute-start | bytes 393224 | tf_op jit(solution)/shard_map/ppermute | solution.py:20
  64.1 1.3 %collective-permute-start.26 = (bf16[2,256,128]{2,1,0:T(8,128)(2,1)S(1)}, bf16[2,256,128]{2,1,0:T(8,128)(2,1)S(1)}, u32[]{:S(2)}, u32[]{:S(2)}) collective-permute-start(bf16[2,256,128]{2,1,0:T(8,128)(2,1)S(1)} %collective-permute-done.22.refs_10_), channel_id=1, source_target_pairs={{0,2},{2,0},{4,6},{6,4},{8,10},{10,8},{12,14},{14,12},{16,18},{18,... | collective-permute-start | bytes 393224 | tf_op jit(solution)/shard_map/ppermute | solution.py:20
  64.8 1.3 %collective-permute-start.25 = (bf16[2,256,128]{2,1,0:T(8,128)(2,1)S(1)}, bf16[2,256,128]{2,1,0:T(8,128)(2,1)S(1)}, u32[]{:S(2)}, u32[]{:S(2)}) collective-permute-start(bf16[2,256,128]{2,1,0:T(8,128)(2,1)S(1)} %collective-permute-done.21.refs_9_), channel_id=1, source_target_pairs={{0,2},{2,0},{4,6},{6,4},{8,10},{10,8},{12,14},{14,12},{16,18},{18,... | collective-permute-start | bytes 393224 | tf_op jit(solution)/shard_map/ppermute | solution.py:20
